TPU v7x, 768 devices: a whole 4x8x12 slice. The times are simulated.
768 devices in a mesh: graph: 48 (over x, z), feat: 16 (over y, core).
Axes of the slice: x: 4, y: 8, z: 12, core: 2. Of those that a mesh axis runs over, the one named last changes fastest.
Arguments:
- feats: bfloat16 [256, 49152], P('feat', 'graph'), may hold values from -6 to 6
- w_self: bfloat16 [256, 256], P('feat'), may hold values from -0.25 to 0.25
- w_neigh: bfloat16 [256, 256], P('feat'), may hold values from -0.25 to 0.25
- bias: float32 [256], P('feat'), may hold values from -1 to 1
- cotangent: bfloat16 [256, 49152], P('feat', 'graph'), may hold values from -6 to 6
- block_ids: int32 [48, 48, 2], P('graph'), may hold values from 0 to 7
- req_counts: int32 [48, 48], P('graph'), may hold values from 1 to 2, as said below
- tile_dst: int32 [48, 48, 2], P('graph'), may hold values from 0 to 7
- adjacency: bfloat16 [48, 48, 2, 128, 128], P('graph'), may hold values from 0 to 1.5, as said below
Outputs:
- output: bfloat16 [256, 49152], P('feat', 'graph')
- feat_grad: float32 [256, 49152], P('feat', 'graph')
Inputs may be any that keep to these rules, and one draw needn't show every extreme that they name: req_counts[p, p] = 2 for every part p. `adjacency`: each entry is 0 or an edge weight of 0.5 to 1.5; tiles of slots at or beyond req_counts hold entries too.
All inputs are finite; a program needn't handle non-finite values.
Results may differ from a plain program's by a relative error of at most 0.0035.
Values may be sent and summed in bfloat16 or wider, within the bound.
No kernel may reach another device: no remote copies, remote signals or barrier semaphores. Data moves between devices by JAX's collectives and lax.ppermute only.
A program may use at most 32 MiB of HBM per device.

v0:
```python
import jax
import jax.numpy as jnp
from jax import lax
from jax.sharding import PartitionSpec as P

BLK = 128
NB = 8
CAP = 2


def per_device(feats, w_self, w_neigh, bias, cotangent, block_ids, req_counts, tile_dst, adjacency):
    highest = lax.Precision.HIGHEST
    graph_parts = lax.axis_size("graph")
    feat_rows, slab_len = feats.shape
    my_ids = block_ids[0]
    slot_ids = jnp.arange(CAP, dtype=jnp.int32)
    block_range = jnp.arange(NB, dtype=jnp.int32)
    live_mask = (slot_ids[None, :] < req_counts[0][:, None]).astype(jnp.bfloat16)
    tile_vals = adjacency[0] * live_mask[:, :, None, None]
    dst_hot = (tile_dst[0][:, :, None] == block_range[None, None, :]).astype(jnp.float32)
    src_hot = (my_ids[:, :, None] == block_range[None, None, :]).astype(jnp.float32)
    shard_piece = lax.all_gather(feats, "graph", axis=1, tiled=True)
    shard_count = shard_piece.shape[1] // slab_len
    wanted_hot = (my_ids[:, :, None] == block_range[None, None, :]).astype(jnp.bfloat16)
    pieces = shard_piece.reshape(feat_rows, shard_count, NB, BLK)
    chosen = jnp.einsum(
        "kcn,hknb->kchb", wanted_hot, pieces, preferred_element_type=jnp.float32
    ).astype(jnp.bfloat16)
    fetched = chosen
    contrib = jnp.einsum("gchi,gcij->hgcj", fetched, tile_vals, preferred_element_type=jnp.float32)
    raw_sums = jnp.einsum("hgcj,gcn->hnj", contrib, dst_hot, precision=highest)
    column_sums = jnp.sum(tile_vals, axis=2, dtype=jnp.float32)
    degree = jnp.einsum("gcj,gcn->nj", column_sums, dst_hot, precision=highest)
    inverse = 1.0 / jnp.maximum(degree, 1.0)
    aggregated = (raw_sums * inverse[None]).astype(jnp.bfloat16).reshape(feat_rows, slab_len)
    node_inverse = inverse.reshape(slab_len)
    partial_value = jnp.einsum(
        "kh,kn->hn", w_self, feats, preferred_element_type=jnp.float32
    ) + jnp.einsum("kh,kn->hn", w_neigh, aggregated, preferred_element_type=jnp.float32)
    preact = (
        lax.psum_scatter(partial_value, "feat", scatter_dimension=0, tiled=True) + bias[:, None]
    )
    sigmoid_pre = jax.nn.sigmoid(preact)
    output = (preact * sigmoid_pre).astype(jnp.bfloat16)
    d_preact = (
        cotangent.astype(jnp.float32) * (sigmoid_pre + preact * sigmoid_pre * (1.0 - sigmoid_pre))
    ).astype(jnp.bfloat16)
    full_grad = lax.all_gather(d_preact, "feat", axis=0, tiled=True)
    self_grad = jnp.dot(w_self, full_grad, preferred_element_type=jnp.float32)
    scaled_grad = (
        jnp.dot(w_neigh, full_grad, preferred_element_type=jnp.float32) * node_inverse[None]
    ).astype(jnp.bfloat16)
    chosen = jnp.einsum(
        "hnj,gcn->hgcj",
        scaled_grad.reshape(feat_rows, NB, BLK),
        dst_hot.astype(jnp.bfloat16),
        preferred_element_type=jnp.float32,
    ).astype(jnp.bfloat16)
    tile_grads = jnp.einsum(
        "hgcj,gcij->gchi", chosen, tile_vals, preferred_element_type=jnp.float32
    )
    dense_terms = jnp.einsum("gchi,gcn->hgni", tile_grads, src_hot, precision=highest)
    dense_terms = dense_terms.reshape(feat_rows, graph_parts * slab_len)
    owner_sums = lax.psum_scatter(dense_terms, "graph", scatter_dimension=1, tiled=True)
    feat_grad = self_grad + owner_sums
    return (output, feat_grad)


def solution(mesh):
    in_specs = (
        P("feat", "graph"),
        P("feat", None),
        P("feat", None),
        P("feat"),
        P("feat", "graph"),
        P("graph", None, None),
        P("graph", None),
        P("graph", None, None),
        P("graph", None, None, None, None),
    )
    out_specs = (P("feat", "graph"), P("feat", "graph"))
    return jax.shard_map(
        per_device, mesh=mesh, in_specs=in_specs, out_specs=out_specs, check_vma=False
    )
```

profile of v0, /device:TPU:6, one launch (start us, length us, event | category | flops | bytes accessed | tf_op | source)
XLA Modules:
  0.0 665.0 jit_solution(1719619976225601023)
XLA Ops:
  7.2 0.0 copy-start
  7.2 0.0 copy-start.5
  7.2 0.0 copy-start.8
  7.2 0.0 copy-start.7
  7.2 0.0 all-gather.2.cloned.1.call-start
  7.3 0.7 all-gather.2.cloned.1.call-update
  7.9 0.0 reduce-scatter.3.cloned.1.call-start
  8.0 0.8 copy.14
  8.8 0.7 fusion.27
  9.5 2.7 convert_reduce_fusion
  12.2 0.0 copy-done.8
  12.2 0.2 fusion.13
  12.4 0.0 copy-done.5
  12.4 0.0 copy-done.7
  12.4 0.0 copy-start.1
  12.4 1.3 fusion.36
  13.7 120.2 %all-gather.2.cloned.1.call-done = bf16[16,49152]{1,0:T(8,128)(2,1)} async-done(((bf16[16,1024]{1,0:T(8,128)(2,1)}), bf16[16,49152]{1,0:T(8,128)(2,1)}) %all-gather.2.cloned.1.call-update) | async-done | bytes 1572880 | tf_op jit(solution)/shard_map/all_gather | solution.py:22
  133.9 1.7 copy.27
  135.6 0.0 copy-start.4
  135.6 0.6 fusion.2
  136.2 0.0 copy-done.1
  136.2 0.0 copy-start.6
  136.2 0.0 copy-start.9
  136.2 1.0 fusion.1
  137.2 0.8 fusion.9
  138.1 0.0 copy-done
  138.1 0.0 copy-done.4
  138.1 1.3 fusion.6
  139.4 0.0 reduce-scatter.3.cloned.1.call-update
  139.4 0.0 reduce-scatter.5.cloned.1.call-start
  139.5 59.5 %reduce-scatter.3.cloned.1.call-done = f32[16,1024]{1,0:T(8,128)} async-done(((f32[256,1024]{1,0:T(8,128)}), f32[16,1024]{1,0:T(8,128)}) %reduce-scatter.3.cloned.1.call-update) | async-done | bytes 65552 | tf_op jit(solution)/shard_map/reduce_scatter | solution.py:41
  198.9 0.0 copy-done.6
  198.9 0.0 copy-done.9
  198.9 1.6 multiply_convert_fusion
  200.5 15.7 %all_gather.7 = bf16[256,1024]{1,0:T(8,128)(2,1)S(1)} all-gather(bf16[16,1024]{1,0:T(8,128)(2,1)S(1)} %get-tuple-element.2), channel_id=1, replica_groups=mesh['graph'=48,'feat'=16] {'feat'}, dimensions={0}, use_global_device_ids=true | all-gather | bytes 557056 | tf_op jit(solution)/shard_map/all_gather | solution.py:48
  216.2 0.0 copy-start.2
  216.2 0.8 copy-done.2
  217.0 0.2 fusion.11
  217.2 0.3 fusion.31
  217.5 1.8 fusion
  219.3 2.2 convolution_bitcast_fusion
  221.6 0.3 copy.17
  221.9 3.5 copy.52
  225.4 0.0 copy-start.3
  225.4 0.0 reduce-scatter.5.cloned.1.call-update
  225.4 431.5 %reduce-scatter.5.cloned.1.call-done = f32[16,1024]{1,0:T(8,128)} async-done(((f32[16,49152]{1,0:T(8,128)}), f32[16,1024]{1,0:T(8,128)}) %reduce-scatter.5.cloned.1.call-update) | async-done | bytes 65552 | tf_op jit(solution)/shard_map/reduce_scatter | solution.py:64
  656.9 0.0 copy-done.3
  656.9 1.7 fusion.8
  (1 shorter events, 0.0 us)
Async XLA Ops:
  7.2 130.9 %copy-start = (bf16[16,256]{1,0:T(8,128)(2,1)S(1)}, bf16[16,256]{1,0:T(8,128)(2,1)}, u32[]{:S(2)}) copy-start(bf16[16,256]{1,0:T(8,128)(2,1)} %param.11) | copy-start | bytes 24580
  7.2 5.2 copy-start.5
  7.2 5.0 copy-start.8
  7.2 5.2 copy-start.7
  7.2 126.7 %all-gather.2.cloned.1.call-start = ((), (), s32[]{:S(2)}) async-start(), calls=%async_computation.2 | async-start | bytes 1605632 | tf_op jit(solution)/shard_map/all_gather | solution.py:22
  7.9 191.0 %reduce-scatter.3.cloned.1.call-start = ((), (), s32[]{:S(2)}) async-start(), calls=%async_computation.3 | async-start | bytes 1114112 | tf_op jit(solution)/shard_map/reduce_scatter | solution.py:41
  12.4 123.8 %copy-start.1 = (bf16[1,48,2,128,128]{4,3,2,1,0:T(8,128)(2,1)S(1)}, bf16[1,48,2,128,128]{4,3,2,1,0:T(8,128)(2,1)}, u32[]{:S(2)}) copy-start(bf16[1,48,2,128,128]{4,3,2,1,0:T(8,128)(2,1)} %param.17) | copy-start | bytes 9437188
  135.6 2.5 copy-start.4
  136.2 62.7 %copy-start.6 = (bf16[16,1024]{1,0:T(8,128)(2,1)S(1)}, bf16[16,1024]{1,0:T(8,128)(2,1)}, u32[]{:S(2)}) copy-start(bf16[16,1024]{1,0:T(8,128)(2,1)} %param.13) | copy-start | bytes 98308
  136.2 62.7 %copy-start.9 = (f32[16]{0:T(128)S(1)}, f32[16]{0:T(128)}, u32[]{:S(2)}) copy-start(f32[16]{0:T(128)} %param.12) | copy-start | bytes 196
  139.4 517.4 %reduce-scatter.5.cloned.1.call-start = ((), (), s32[]{:S(2)}) async-start(), calls=%async_computation.4 | async-start | bytes 3211264 | tf_op jit(solution)/shard_map/reduce_scatter | solution.py:64
  216.2 0.8 copy-start.2
  225.4 431.5 %copy-start.3 = (bf16[256,1024]{1,0:T(8,128)(2,1)S(1)}, bf16[256,1024]{1,0:T(8,128)(2,1)}, u32[]{:S(2)}) copy-start(bf16[256,1024]{1,0:T(8,128)(2,1)} %copy-done.2) | copy-start | bytes 1572868
Sparse Core Ops, SparseCore 0:
  11.6 122.1 all-gather.1
  139.5 59.3 reduce-scatter.2
  225.5 431.2 reduce-scatter.4
where the time goes:
time: 666 us; the launch traced here: 665 us
  waiting for transfers between devices  612 us (92%)
  blocking collectives  15.7 us (2%)
  between operations  13.9 us (2%)
  matrix products  11.4 us (2%)
  local copies, waits for them, and re-layouts  7.09 us (1%)
    reduce_scatter x1, waiting for transfers between devices, per_device(): lax.psum_scatter(dense_terms, 'graph', scatter_dimension=1, tiled=True)  431 us
    all_gather x1, waiting for transfers between devices, per_device(): shard_piece = lax.all_gather(feats, 'graph', axis=1, tiled=True)  120 us
    reduce_scatter x1, waiting for transfers between devices, per_device(): lax.psum_scatter(partial_value, 'feat', scatter_dimension=0, tiled=True)  59.5 us
    all_gather x1, blocking collectives, per_device(): full_grad = lax.all_gather(d_preact, 'feat', axis=0, tiled=True)  15.7 us
  transfers between devices with their start and end apart: 3, of which 3 were waited for; matrix products, arithmetic and copies ran while one was open for 1% of the time, Pallas kernels for 0%

commit v1 on v0

v1 whole, which is shorter than its diff:
```python
import jax
import jax.numpy as jnp
from jax import lax
from jax.experimental import pallas as pl
from jax.experimental.pallas import tpu as pltpu
from jax.sharding import PartitionSpec as P

BLK = 128
NB = 8
CAP = 2
CHUNK = 8
VMEM_LIMIT = 24 * 1024 * 1024

SMEM_SPEC = pl.BlockSpec(memory_space=pltpu.SMEM)
VMEM_SPEC = pl.BlockSpec(memory_space=pltpu.VMEM)


def chunk_of(tiles):
    return CHUNK if tiles % CHUNK == 0 else CAP


def select_kernel(ids_ref, feats_ref, out_ref):
    for t in range(out_ref.shape[0]):
        start = pl.multiple_of(ids_ref[t] * BLK, BLK)
        out_ref[t] = feats_ref[:, pl.ds(start, BLK)]


def aggregate_kernel(dst_ref, counts_ref, fetched_ref, adj_ref, agg_ref, inv_ref):
    tiles, rows, _ = fetched_ref.shape
    chunk = chunk_of(tiles)
    row_ids = lax.broadcasted_iota(jnp.int32, (16, BLK), 0)
    zero = jnp.zeros((rows, BLK), jnp.bfloat16)

    def step(k, acc):
        columns = []
        for i in range(chunk):
            t = k * chunk + i
            live = (i % CAP) < counts_ref[t // CAP]
            dst = jnp.where(live, dst_ref[t], NB)
            block = fetched_ref[t]
            pieces = [jnp.where(dst == n, block, zero) for n in range(NB)]
            pieces.append((row_ids == dst).astype(jnp.float32).astype(jnp.bfloat16))
            columns.append(jnp.concatenate(pieces, axis=0))
        lhs = jnp.concatenate(columns, axis=1)
        start = pl.multiple_of(k * (chunk * BLK), chunk * BLK)
        weights = adj_ref[pl.ds(start, chunk * BLK), :]
        return acc + jnp.dot(lhs, weights, preferred_element_type=jnp.float32)

    acc = lax.fori_loop(
        0, tiles // chunk, step, jnp.zeros((NB * rows + 16, BLK), jnp.float32)
    )
    inverse = 1.0 / jnp.maximum(acc[NB * rows : NB * rows + NB], 1.0)
    inv_ref[...] = inverse
    for n in range(NB):
        part = acc[n * rows : (n + 1) * rows] * inverse[n : n + 1]
        agg_ref[:, n * BLK : (n + 1) * BLK] = part.astype(jnp.bfloat16)


def update_kernel(
    first_ref,
    dst_ref,
    counts_ref,
    agg_ref,
    bundle_ref,
    w_self_ref,
    w_neigh_ref,
    inv_ref,
    adj_ref,
    out_ref,
    self_ref,
    grads_ref,
    out_all,
    scaled,
):
    hidden, slab = agg_ref.shape
    rows = w_self_ref.shape[0]
    tiles = grads_ref.shape[0]
    chunk = chunk_of(tiles)
    weights = 2 * slab
    tail = bundle_ref[:, weights + 2 * hidden : weights + 2 * hidden + BLK].astype(jnp.float32)
    bias = tail[:, 0:1] + tail[:, 1:2] + tail[:, 2:3]
    w_self_all = bundle_ref[:, weights : weights + hidden]
    w_neigh_all = bundle_ref[:, weights + hidden : weights + 2 * hidden]
    contract_rows = (((0,), (0,)), ((), ()))
    width = 2 * BLK
    for start in range(0, slab, width):
        columns = slice(start, start + width)
        preact = (
            lax.dot_general(
                w_self_all, bundle_ref[:, columns], contract_rows, preferred_element_type=jnp.float32
            )
            + lax.dot_general(
                w_neigh_all, agg_ref[:, columns], contract_rows, preferred_element_type=jnp.float32
            )
            + bias
        )
        s = 1.0 / (1.0 + jnp.exp(-preact))
        silu = preact * s
        out_all[:, columns] = silu.astype(jnp.bfloat16)
        cotangent = bundle_ref[:, slab + start : slab + start + width].astype(jnp.float32)
        d_preact = (cotangent * (s + silu * (1.0 - s))).astype(jnp.bfloat16)
        self_ref[:, columns] = jnp.dot(
            w_self_ref[...], d_preact, preferred_element_type=jnp.float32
        )
        neigh = jnp.dot(w_neigh_ref[...], d_preact, preferred_element_type=jnp.float32)
        for half in range(width // BLK):
            n = start // BLK + half
            part = neigh[:, half * BLK : (half + 1) * BLK] * inv_ref[n : n + 1]
            scaled[n] = part.astype(jnp.bfloat16)
    out_ref[...] = out_all[pl.ds(pl.multiple_of(first_ref[0], rows), rows), :]

    zero = jnp.zeros((rows, BLK), jnp.bfloat16)
    contract_columns = (((1,), (1,)), ((), ()))

    def step(k, carry):
        for i in range(chunk):
            t = k * chunk + i
            live = (i % CAP) < counts_ref[t // CAP]
            chosen = jnp.where(live, scaled[dst_ref[t]], zero)
            start = pl.multiple_of(t * BLK, BLK)
            grads = lax.dot_general(
                chosen,
                adj_ref[pl.ds(start, BLK), :],
                contract_columns,
                preferred_element_type=jnp.float32,
            )
            grads_ref[t] = grads.astype(jnp.bfloat16)
        return carry

    lax.fori_loop(0, tiles // chunk, step, 0)


def sum_kernel(ids_ref, grads_ref, self_ref, out_ref):
    tiles, rows, _ = grads_ref.shape

    def step(t, sums):
        block = grads_ref[t].astype(jnp.float32)
        return tuple(
            total + jnp.where(ids_ref[t] == n, block, 0.0) for n, total in enumerate(sums)
        )

    start = tuple(self_ref[:, n * BLK : (n + 1) * BLK] for n in range(NB))
    sums = lax.fori_loop(0, tiles, step, start, unroll=4)
    for n in range(NB):
        out_ref[:, n * BLK : (n + 1) * BLK] = sums[n]


def params():
    return pltpu.CompilerParams(vmem_limit_bytes=VMEM_LIMIT)


def per_device(feats, w_self, w_neigh, bias, cotangent, block_ids, req_counts, tile_dst, adjacency):
    graph_parts = lax.axis_size("graph")
    hidden = w_self.shape[1]
    rows, slab = feats.shape
    tiles = graph_parts * CAP
    adj = adjacency.reshape(tiles * BLK, BLK)
    dst = tile_dst.reshape(tiles)
    counts = req_counts.reshape(graph_parts)
    first_row = (lax.axis_index("feat") * rows).astype(jnp.int32).reshape(1)

    high = lax.reduce_precision(bias, 8, 7)
    middle = lax.reduce_precision(bias - high, 8, 7)
    low = bias - high - middle
    terms = jnp.stack([high, middle, low], axis=1).astype(jnp.bfloat16)
    terms = jnp.pad(terms, ((0, 0), (0, BLK - 3)))
    bundle = jnp.concatenate([feats, cotangent, w_self, w_neigh, terms], axis=1)
    bundle = lax.all_gather(bundle, "feat", axis=0, tiled=True)

    asked = lax.all_to_all(block_ids[0], "graph", 0, 0).reshape(tiles)
    picked = pl.pallas_call(
        select_kernel,
        out_shape=jax.ShapeDtypeStruct((tiles, rows, BLK), jnp.bfloat16),
        in_specs=[SMEM_SPEC, VMEM_SPEC],
        out_specs=VMEM_SPEC,
        compiler_params=params(),
        name="select_blocks",
    )(asked, feats)
    fetched = lax.all_to_all(
        picked.reshape(graph_parts, CAP, rows, BLK), "graph", 0, 0
    ).reshape(tiles, rows, BLK)
    agg, inverse = pl.pallas_call(
        aggregate_kernel,
        out_shape=(
            jax.ShapeDtypeStruct((rows, slab), jnp.bfloat16),
            jax.ShapeDtypeStruct((NB, BLK), jnp.float32),
        ),
        in_specs=[SMEM_SPEC, SMEM_SPEC, VMEM_SPEC, VMEM_SPEC],
        out_specs=(VMEM_SPEC, VMEM_SPEC),
        compiler_params=params(),
        name="aggregate",
    )(dst, counts, fetched, adj)
    agg_all = lax.all_gather(agg, "feat", axis=0, tiled=True)
    output, self_grad, grads = pl.pallas_call(
        update_kernel,
        out_shape=(
            jax.ShapeDtypeStruct((rows, slab), jnp.bfloat16),
            jax.ShapeDtypeStruct((rows, slab), jnp.float32),
            jax.ShapeDtypeStruct((tiles, rows, BLK), jnp.bfloat16),
        ),
        in_specs=[SMEM_SPEC] * 3 + [VMEM_SPEC] * 6,
        out_specs=(VMEM_SPEC,) * 3,
        scratch_shapes=[
            pltpu.VMEM((hidden, slab), jnp.bfloat16),
            pltpu.VMEM((NB, rows, BLK), jnp.bfloat16),
        ],
        compiler_params=params(),
        name="update",
    )(first_row, dst, counts, agg_all, bundle, w_self, w_neigh, inverse, adj)
    returned = lax.all_to_all(
        grads.reshape(graph_parts, CAP, rows, BLK), "graph", 0, 0
    ).reshape(tiles, rows, BLK)
    feat_grad = pl.pallas_call(
        sum_kernel,
        out_shape=jax.ShapeDtypeStruct((rows, slab), jnp.float32),
        in_specs=[SMEM_SPEC, VMEM_SPEC, VMEM_SPEC],
        out_specs=VMEM_SPEC,
        compiler_params=params(),
        name="sum_returned",
    )(asked, returned, self_grad)
    return (output, feat_grad)


def solution(mesh):
    in_specs = (
        P("feat", "graph"),
        P("feat", None),
        P("feat", None),
        P("feat"),
        P("feat", "graph"),
        P("graph", None, None),
        P("graph", None),
        P("graph", None, None),
        P("graph", None, None, None, None),
    )
    out_specs = (P("feat", "graph"), P("feat", "graph"))
    return jax.shard_map(
        per_device, mesh=mesh, in_specs=in_specs, out_specs=out_specs, check_vma=False
    )
```

time: 666 us -> 145 us (0.22)
  waiting for transfers between devices: 612 us -> 18 us
  blocking collectives: 15.7 us -> 76.2 us
  Pallas kernels: 0 us -> 12.6 us
  matrix products: 11.4 us -> 0 us
  local copies, waits for them, and re-layouts: 7.09 us -> 15.3 us
    reduce_scatter x2 -> x0, waiting for transfers between devices: 491 us -> none  [the longest x1 431 us: per_device(): lax.psum_scatter(dense_terms, 'graph', scatter_dimension=1, tiled=True)]
    all_gather x1, waiting for transfers between devices: 120 us -> 0.01 us  [per_device(): bundle = lax.all_gather(bundle, 'feat', axis=0, tiled=True)]
    all_to_all x0 -> x2, blocking collectives: none -> 55.7 us  [the longest x1 28.7 us: per_device(): asked = lax.all_to_all(block_ids[0], 'graph', 0, 0).reshape(tiles)]
    all_to_all x0 -> x1, waiting for transfers between devices: none -> 18 us  [per_device(): lax.all_to_all(picked.reshape(graph_parts, CAP, rows, BLK), 'graph', 0, 0)]
    pallas_call x0 -> x4, Pallas kernels: none -> 12.6 us  [the longest x1 5.64 us: per_device(): pl.pallas_call(update_kernel, out_shape=(jax.ShapeDtypeStruct((rows, slab...]
    dot_general x11 -> x0, matrix products: 11.4 us -> none  [the longest x1 2.24 us: per_device(): jnp.einsum('gchi,gcn->hgni', tile_grads, src_hot, precision=highest)]
    unnamed x23 -> x37, local copies, waits for them, and re-layouts: 6.02 us -> 13.2 us
  transfers between devices with their start and end apart: 3 -> 2, of which waited for: 3 -> 1; matrix products, arithmetic and copies ran while one was open for 1% -> 2% of each run, Pallas kernels for 0% -> 3%
where the time goes in v1:
time: 145 us; the launch traced here: 144 us
  blocking collectives  76.2 us (53%)
  waiting for transfers between devices  18 us (12%)
  local copies, waits for them, and re-layouts  15.3 us (11%)
  between operations  14.1 us (10%)
  Pallas kernels  12.6 us (9%)
  starting transfers between devices  6.5 us (4%)
    all_to_all x1, blocking collectives, per_device(): asked = lax.all_to_all(block_ids[0], 'graph', 0, 0).reshape(tiles)  28.7 us
    all_to_all x1, blocking collectives, per_device(): lax.all_to_all(grads.reshape(graph_parts, CAP, rows, BLK), 'graph', 0, 0)  27 us
    all_gather x1, blocking collectives, per_device(): agg_all = lax.all_gather(agg, 'feat', axis=0, tiled=True)  20.5 us
    all_to_all x1, waiting for transfers between devices, per_device(): lax.all_to_all(picked.reshape(graph_parts, CAP, rows, BLK), 'graph', 0, 0)  18 us
    unnamed x37, local copies, waits for them, and re-layouts  13.2 us
    all_to_all x1, starting transfers between devices, per_device(): lax.all_to_all(picked.reshape(graph_parts, CAP, rows, BLK), 'graph', 0, 0)  6.46 us
    pallas_call x1, Pallas kernels, per_device(): pl.pallas_call(update_kernel, out_shape=(jax.ShapeDtypeStruct((rows, slab...  5.64 us
    pallas_call x1, Pallas kernels, per_device(): pl.pallas_call(aggregate_kernel, out_shape=(jax.ShapeDtypeStruct((rows, s...  3.58 us
  transfers between devices with their start and end apart: 2, of which 1 were waited for; matrix products, arithmetic and copies ran while one was open for 2% of the time, Pallas kernels for 3%

profile of v1, /device:TPU:6, one launch (start us, length us, event | category | flops | bytes accessed | tf_op | source)
XLA Modules:
  0.0 144.2 jit_solution(10244453853194888604)
XLA Ops:
  7.2 0.0 copy-start.5
  7.2 0.0 copy-start.6
  7.2 0.0 all-gather.2.cloned.1.call-start
  7.2 0.7 fusion
  7.9 0.1 copy.23
  8.0 0.8 constant_dynamic-update-slice_fusion.4
  8.8 0.8 constant_dynamic-update-slice_fusion.3
  9.5 0.7 constant_dynamic-update-slice_fusion.2
  10.2 0.7 constant_dynamic-update-slice_fusion.1
  10.9 0.0 copy-start.15
  10.9 0.6 copy-done.15
  11.6 0.0 all-gather.2.cloned.1.call-update
  11.6 0.8 copy.22
  12.4 28.7 %all_to_all.19 = s32[48,1,2]{2,1,0:T(1,128)S(1)} all-to-all(s32[48,1,2]{2,1,0:T(1,128)S(1)} %copy.22), channel_id=1, replica_groups=mesh['graph'=48,'feat'=16] {'graph'}, dimensions={0} | all-to-all | bytes 768 | tf_op jit(solution)/shard_map/all_to_all | solution.py:170
  41.1 0.5 broadcast.5
  41.6 0.7 reduce.3
  42.3 0.1 reshape.38.ids_ref
  42.4 0.0 copy-start.4
  42.4 0.8 copy-done.4
  43.2 0.0 copy-start.7
  43.2 1.4 select_blocks.1
  44.6 6.5 %all-to-all-start.1 = ((bf16[48,2,16,128]{3,2,1,0:T(8,128)(2,1)}), bf16[48,2,16,128]{3,2,1,0:T(8,128)(2,1)S(1)}, u32[]{:S(2)}, u32[]{:S(2)}) async-start(bf16[48,2,16,128]{3,2,1,0:T(8,128)(2,1)} %bitcast.3), calls=%async_computation.1 | async-start | bytes 786432 | tf_op jit(solution)/shard_map/all_to_all | solution.py:179
  51.1 0.8 copy.21
  51.8 0.6 reshape.36.dst_ref
  52.5 18.0 %all-to-all-done.1 = bf16[48,2,16,128]{3,2,1,0:T(8,128)(2,1)S(1)} async-done(((bf16[48,2,16,128]{3,2,1,0:T(8,128)(2,1)}), bf16[48,2,16,128]{3,2,1,0:T(8,128)(2,1)S(1)}, u32[]{:S(2)}, u32[]{:S(2)}) %all-to-all-start.1) | async-done | bytes 393248 | tf_op jit(solution)/shard_map/all_to_all | solution.py:179
  70.5 0.0 copy-done.7
  70.5 0.0 copy-start
  70.5 1.9 %copy-done = bf16[1,48,2,128,128]{4,3,2,1,0:T(8,128)(2,1)S(1)} copy-done((bf16[1,48,2,128,128]{4,3,2,1,0:T(8,128)(2,1)S(1)}, bf16[1,48,2,128,128]{4,3,2,1,0:T(8,128)(2,1)}, u32[]{:S(2)}) %copy-start) | copy-done | bytes 3145752
  72.4 0.0 copy-start.9
  72.4 0.6 copy-done.9
  73.0 0.0 copy-start.13
  73.0 0.7 copy-done.13
  73.6 0.0 copy-start.1
  73.6 3.6 %aggregate.1 = (bf16[16,1024]{1,0:T(8,128)(2,1)S(1)}, f32[8,128]{1,0:T(8,128)S(1)}) custom-call(s32[96]{0:T(128)S(1)} %copy-done.9, s32[48]{0:T(128)S(1)} %bitcast.19, bf16[96,16,128]{2,1,0:T(8,128)(2,1)S(1)} %bitcast.17, bf16[12288,128]{1,0:T(8,128)(2,1)S(1)} %bitcast.14), custom_call_target="tpu_custom_call" | custom-call | tf_op jit(solution)/shard_map/aggregate/pallas_call | solution.py:182
  77.2 0.0 copy-start.11
  77.2 0.6 copy-done.11
  77.8 0.0 copy-start.8
  77.8 20.5 %all_gather.6.agg_ref = bf16[256,1024]{1,0:T(8,128)(2,1)} all-gather(bf16[16,1024]{1,0:T(8,128)(2,1)S(1)} %get-tuple-element.7), channel_id=1, replica_groups=mesh['graph'=48,'feat'=16] {'feat'}, dimensions={0}, use_global_device_ids=true | all-gather | bytes 557056 | tf_op jit(solution)/shard_map/all_gather | solution.py:193
  98.4 0.0 all-gather.2.cloned.1.call-done.bundle_ref
  98.4 0.0 copy-done.5
  98.4 0.0 copy-done.6
  98.4 0.0 copy-done.1
  98.4 0.0 copy-start.2
  98.4 1.0 copy-done.2
  99.4 0.0 copy-start.3
  99.4 1.3 copy-done.3
  100.7 0.0 copy-start.10
  100.7 0.6 copy-done.10
  101.4 0.0 copy-start.12
  101.4 0.7 copy-done.12
  102.0 0.0 copy-start.14
  102.0 0.7 copy-done.14
  102.7 5.6 %update.1 = (bf16[16,1024]{1,0:T(8,128)(2,1)}, f32[16,1024]{1,0:T(8,128)S(1)}, bf16[96,16,128]{2,1,0:T(8,128)(2,1)S(1)}) custom-call(s32[1]{0:T(128)} %bitcast.first_ref, s32[96]{0:T(128)S(1)} %copy-done.10, s32[48]{0:T(128)S(1)} %bitcast.20, bf16[256,1024]{1,0:T(8,128)(2,1)S(1)} %copy-done.2, bf16[256,2688]{1,0:T(8,128)(2,1)S(1)} %copy-done.3, ...), custom_call_target="tpu_custom_call" | custom-call | tf_op jit(solution)/shard_map/update/pallas_call | solution.py:194
  108.3 27.0 %all_to_all.20 = bf16[48,2,16,128]{3,2,1,0:T(8,128)(2,1)S(1)} all-to-all(bf16[48,2,16,128]{3,2,1,0:T(8,128)(2,1)S(1)} %bitcast.18), channel_id=1, replica_groups=mesh['graph'=48,'feat'=16] {'graph'}, dimensions={0} | all-to-all | bytes 786432 | tf_op jit(solution)/shard_map/all_to_all | solution.py:210
  135.3 0.0 copy-done.8
  135.3 2.0 %sum_returned.1 = f32[16,1024]{1,0:T(8,128)} custom-call(s32[96]{0:T(128)S(1)} %copy-done.8, bf16[96,16,128]{2,1,0:T(8,128)(2,1)S(1)} %bitcast.16, f32[16,1024]{1,0:T(8,128)S(1)} %get-tuple-element.11.self_ref), custom_call_target="tpu_custom_call" | custom-call | tf_op jit(solution)/shard_map/sum_returned/pallas_call | solution.py:213
  (2 shorter events, 0.0 us)
Async XLA Ops:
  7.2 91.2 %copy-start.5 = (bf16[16,256]{1,0:T(8,128)(2,1)S(1)}, bf16[16,256]{1,0:T(8,128)(2,1)}, u32[]{:S(2)}) copy-start(bf16[16,256]{1,0:T(8,128)(2,1)} %w_self_ref.1) | copy-start | bytes 24580
  7.2 91.2 %copy-start.6 = (bf16[16,256]{1,0:T(8,128)(2,1)S(1)}, bf16[16,256]{1,0:T(8,128)(2,1)}, u32[]{:S(2)}) copy-start(bf16[16,256]{1,0:T(8,128)(2,1)} %w_neigh_ref.1) | copy-start | bytes 24580
  7.2 91.2 %all-gather.2.cloned.1.call-start = ((), (), s32[]{:S(2)}) async-start(), calls=%async_computation.3 | async-start | bytes 1462272 | tf_op jit(solution)/shard_map/all_gather | solution.py:168
  10.9 0.6 copy-start.15
  42.4 0.8 copy-start.4
  43.2 27.3 %copy-start.7 = (s32[96]{0:T(128)}, s32[96]{0:T(128)S(1)}, u32[]{:S(2)}) copy-start(s32[96]{0:T(128)S(1)} %reshape.38.ids_ref) | copy-start | bytes 1156
  44.6 25.9 %all-to-all-start.1 = ((bf16[48,2,16,128]{3,2,1,0:T(8,128)(2,1)}), bf16[48,2,16,128]{3,2,1,0:T(8,128)(2,1)S(1)}, u32[]{:S(2)}, u32[]{:S(2)}) async-start(bf16[48,2,16,128]{3,2,1,0:T(8,128)(2,1)} %bitcast.3), calls=%async_computation.1 | async-start | bytes 786432 | tf_op jit(solution)/shard_map/all_to_all | solution.py:179
  70.5 1.9 %copy-start = (bf16[1,48,2,128,128]{4,3,2,1,0:T(8,128)(2,1)S(1)}, bf16[1,48,2,128,128]{4,3,2,1,0:T(8,128)(2,1)}, u32[]{:S(2)}) copy-start(bf16[1,48,2,128,128]{4,3,2,1,0:T(8,128)(2,1)} %param.17) | copy-start | bytes 9437188
  72.4 0.6 copy-start.9
  73.0 0.7 copy-start.13
  73.6 24.7 %copy-start.1 = (bf16[1,48,2,128,128]{4,3,2,1,0:T(8,128)(2,1)S(1)}, bf16[1,48,2,128,128]{4,3,2,1,0:T(8,128)(2,1)}, u32[]{:S(2)}) copy-start(bf16[1,48,2,128,128]{4,3,2,1,0:T(8,128)(2,1)} %param.17) | copy-start | bytes 9437188
  77.2 0.6 copy-start.11
  77.8 57.5 %copy-start.8 = (s32[96]{0:T(128)S(1)}, s32[96]{0:T(128)}, u32[]{:S(2)}) copy-start(s32[96]{0:T(128)} %copy-done.7) | copy-start | bytes 1156
  98.4 1.0 copy-start.2
  99.4 1.3 copy-start.3
  100.7 0.6 copy-start.10
  101.4 0.7 copy-start.12
  102.0 0.7 copy-start.14
Sparse Core Ops, SparseCore 0:
  11.7 50.5 all-gather.1

commit v2 on v1

v2 whole, which is shorter than its diff:
```python
import jax
import jax.numpy as jnp
from jax import lax
from jax.experimental import pallas as pl
from jax.experimental.pallas import tpu as pltpu
from jax.sharding import Mesh, PartitionSpec as P

BLK = 128
NB = 8
CAP = 2
VMEM_LIMIT = 24 * 1024 * 1024

SMEM = pl.BlockSpec(memory_space=pltpu.SMEM)
VMEM = pl.BlockSpec(memory_space=pltpu.VMEM)
HBM = pl.BlockSpec(memory_space=pltpu.HBM)

f32 = jnp.float32
bf16 = jnp.bfloat16


def chunk_of(tiles):
    return 8 if tiles % 8 == 0 else tiles


def prepare_kernel(
    ids_hbm,
    bias_hbm,
    feats_hbm,
    cot_hbm,
    w_self_hbm,
    w_neigh_hbm,
    slab_ref,
    ask_ref,
    bundle_ref,
    pad,
    ids_ref,
    bias_ref,
    sems,
):
    rows, slab = feats_hbm.shape
    parts = ids_hbm.shape[1]
    hidden = w_self_hbm.shape[1]
    ends = (0, slab, 2 * slab, 2 * slab + hidden, 2 * slab + 2 * hidden)
    pieces = [bundle_ref.at[:, pl.ds(i, j - i)] for i, j in zip(ends, ends[1:])]
    sources = (ids_hbm, bias_hbm, feats_hbm, feats_hbm, cot_hbm, w_self_hbm, w_neigh_hbm)
    targets = [ids_ref, bias_ref, slab_ref.at[:, pl.ds(0, slab)]] + pieces
    copies = [
        pltpu.make_async_copy(source, target, sems.at[i])
        for i, (source, target) in enumerate(zip(sources, targets))
    ]
    for copy in copies:
        copy.start()
    pad[...] = jnp.zeros_like(pad)
    copies[0].wait()
    pad[0:CAP, 0:parts] = ids_ref[...]
    for i in range(ask_ref.shape[0]):
        ask_ref[i] = pad[0:CAP, :]
    row = lax.broadcasted_iota(jnp.int32, (rows, BLK), 0)
    mine = row == lax.axis_index("z")
    for c in range(CAP):
        ids = jnp.broadcast_to(pad[c : c + 1, :], (rows, BLK))
        plane = jnp.where(mine, ids, 0).astype(f32).astype(bf16)
        slab_ref[:, slab + c * BLK : slab + (c + 1) * BLK] = plane
    copies[1].wait()
    wide = jnp.broadcast_to(bias_ref[...], (rows, rows))
    place = lax.broadcasted_iota(jnp.int32, (rows, rows), 0)
    place = place == lax.broadcasted_iota(jnp.int32, (rows, rows), 1)
    bias = jnp.sum(jnp.where(place, wide, 0.0), axis=1, keepdims=True)
    high = bias.astype(bf16).astype(f32)
    middle = (bias - high).astype(bf16).astype(f32)
    low = bias - high - middle
    lane = lax.broadcasted_iota(jnp.int32, (rows, BLK), 1)
    terms = jnp.where(lane == 0, high, jnp.where(lane == 1, middle, jnp.where(lane == 2, low, 0.0)))
    bundle_ref[:, ends[-1] :] = terms.astype(bf16)
    for copy in copies[2:]:
        copy.wait()


def select_kernel(ask_ref, slabs_ref, out_ref):
    along, _, rows, _ = out_ref.shape
    column = slabs_ref.shape[0]
    slab = NB * BLK
    first = lax.axis_index("x") * column
    for i in range(along):
        for k in range(column):
            for c in range(CAP):
                start = pl.multiple_of(ask_ref[i, c, first + k] * BLK, BLK)
                out_ref[i, k * CAP + c] = slabs_ref[k, :, pl.ds(start, BLK)]
    for c in range(CAP):
        plane = jnp.zeros((rows, BLK), f32)
        for k in range(column):
            plane += slabs_ref[k, :, slab + c * BLK : slab + (c + 1) * BLK].astype(f32)
        for i in range(along):
            out_ref[i, column * CAP + c] = plane.astype(bf16)


def tile_copies(adj_ref, adj, sems, step):
    return [
        pltpu.make_async_copy(
            adj_ref.at[pl.ds(k * step, step)], adj.at[pl.ds(k * step, step)], sems.at[k]
        )
        for k in range(adj_ref.shape[0] // step)
    ]


def wait_tiles(adj_ref, adj, sems, step, k):
    part = pl.ds(pl.multiple_of(k * step, step), step)
    pltpu.make_async_copy(adj_ref.at[part], adj.at[part], sems.at[k]).wait()


def aggregate_kernel(
    dst_hbm, counts_hbm, fetched_ref, adj_ref, agg_ref, inv_hbm, dst_ref, counts_ref, inv, adj, sems, small
):
    along, slots, rows, _ = fetched_ref.shape
    per_row = slots - CAP
    chunk = chunk_of(per_row)
    step_rows = chunk * BLK
    dst_copy = pltpu.make_async_copy(dst_hbm, dst_ref, small.at[0])
    counts_copy = pltpu.make_async_copy(counts_hbm, counts_ref, small.at[1])
    dst_copy.start()
    counts_copy.start()
    for copy in tile_copies(adj_ref, adj, sems, step_rows):
        copy.start()
    row_ids = lax.broadcasted_iota(jnp.int32, (16, BLK), 0)
    zero = jnp.zeros((rows, BLK), bf16)
    chunks = per_row // chunk
    dst_copy.wait()
    counts_copy.wait()

    def step(k, acc):
        columns = []
        for i in range(chunk):
            q = k * (chunk // CAP) + i // CAP
            live = (i % CAP) < counts_ref[0, q]
            dst = jnp.where(live, dst_ref[i % CAP, q], NB)
            block = fetched_ref[k // chunks, (k % chunks) * chunk + i]
            pieces = [jnp.where(dst == n, block, zero) for n in range(NB)]
            pieces.append((row_ids == dst).astype(f32).astype(bf16))
            columns.append(jnp.concatenate(pieces, axis=0))
        lhs = jnp.concatenate(columns, axis=1)
        wait_tiles(adj_ref, adj, sems, step_rows, k)
        weights = adj[pl.ds(pl.multiple_of(k * step_rows, step_rows), step_rows), :]
        return acc + jnp.dot(lhs, weights, preferred_element_type=f32)

    acc = lax.fori_loop(0, along * chunks, step, jnp.zeros((NB * rows + 16, BLK), f32))
    inverse = 1.0 / jnp.maximum(acc[NB * rows : NB * rows + NB], 1.0)
    inv[...] = inverse
    inv_copy = pltpu.make_async_copy(inv, inv_hbm, small.at[2])
    inv_copy.start()
    for n in range(NB):
        part = acc[n * rows : (n + 1) * rows] * inverse[n : n + 1]
        agg_ref[:, n * BLK : (n + 1) * BLK] = part.astype(bf16)
    inv_copy.wait()


def update_kernel(
    dst_hbm,
    counts_hbm,
    inv_hbm,
    agg_hbm,
    bundle_hbm,
    w_self_ref,
    w_neigh_ref,
    adj_ref,
    out_ref,
    self_ref,
    grads_ref,
    dst_ref,
    counts_ref,
    inv_ref,
    agg_ref,
    bundle_ref,
    out_all,
    scaled,
    adj,
    sems,
    small,
):
    hidden, slab = agg_ref.shape
    rows = w_self_ref.shape[0]
    tiles = grads_ref.shape[0]
    chunk = chunk_of(tiles)
    step_rows = chunk * BLK
    copies = [
        pltpu.make_async_copy(source, target, small.at[i])
        for i, (source, target) in enumerate(
            (
                (bundle_hbm, bundle_ref),
                (agg_hbm, agg_ref),
                (inv_hbm, inv_ref),
                (dst_hbm, dst_ref),
                (counts_hbm, counts_ref),
            )
        )
    ]
    for copy in copies + tile_copies(adj_ref, adj, sems, step_rows):
        copy.start()
    for copy in copies:
        copy.wait()
    weights = 2 * slab
    tail = bundle_ref[:, weights + 2 * hidden : weights + 2 * hidden + BLK].astype(f32)
    bias = tail[:, 0:1] + tail[:, 1:2] + tail[:, 2:3]
    w_self_all = bundle_ref[:, weights : weights + hidden]
    w_neigh_all = bundle_ref[:, weights + hidden : weights + 2 * hidden]
    contract_rows = (((0,), (0,)), ((), ()))
    width = 2 * BLK
    for start in range(0, slab, width):
        columns = slice(start, start + width)
        preact = (
            lax.dot_general(
                w_self_all, bundle_ref[:, columns], contract_rows, preferred_element_type=f32
            )
            + lax.dot_general(
                w_neigh_all, agg_ref[:, columns], contract_rows, preferred_element_type=f32
            )
            + bias
        )
        s = 1.0 / (1.0 + jnp.exp(-preact))
        silu = preact * s
        out_all[:, columns] = silu.astype(bf16)
        cotangent = bundle_ref[:, slab + start : slab + start + width].astype(f32)
        d_preact = (cotangent * (s + silu * (1.0 - s))).astype(bf16)
        self_ref[:, columns] = jnp.dot(w_self_ref[...], d_preact, preferred_element_type=f32)
        neigh = jnp.dot(w_neigh_ref[...], d_preact, preferred_element_type=f32)
        for half in range(width // BLK):
            n = start // BLK + half
            part = neigh[:, half * BLK : (half + 1) * BLK] * inv_ref[n : n + 1]
            scaled[n] = part.astype(bf16)
    first = pl.multiple_of(lax.axis_index("feat") * rows, rows)
    out_ref[...] = out_all[pl.ds(first, rows), :]

    zero = jnp.zeros((rows, BLK), bf16)
    contract_columns = (((1,), (1,)), ((), ()))

    def step(k, carry):
        wait_tiles(adj_ref, adj, sems, step_rows, k)
        for i in range(chunk):
            t = k * chunk + i
            q = k * (chunk // CAP) + i // CAP
            live = (i % CAP) < counts_ref[0, q]
            chosen = jnp.where(live, scaled[dst_ref[i % CAP, q]], zero)
            start = pl.multiple_of(t * BLK, BLK)
            grads = lax.dot_general(
                chosen, adj[pl.ds(start, BLK), :], contract_columns, preferred_element_type=f32
            )
            grads_ref[t] = grads.astype(bf16)
        return carry

    lax.fori_loop(0, tiles // chunk, step, 0)


def sum_kernel(ids_ref, grads_ref, self_ref, out_ref):
    tiles = grads_ref.shape[0]
    along = ids_ref.shape[0]
    column = tiles // (along * CAP)

    def step(q, sums):
        for c in range(CAP):
            block = grads_ref[q * CAP + c].astype(f32)
            asked = ids_ref[q // column, c, q % column]
            sums = [total + jnp.where(asked == n, block, 0.0) for n, total in enumerate(sums)]
        return tuple(sums)

    start = tuple(self_ref[:, n * BLK : (n + 1) * BLK] for n in range(NB))
    sums = lax.fori_loop(0, tiles // CAP, step, start, unroll=2)
    for n in range(NB):
        out_ref[:, n * BLK : (n + 1) * BLK] = sums[n]


def params(limit=VMEM_LIMIT):
    return pltpu.CompilerParams(vmem_limit_bytes=limit)


def shape(dims, dtype):
    return jax.ShapeDtypeStruct(dims, dtype)


def per_device(feats, w_self, w_neigh, bias, cotangent, block_ids, req_counts, tile_dst, adjacency):
    along, column = lax.axis_size("x"), lax.axis_size("z")
    graph_parts = along * column
    hidden = w_self.shape[1]
    rows, slab = feats.shape
    tiles = graph_parts * CAP
    per_row = column * CAP
    adj = adjacency.reshape(tiles * BLK, BLK)
    dst = tile_dst[0].T
    width = 2 * slab + 2 * hidden + BLK

    packed, ask, bundle = pl.pallas_call(
        prepare_kernel,
        out_shape=(
            shape((rows, slab + CAP * BLK), bf16),
            shape((along, CAP, BLK), jnp.int32),
            shape((rows, width), bf16),
        ),
        in_specs=[HBM] * 6,
        out_specs=(VMEM,) * 3,
        scratch_shapes=[
            pltpu.VMEM((8, BLK), jnp.int32),
            pltpu.VMEM((CAP, graph_parts), jnp.int32),
            pltpu.VMEM((1, rows), f32),
            pltpu.SemaphoreType.DMA((7,)),
        ],
        compiler_params=params(66_800_000),
        name="prepare",
    )(block_ids[0].T, bias.reshape(1, rows), feats, cotangent, w_self, w_neigh)
    bundle = lax.all_gather(bundle, "feat", axis=0, tiled=True)
    asked = lax.all_to_all(ask, "x", 0, 0)
    slabs = lax.all_gather(packed, "z", axis=0)
    picked = pl.pallas_call(
        select_kernel,
        out_shape=shape((along, per_row + CAP, rows, BLK), bf16),
        in_specs=[SMEM, VMEM],
        out_specs=VMEM,
        compiler_params=params(),
        name="select_blocks",
    )(asked, slabs)
    fetched = lax.all_to_all(picked, "x", 0, 0)
    steps = along * per_row // chunk_of(per_row)
    agg, inverse = pl.pallas_call(
        aggregate_kernel,
        out_shape=(shape((rows, slab), bf16), shape((NB, BLK), f32)),
        in_specs=[HBM, HBM, VMEM, HBM],
        out_specs=(VMEM, HBM),
        scratch_shapes=[
            pltpu.SMEM((CAP, graph_parts), jnp.int32),
            pltpu.SMEM((1, graph_parts), jnp.int32),
            pltpu.VMEM((NB, BLK), f32),
            pltpu.VMEM((tiles * BLK, BLK), bf16),
            pltpu.SemaphoreType.DMA((steps,)),
            pltpu.SemaphoreType.DMA((3,)),
        ],
        compiler_params=params(66_400_000),
        name="aggregate",
    )(dst, req_counts, fetched, adj)
    agg_all = lax.all_gather(agg, "feat", axis=0, tiled=True)
    output, self_grad, grads = pl.pallas_call(
        update_kernel,
        out_shape=(
            shape((rows, slab), bf16),
            shape((rows, slab), f32),
            shape((tiles, rows, BLK), bf16),
        ),
        in_specs=[HBM] * 5 + [VMEM] * 2 + [HBM],
        out_specs=(VMEM,) * 3,
        scratch_shapes=[
            pltpu.SMEM((CAP, graph_parts), jnp.int32),
            pltpu.SMEM((1, graph_parts), jnp.int32),
            pltpu.VMEM((NB, BLK), f32),
            pltpu.VMEM((hidden, slab), bf16),
            pltpu.VMEM((hidden, width), bf16),
            pltpu.VMEM((hidden, slab), bf16),
            pltpu.VMEM((NB, rows, BLK), bf16),
            pltpu.VMEM((tiles * BLK, BLK), bf16),
            pltpu.SemaphoreType.DMA((tiles // chunk_of(tiles),)),
            pltpu.SemaphoreType.DMA((5,)),
        ],
        compiler_params=params(66_800_000),
        name="update",
    )(dst, req_counts, inverse, agg_all, bundle, w_self, w_neigh, adj)
    returned = lax.all_to_all(
        grads.reshape(graph_parts, CAP, rows, BLK), ("x", "z"), 0, 0
    ).reshape(tiles, rows, BLK)
    me = lax.axis_index("x") * column + lax.axis_index("z")
    ids = lax.dynamic_slice(
        fetched, (0, per_row, 0, me), (along, CAP, rows, 1)
    )
    ids = ids.reshape(along, CAP, rows).astype(jnp.int32)
    feat_grad = pl.pallas_call(
        sum_kernel,
        out_shape=shape((rows, slab), f32),
        in_specs=[SMEM, VMEM, VMEM],
        out_specs=VMEM,
        compiler_params=params(),
        name="sum_returned",
    )(ids, returned, self_grad)
    return (output, feat_grad)


def solution(mesh):
    graph, feat = mesh.devices.shape
    along = 4 if graph % 12 == 0 else 2
    mesh = Mesh(mesh.devices.reshape(along, graph // along, feat), ("x", "z", "feat"))
    graph = ("x", "z")
    in_specs = (
        P("feat", graph),
        P("feat", None),
        P("feat", None),
        P("feat"),
        P("feat", graph),
        P(graph, None, None),
        P(graph, None),
        P(graph, None, None),
        P(graph, None, None, None, None),
    )
    out_specs = (P("feat", graph), P("feat", graph))
    return jax.shard_map(
        per_device, mesh=mesh, in_specs=in_specs, out_specs=out_specs, check_vma=False
    )
```

time: 145 us -> 135 us (0.931)
  blocking collectives: 76.2 us -> 58.4 us
  local copies, waits for them, and re-layouts: 15.3 us -> 0.84 us
  starting transfers between devices: 6.5 us -> 19.2 us
  Pallas kernels: 12.6 us -> 20.2 us
  waiting for transfers between devices: 18 us -> 20.3 us
    all_to_all x2 -> x1, blocking collectives: 55.7 us -> 10.2 us  [per_device(): fetched = lax.all_to_all(picked, 'x', 0, 0)]
    all_gather x0 -> x1, blocking collectives: none -> 27.6 us  [per_device(): slabs = lax.all_gather(packed, 'z', axis=0)]
    all_to_all x1 -> x2, starting transfers between devices: 6.46 us -> 19.1 us  [the longest x1 12.7 us: per_device(): asked = lax.all_to_all(ask, 'x', 0, 0)]
    unnamed x37 -> x2, local copies, waits for them, and re-layouts: 13.2 us -> 0.84 us
    pallas_call x4 -> x5, Pallas kernels: 12.6 us -> 20.2 us  [the longest x1 8.38 us: per_device(): pl.pallas_call(update_kernel, out_shape=(shape((rows, slab), bf16), shape...]
    all_to_all x1 -> x2, waiting for transfers between devices: 18 us -> 20.3 us  [the longest x1 20.3 us: per_device(): lax.all_to_all(grads.reshape(graph_parts, CAP, rows, BLK), ('x', 'z'), 0, 0)]
  transfers between devices with their start and end apart: 2 -> 3, of which waited for: 1 -> 1; matrix products, arithmetic and copies ran while one was open for 2% -> 1% of each run, Pallas kernels for 3% -> 6%
where the time goes in v2:
time: 135 us; the launch traced here: 134 us
  blocking collectives  58.4 us (43%)
  waiting for transfers between devices  20.3 us (15%)
  Pallas kernels  20.2 us (15%)
  starting transfers between devices  19.2 us (14%)
  between operations  14.1 us (10%)
    all_gather x1, blocking collectives, per_device(): slabs = lax.all_gather(packed, 'z', axis=0)  27.6 us
    all_gather x1, blocking collectives, per_device(): agg_all = lax.all_gather(agg, 'feat', axis=0, tiled=True)  20.7 us
    all_to_all x1, waiting for transfers between devices, per_device(): lax.all_to_all(grads.reshape(graph_parts, CAP, rows, BLK), ('x', 'z'), 0, 0)  20.3 us
    all_to_all x1, starting transfers between devices, per_device(): asked = lax.all_to_all(ask, 'x', 0, 0)  12.7 us
    all_to_all x1, blocking collectives, per_device(): fetched = lax.all_to_all(picked, 'x', 0, 0)  10.2 us
    pallas_call x1, Pallas kernels, per_device(): pl.pallas_call(update_kernel, out_shape=(shape((rows, slab), bf16), shape...  8.38 us
    pallas_call x1, Pallas kernels, per_device(): pl.pallas_call(aggregate_kernel, out_shape=(shape((rows, slab), bf16), sh...  6.86 us
    all_to_all x1, starting transfers between devices, per_device(): lax.all_to_all(grads.reshape(graph_parts, CAP, rows, BLK), ('x', 'z'), 0, 0)  6.4 us
  transfers between devices with their start and end apart: 3, of which 1 were waited for; matrix products, arithmetic and copies ran while one was open for 1% of the time, Pallas kernels for 6%

profile of v2, /device:TPU:6, one launch (start us, length us, event | category | flops | bytes accessed | tf_op | source)
XLA Modules:
  0.0 134.0 jit_solution(567982598859992416)
XLA Ops:
  7.2 0.0 all-gather.3.cloned.1.call-start
  7.2 1.5 %prepare.1 = (bf16[16,1280]{1,0:T(8,128)(2,1)}, s32[4,2,128]{2,1,0:T(2,128)}, bf16[16,2688]{1,0:T(8,128)(2,1)}) custom-call(s32[2,48]{1,0:T(2,128)} %bitcast.18, f32[1,16]{1,0:T(1,128)} %bitcast.19, bf16[16,1024]{1,0:T(8,128)(2,1)} %feats_hbm.1, bf16[16,1024]{1,0:T(8,128)(2,1)} %cot_hbm.1, bf16[16,256]{1,0:T(8,128)(2,1)} %w_self_ref.1, ...), custom_call_target="tpu_custom_call" | custom-call | tf_op jit(solution)/shard_map/prepare/pallas_call | solution.py:289
  8.8 0.0 all-gather.3.cloned.1.call-update
  8.8 12.7 %all-to-all-start = ((s32[4,2,128]{2,1,0:T(2,128)}), s32[4,2,128]{2,1,0:T(2,128)S(1)}, u32[]{:S(2)}, u32[]{:S(2)}) async-start(s32[4,2,128]{2,1,0:T(2,128)} %get-tuple-element.10), calls=%async_computation | async-start | bytes 8192 | tf_op jit(solution)/shard_map/all_to_all | solution.py:308
  21.5 27.6 %all-gather = bf16[192,1280]{1,0:T(8,128)(2,1)S(1)} all-gather(bf16[16,1280]{1,0:T(8,128)(2,1)} %get-tuple-element.11), channel_id=2, replica_groups=mesh['x'=4,'z'=12,'feat'=16] {'z'}, dimensions={0}, use_global_device_ids=true | all-gather | bytes 532480 | tf_op jit(solution)/shard_map/all_gather | solution.py:309
  49.1 0.0 all-to-all-done.ask_ref
  49.1 0.9 select_blocks.1
  49.9 10.2 %all_to_all.15.fetched_ref = bf16[4,26,16,128]{3,2,1,0:T(8,128)(2,1)} all-to-all(bf16[4,26,16,128]{3,2,1,0:T(8,128)(2,1)S(1)} %select_blocks.1), channel_id=1, replica_groups=mesh['x'=4,'z'=12,'feat'=16] {'x'}, dimensions={0} | all-to-all | bytes 851968 | tf_op jit(solution)/shard_map/all_to_all | solution.py:318
  60.1 6.9 %aggregate.1 = (bf16[16,1024]{1,0:T(8,128)(2,1)}, f32[8,128]{1,0:T(8,128)}) custom-call(s32[2,48]{1,0:T(2,128)} %bitcast.16, s32[1,48]{1,0:T(1,128)} %counts_hbm.3, bf16[4,26,16,128]{3,2,1,0:T(8,128)(2,1)} %all_to_all.15.fetched_ref, bf16[12288,128]{1,0:T(8,128)(2,1)} %bitcast.13), custom_call_target="tpu_custom_call" | custom-call | tf_op jit(solution)/shard_map/aggregate/pallas_call | solution.py:320
  67.0 20.7 %all_gather.14.agg_hbm = bf16[256,1024]{1,0:T(8,128)(2,1)} all-gather(bf16[16,1024]{1,0:T(8,128)(2,1)} %get-tuple-element.13), channel_id=1, replica_groups=mesh['x'=4,'z'=12,'feat'=16] {'feat'}, dimensions={0}, use_global_device_ids=true | all-gather | bytes 557056 | tf_op jit(solution)/shard_map/all_gather | solution.py:336
  87.7 0.0 all-gather.3.cloned.1.call-done.bundle_hbm
  87.7 8.4 %update.1 = (bf16[16,1024]{1,0:T(8,128)(2,1)}, f32[16,1024]{1,0:T(8,128)}, bf16[96,16,128]{2,1,0:T(8,128)(2,1)}) custom-call(s32[2,48]{1,0:T(2,128)} %bitcast.17, s32[1,48]{1,0:T(1,128)} %counts_hbm.3, f32[8,128]{1,0:T(8,128)} %get-tuple-element.12.inv_hbm, bf16[256,1024]{1,0:T(8,128)(2,1)} %all_gather.14.agg_hbm, ...), custom_call_target="tpu_custom_call" | custom-call | tf_op jit(solution)/shard_map/update/pallas_call | solution.py:337
  96.1 6.4 %all-to-all-start.2 = ((bf16[48,2,16,128]{3,2,1,0:T(8,128)(2,1)}), bf16[48,2,16,128]{3,2,1,0:T(8,128)(2,1)S(1)}, u32[]{:S(2)}, u32[]{:S(2)}) async-start(bf16[48,2,16,128]{3,2,1,0:T(8,128)(2,1)} %bitcast.15), calls=%async_computation.2 | async-start | bytes 786432 | tf_op jit(solution)/shard_map/all_to_all | solution.py:361
  102.5 1.1 convert_reduce_fusion.ids_ref
  103.5 20.3 %all-to-all-done.2 = bf16[48,2,16,128]{3,2,1,0:T(8,128)(2,1)S(1)} async-done(((bf16[48,2,16,128]{3,2,1,0:T(8,128)(2,1)}), bf16[48,2,16,128]{3,2,1,0:T(8,128)(2,1)S(1)}, u32[]{:S(2)}, u32[]{:S(2)}) %all-to-all-start.2) | async-done | bytes 393248 | tf_op jit(solution)/shard_map/all_to_all | solution.py:361
  123.8 0.0 copy-start
  123.8 0.8 copy-done
  124.7 2.5 %sum_returned.1 = f32[16,1024]{1,0:T(8,128)} custom-call(s32[4,2,16]{2,1,0:T(2,128)S(1)} %convert_reduce_fusion.ids_ref, bf16[96,16,128]{2,1,0:T(8,128)(2,1)S(1)} %bitcast.12, f32[16,1024]{1,0:T(8,128)S(1)} %copy-done), custom_call_target="tpu_custom_call" | custom-call | tf_op jit(solution)/shard_map/sum_returned/pallas_call | solution.py:369
Async XLA Ops:
  7.2 80.5 %all-gather.3.cloned.1.call-start = ((), (), s32[]{:S(2)}) async-start(), calls=%async_computation.3 | async-start | bytes 1462272 | tf_op jit(solution)/shard_map/all_gather | solution.py:307
  8.8 40.3 %all-to-all-start = ((s32[4,2,128]{2,1,0:T(2,128)}), s32[4,2,128]{2,1,0:T(2,128)S(1)}, u32[]{:S(2)}, u32[]{:S(2)}) async-start(s32[4,2,128]{2,1,0:T(2,128)} %get-tuple-element.10), calls=%async_computation | async-start | bytes 8192 | tf_op jit(solution)/shard_map/all_to_all | solution.py:308
  96.1 27.8 %all-to-all-start.2 = ((bf16[48,2,16,128]{3,2,1,0:T(8,128)(2,1)}), bf16[48,2,16,128]{3,2,1,0:T(8,128)(2,1)S(1)}, u32[]{:S(2)}, u32[]{:S(2)}) async-start(bf16[48,2,16,128]{3,2,1,0:T(8,128)(2,1)} %bitcast.15), calls=%async_computation.2 | async-start | bytes 786432 | tf_op jit(solution)/shard_map/all_to_all | solution.py:361
  123.8 0.8 copy-start
Sparse Core Ops, SparseCore 0:
  10.4 50.6 all-gather.2

commit v3 on v2

--- a/solution.py
+++ b/solution.py
@@ -31,11 +31,13 @@
     w_neigh_hbm,
     slab_ref,
     ask_ref,
+    out_hbm,
     bundle_ref,
     pad,
     ids_ref,
     bias_ref,
     sems,
+    out_sems,
 ):
     rows, slab = feats_hbm.shape
     parts = ids_hbm.shape[1]
@@ -53,8 +55,7 @@
     pad[...] = jnp.zeros_like(pad)
     copies[0].wait()
     pad[0:CAP, 0:parts] = ids_ref[...]
-    for i in range(ask_ref.shape[0]):
-        ask_ref[i] = pad[0:CAP, :]
+    ask_ref[...] = pad[0:CAP, :]
     row = lax.broadcasted_iota(jnp.int32, (rows, BLK), 0)
     mine = row == lax.axis_index("z")
     for c in range(CAP):
@@ -74,24 +75,40 @@
     bundle_ref[:, ends[-1] :] = terms.astype(bf16)
     for copy in copies[2:]:
         copy.wait()
-
-
-def select_kernel(ask_ref, slabs_ref, out_ref):
+    copies = [
+        pltpu.make_async_copy(bundle_ref, out_hbm.at[i], out_sems.at[i])
+        for i in range(out_hbm.shape[0])
+    ]
+    for copy in copies:
+        copy.start()
+    for copy in copies:
+        copy.wait()
+
+
+def select_kernel(*refs):
+    *asks, slabs_ref, out_ref, ask_ref, sems = refs
+    copies = [
+        pltpu.make_async_copy(ask, ask_ref.at[s], sems.at[s]) for s, ask in enumerate(asks)
+    ]
+    for copy in copies:
+        copy.start()
     along, _, rows, _ = out_ref.shape
     column = slabs_ref.shape[0]
     slab = NB * BLK
-    first = lax.axis_index("x") * column
-    for i in range(along):
-        for k in range(column):
-            for c in range(CAP):
-                start = pl.multiple_of(ask_ref[i, c, first + k] * BLK, BLK)
-                out_ref[i, k * CAP + c] = slabs_ref[k, :, pl.ds(start, BLK)]
+    x = lax.axis_index("x")
     for c in range(CAP):
         plane = jnp.zeros((rows, BLK), f32)
         for k in range(column):
             plane += slabs_ref[k, :, slab + c * BLK : slab + (c + 1) * BLK].astype(f32)
         for i in range(along):
             out_ref[i, column * CAP + c] = plane.astype(bf16)
+    for s in range(along):
+        copies[s].wait()
+        i = lax.rem(x - s + along, along)
+        for k in range(column):
+            for c in range(CAP):
+                start = pl.multiple_of(ask_ref[s, c, x * column + k] * BLK, BLK)
+                out_ref[i, k * CAP + c] = slabs_ref[k, :, pl.ds(start, BLK)]
 
 
 def tile_copies(adj_ref, adj, sems, step):
@@ -249,8 +266,10 @@
     lax.fori_loop(0, tiles // chunk, step, 0)
 
 
-def sum_kernel(ids_ref, grads_ref, self_ref, out_ref):
-    tiles = grads_ref.shape[0]
+def sum_kernel(ids_ref, grads_ref, self_hbm, out_ref, self_ref, sem):
+    self_copy = pltpu.make_async_copy(self_hbm, self_ref, sem)
+    self_copy.start()
+    tiles, rows, _ = grads_ref.shape
     along = ids_ref.shape[0]
     column = tiles // (along * CAP)
 
@@ -261,10 +280,12 @@
             sums = [total + jnp.where(asked == n, block, 0.0) for n, total in enumerate(sums)]
         return tuple(sums)
 
-    start = tuple(self_ref[:, n * BLK : (n + 1) * BLK] for n in range(NB))
+    start = (jnp.zeros((rows, BLK), f32),) * NB
     sums = lax.fori_loop(0, tiles // CAP, step, start, unroll=2)
+    self_copy.wait()
     for n in range(NB):
-        out_ref[:, n * BLK : (n + 1) * BLK] = sums[n]
+        columns = slice(n * BLK, (n + 1) * BLK)
+        out_ref[:, columns] = self_ref[:, columns] + sums[n]
 
 
 def params(limit=VMEM_LIMIT):
@@ -285,36 +306,47 @@
     adj = adjacency.reshape(tiles * BLK, BLK)
     dst = tile_dst[0].T
     width = 2 * slab + 2 * hidden + BLK
+    receivers = lax.axis_size("feat")
 
     packed, ask, bundle = pl.pallas_call(
         prepare_kernel,
         out_shape=(
             shape((rows, slab + CAP * BLK), bf16),
-            shape((along, CAP, BLK), jnp.int32),
-            shape((rows, width), bf16),
+            shape((CAP, BLK), jnp.int32),
+            shape((receivers, rows, width), bf16),
         ),
         in_specs=[HBM] * 6,
-        out_specs=(VMEM,) * 3,
+        out_specs=(VMEM, VMEM, HBM),
         scratch_shapes=[
+            pltpu.VMEM((rows, width), bf16),
             pltpu.VMEM((8, BLK), jnp.int32),
             pltpu.VMEM((CAP, graph_parts), jnp.int32),
             pltpu.VMEM((1, rows), f32),
             pltpu.SemaphoreType.DMA((7,)),
+            pltpu.SemaphoreType.DMA((receivers,)),
         ],
         compiler_params=params(66_800_000),
         name="prepare",
     )(block_ids[0].T, bias.reshape(1, rows), feats, cotangent, w_self, w_neigh)
-    bundle = lax.all_gather(bundle, "feat", axis=0, tiled=True)
-    asked = lax.all_to_all(ask, "x", 0, 0)
+    bundle = lax.all_to_all(bundle, "feat", 0, 0).reshape(hidden, width)
+    asked = [ask] + [
+        lax.ppermute(ask, "x", [(i, (i + s) % along) for i in range(along)])
+        for s in range(1, along)
+    ]
     slabs = lax.all_gather(packed, "z", axis=0)
     picked = pl.pallas_call(
         select_kernel,
         out_shape=shape((along, per_row + CAP, rows, BLK), bf16),
-        in_specs=[SMEM, VMEM],
+        in_specs=[HBM] * along + [VMEM],
         out_specs=VMEM,
+        scratch_shapes=[
+            pltpu.SMEM((along, CAP, BLK), jnp.int32),
+            pltpu.SemaphoreType.DMA((along,)),
+        ],
         compiler_params=params(),
         name="select_blocks",
-    )(asked, slabs)
+    )(*asked, slabs)
+    picked, bundle = lax.optimization_barrier((picked, bundle))
     fetched = lax.all_to_all(picked, "x", 0, 0)
     steps = along * per_row // chunk_of(per_row)
     agg, inverse = pl.pallas_call(
@@ -369,9 +401,10 @@
     feat_grad = pl.pallas_call(
         sum_kernel,
         out_shape=shape((rows, slab), f32),
-        in_specs=[SMEM, VMEM, VMEM],
+        in_specs=[SMEM, VMEM, HBM],
         out_specs=VMEM,
-        compiler_params=params(),
+        scratch_shapes=[pltpu.VMEM((rows, slab), f32), pltpu.SemaphoreType.DMA],
+        compiler_params=params(66_500_000),
         name="sum_returned",
     )(ids, returned, self_grad)
     return (output, feat_grad)

time: 135 us -> 134 us (level)
  between operations: 14.1 us -> 0.77 us
  starting transfers between devices: 19.2 us -> 26.9 us
  blocking collectives: 58.4 us -> 62 us
  Pallas kernels: 20.2 us -> 21.8 us
    ppermute x0 -> x3, starting transfers between devices: none -> 13.2 us  [per_device(): lax.ppermute(ask, 'x', [(i, (i + s) % along) for i in range(along)])]
    all_to_all x1, starting transfers between devices: 12.7 us -> 7.35 us  [per_device(): bundle = lax.all_to_all(bundle, 'feat', 0, 0).reshape(hidden, width)]
    all_gather x1, blocking collectives: 27.6 us -> 31.9 us  [per_device(): slabs = lax.all_gather(packed, 'z', axis=0)]
  transfers between devices with their start and end apart: 3 -> 5, of which waited for: 1 -> 1; matrix products, arithmetic and copies ran while one was open for 1% -> 1% of each run, Pallas kernels for 6% -> 1%
where the time goes in v3:
time: 134 us
  blocking collectives  62 us (46%)
  starting transfers between devices  26.9 us (20%)
  Pallas kernels  21.8 us (16%)
  waiting for transfers between devices  19.7 us (15%)
  other arithmetic  1.66 us (1%)
    all_gather x1, blocking collectives, per_device(): slabs = lax.all_gather(packed, 'z', axis=0)  31.9 us
    all_gather x1, blocking collectives, per_device(): agg_all = lax.all_gather(agg, 'feat', axis=0, tiled=True)  20.2 us
    all_to_all x1, waiting for transfers between devices, per_device(): lax.all_to_all(grads.reshape(graph_parts, CAP, rows, BLK), ('x', 'z'), 0, 0)  19.7 us
    ppermute x3, starting transfers between devices, per_device(): lax.ppermute(ask, 'x', [(i, (i + s) % along) for i in range(along)])  13.2 us
    all_to_all x1, blocking collectives, per_device(): fetched = lax.all_to_all(picked, 'x', 0, 0)  9.9 us
    pallas_call x1, Pallas kernels, per_device(): pl.pallas_call(update_kernel, out_shape=(shape((rows, slab), bf16), shape...  8.39 us
    all_to_all x1, starting transfers between devices, per_device(): bundle = lax.all_to_all(bundle, 'feat', 0, 0).reshape(hidden, width)  7.35 us
    pallas_call x1, Pallas kernels, per_device(): pl.pallas_call(aggregate_kernel, out_shape=(shape((rows, slab), bf16), sh...  6.86 us
  transfers between devices with their start and end apart: 5, of which 1 were waited for; matrix products, arithmetic and copies ran while one was open for 1% of the time, Pallas kernels for 1%

profile of v3, /device:TPU:6, one launch (start us, length us, event | category | flops | bytes accessed | tf_op | source)
XLA Modules:
  0.0 133.7 jit_solution(2157447747394011659)
XLA Ops:
  0.6 2.8 %prepare.1 = (bf16[16,1280]{1,0:T(8,128)(2,1)}, s32[2,128]{1,0:T(2,128)}, bf16[16,16,2688]{2,1,0:T(8,128)(2,1)}) custom-call(s32[2,48]{1,0:T(2,128)} %bitcast.20, f32[1,16]{1,0:T(1,128)} %bitcast.21, bf16[16,1024]{1,0:T(8,128)(2,1)} %feats_hbm.1, bf16[16,1024]{1,0:T(8,128)(2,1)} %cot_hbm.1, bf16[16,256]{1,0:T(8,128)(2,1)} %w_self_ref.1, ...), custom_call_target="tpu_custom_call" | custom-call | tf_op jit(solution)/shard_map/prepare/pallas_call | solution.py:311
  3.4 0.0 copy-start
  3.4 0.0 copy-start.3
  3.4 7.3 %all-to-all-start = ((bf16[16,16,2688]{2,1,0:T(8,128)(2,1)}), bf16[16,16,2688]{2,1,0:T(8,128)(2,1)S(1)}, u32[]{:S(2)}, u32[]{:S(2)}) async-start(bf16[16,16,2688]{2,1,0:T(8,128)(2,1)} %get-tuple-element.14), calls=%async_computation | async-start | bytes 2752512 | tf_op jit(solution)/shard_map/all_to_all | solution.py:331
  10.8 0.0 copy-done
  10.8 2.7 %collective-permute-start.2 = (s32[2,128]{1,0:T(2,128)S(1)}, s32[2,128]{1,0:T(2,128)S(1)}, u32[]{:S(2)}, u32[]{:S(2)}) collective-permute-start(s32[2,128]{1,0:T(2,128)S(1)} %copy-done), channel_id=1, source_target_pairs={{0,576},{192,0},{384,192},{576,384},{1,577},{193,1},{385,193},{577... | collective-permute-start | bytes 3080 | tf_op jit(solution)/shard_map/ppermute | solution.py:333
  13.5 8.5 %collective-permute-start.1 = (s32[2,128]{1,0:T(2,128)S(1)}, s32[2,128]{1,0:T(2,128)S(1)}, u32[]{:S(2)}, u32[]{:S(2)}) collective-permute-start(s32[2,128]{1,0:T(2,128)S(1)} %copy-done), channel_id=1, source_target_pairs={{0,384},{192,576},{384,0},{576,192},{1,385},{193,577},{385,1},{577... | collective-permute-start | bytes 3080 | tf_op jit(solution)/shard_map/ppermute | solution.py:333
  22.1 1.9 %collective-permute-start = (s32[2,128]{1,0:T(2,128)S(1)}, s32[2,128]{1,0:T(2,128)S(1)}, u32[]{:S(2)}, u32[]{:S(2)}) collective-permute-start(s32[2,128]{1,0:T(2,128)S(1)} %copy-done), channel_id=1, source_target_pairs={{0,192},{192,384},{384,576},{576,0},{1,193},{193,385},{385,577},{5... | collective-permute-start | bytes 3080 | tf_op jit(solution)/shard_map/ppermute | solution.py:333
  24.0 0.0 copy-done.3
  24.0 31.9 %all-gather = bf16[192,1280]{1,0:T(8,128)(2,1)S(1)} all-gather(bf16[16,1280]{1,0:T(8,128)(2,1)S(1)} %copy-done.3), channel_id=2, replica_groups=mesh['x'=4,'z'=12,'feat'=16] {'z'}, dimensions={0}, use_global_device_ids=true | all-gather | bytes 532480 | tf_op jit(solution)/shard_map/all_gather | solution.py:336
  55.9 0.0 collective-permute-done.2.refs_3_
  55.9 0.0 collective-permute-done.1.refs_2_
  55.9 0.0 collective-permute-done.refs_1_
  55.9 0.9 select_blocks.1
  56.8 0.0 all-to-all-done
  56.8 0.0 copy-start.1
  56.8 9.9 %all_to_all.15.fetched_ref = bf16[4,26,16,128]{3,2,1,0:T(8,128)(2,1)} all-to-all(bf16[4,26,16,128]{3,2,1,0:T(8,128)(2,1)S(1)} %select_blocks.1), channel_id=1, replica_groups=mesh['x'=4,'z'=12,'feat'=16] {'x'}, dimensions={0} | all-to-all | bytes 851968 | tf_op jit(solution)/shard_map/all_to_all | solution.py:350
  66.7 0.0 copy-done.1
  66.7 6.9 %aggregate.1 = (bf16[16,1024]{1,0:T(8,128)(2,1)}, f32[8,128]{1,0:T(8,128)}) custom-call(s32[2,48]{1,0:T(2,128)} %bitcast.18, s32[1,48]{1,0:T(1,128)} %counts_hbm.3, bf16[4,26,16,128]{3,2,1,0:T(8,128)(2,1)} %all_to_all.15.fetched_ref, bf16[12288,128]{1,0:T(8,128)(2,1)} %bitcast.13), custom_call_target="tpu_custom_call" | custom-call | tf_op jit(solution)/shard_map/aggregate/pallas_call | solution.py:352
  73.6 20.2 %all_gather.11.agg_hbm = bf16[256,1024]{1,0:T(8,128)(2,1)} all-gather(bf16[16,1024]{1,0:T(8,128)(2,1)} %get-tuple-element.17), channel_id=1, replica_groups=mesh['x'=4,'z'=12,'feat'=16] {'feat'}, dimensions={0}, use_global_device_ids=true | all-gather | bytes 557056 | tf_op jit(solution)/shard_map/all_gather | solution.py:368
  93.8 8.4 %update.1 = (bf16[16,1024]{1,0:T(8,128)(2,1)}, f32[16,1024]{1,0:T(8,128)}, bf16[96,16,128]{2,1,0:T(8,128)(2,1)}) custom-call(s32[2,48]{1,0:T(2,128)} %bitcast.19, s32[1,48]{1,0:T(1,128)} %counts_hbm.3, f32[8,128]{1,0:T(8,128)} %get-tuple-element.16.inv_hbm, bf16[256,1024]{1,0:T(8,128)(2,1)} %all_gather.11.agg_hbm, bf16[256,2688]{1,0:T(8,128)(2,1)} %bitcast.15, ...), custom_call_target="tpu_custom_call" | custom-call | tf_op jit(solution)/shard_map/update/pallas_call | solution.py:369
  102.2 6.4 %all-to-all-start.2 = ((bf16[48,2,16,128]{3,2,1,0:T(8,128)(2,1)}), bf16[48,2,16,128]{3,2,1,0:T(8,128)(2,1)S(1)}, u32[]{:S(2)}, u32[]{:S(2)}) async-start(bf16[48,2,16,128]{3,2,1,0:T(8,128)(2,1)} %bitcast.17), calls=%async_computation.2 | async-start | bytes 786432 | tf_op jit(solution)/shard_map/all_to_all | solution.py:393
  108.6 1.7 %convert_reduce_fusion.ids_ref = s32[4,2,16]{2,1,0:T(2,128)} fusion(bf16[4,26,16,128]{3,2,1,0:T(8,128)(2,1)} %all_to_all.15.fetched_ref, s32[]{:T(128)S(6)} %select_n.3), kind=kLoop, calls=%fused_computation | loop fusion | flops 128 | bytes 772 | tf_op jit(solution)/shard_map/convert_element_type | solution.py:400
  110.3 19.7 %all-to-all-done.2 = bf16[48,2,16,128]{3,2,1,0:T(8,128)(2,1)S(1)} async-done(((bf16[48,2,16,128]{3,2,1,0:T(8,128)(2,1)}), bf16[48,2,16,128]{3,2,1,0:T(8,128)(2,1)S(1)}, u32[]{:S(2)}, u32[]{:S(2)}) %all-to-all-start.2) | async-done | bytes 393248 | tf_op jit(solution)/shard_map/all_to_all | solution.py:393
  129.9 0.0 copy-start.2
  130.0 0.7 copy-done.2
  130.7 3.0 %sum_returned.1 = f32[16,1024]{1,0:T(8,128)} custom-call(s32[4,2,16]{2,1,0:T(2,128)} %convert_reduce_fusion.ids_ref, bf16[96,16,128]{2,1,0:T(8,128)(2,1)} %bitcast.16, f32[16,1024]{1,0:T(8,128)} %get-tuple-element.21.self_hbm), custom_call_target="tpu_custom_call" | custom-call | tf_op jit(solution)/shard_map/sum_returned/pallas_call | solution.py:401
Async XLA Ops:
  3.4 7.4 %copy-start = (s32[2,128]{1,0:T(2,128)S(1)}, s32[2,128]{1,0:T(2,128)}, u32[]{:S(2)}) copy-start(s32[2,128]{1,0:T(2,128)} %get-tuple-element.12.refs_0_) | copy-start | bytes 3076
  3.4 20.6 %copy-start.3 = (bf16[16,1280]{1,0:T(8,128)(2,1)S(1)}, bf16[16,1280]{1,0:T(8,128)(2,1)}, u32[]{:S(2)}) copy-start(bf16[16,1280]{1,0:T(8,128)(2,1)} %get-tuple-element.13) | copy-start | bytes 122884
  3.4 53.4 %all-to-all-start = ((bf16[16,16,2688]{2,1,0:T(8,128)(2,1)}), bf16[16,16,2688]{2,1,0:T(8,128)(2,1)S(1)}, u32[]{:S(2)}, u32[]{:S(2)}) async-start(bf16[16,16,2688]{2,1,0:T(8,128)(2,1)} %get-tuple-element.14), calls=%async_computation | async-start | bytes 2752512 | tf_op jit(solution)/shard_map/all_to_all | solution.py:331
  10.8 45.1 %collective-permute-start.2 = (s32[2,128]{1,0:T(2,128)S(1)}, s32[2,128]{1,0:T(2,128)S(1)}, u32[]{:S(2)}, u32[]{:S(2)}) collective-permute-start(s32[2,128]{1,0:T(2,128)S(1)} %copy-done), channel_id=1, source_target_pairs={{0,576},{192,0},{384,192},{576,384},{1,577},{193,1},{385,193},{577... | collective-permute-start | bytes 3080 | tf_op jit(solution)/shard_map/ppermute | solution.py:333
  13.5 42.4 %collective-permute-start.1 = (s32[2,128]{1,0:T(2,128)S(1)}, s32[2,128]{1,0:T(2,128)S(1)}, u32[]{:S(2)}, u32[]{:S(2)}) collective-permute-start(s32[2,128]{1,0:T(2,128)S(1)} %copy-done), channel_id=1, source_target_pairs={{0,384},{192,576},{384,0},{576,192},{1,385},{193,577},{385,1},{577... | collective-permute-start | bytes 3080 | tf_op jit(solution)/shard_map/ppermute | solution.py:333
  22.1 33.9 %collective-permute-start = (s32[2,128]{1,0:T(2,128)S(1)}, s32[2,128]{1,0:T(2,128)S(1)}, u32[]{:S(2)}, u32[]{:S(2)}) collective-permute-start(s32[2,128]{1,0:T(2,128)S(1)} %copy-done), channel_id=1, source_target_pairs={{0,192},{192,384},{384,576},{576,0},{1,193},{193,385},{385,577},{5... | collective-permute-start | bytes 3080 | tf_op jit(solution)/shard_map/ppermute | solution.py:333
  56.8 9.9 %copy-start.1 = (bf16[16,16,2688]{2,1,0:T(8,128)(2,1)}, bf16[16,16,2688]{2,1,0:T(8,128)(2,1)S(1)}, u32[]{:S(2)}) copy-start(bf16[16,16,2688]{2,1,0:T(8,128)(2,1)S(1)} %all-to-all-done) | copy-start | bytes 4128772
  102.2 27.8 %all-to-all-start.2 = ((bf16[48,2,16,128]{3,2,1,0:T(8,128)(2,1)}), bf16[48,2,16,128]{3,2,1,0:T(8,128)(2,1)S(1)}, u32[]{:S(2)}, u32[]{:S(2)}) async-start(bf16[48,2,16,128]{3,2,1,0:T(8,128)(2,1)} %bitcast.17), calls=%async_computation.2 | async-start | bytes 786432 | tf_op jit(solution)/shard_map/all_to_all | solution.py:393
  129.9 0.7 copy-start.2

commit v4 on v3

--- a/solution.py
+++ b/solution.py
@@ -85,30 +85,22 @@
         copy.wait()
 
 
-def select_kernel(*refs):
-    *asks, slabs_ref, out_ref, ask_ref, sems = refs
-    copies = [
-        pltpu.make_async_copy(ask, ask_ref.at[s], sems.at[s]) for s, ask in enumerate(asks)
-    ]
-    for copy in copies:
-        copy.start()
+def select_kernel(ask_ref, slabs_ref, out_ref):
     along, _, rows, _ = out_ref.shape
     column = slabs_ref.shape[0]
     slab = NB * BLK
-    x = lax.axis_index("x")
+    first = lax.axis_index("x") * column
+    for i in range(along):
+        for k in range(column):
+            for c in range(CAP):
+                start = pl.multiple_of(ask_ref[i, c, first + k] * BLK, BLK)
+                out_ref[i, k * CAP + c] = slabs_ref[k, :, pl.ds(start, BLK)]
     for c in range(CAP):
         plane = jnp.zeros((rows, BLK), f32)
         for k in range(column):
             plane += slabs_ref[k, :, slab + c * BLK : slab + (c + 1) * BLK].astype(f32)
         for i in range(along):
             out_ref[i, column * CAP + c] = plane.astype(bf16)
-    for s in range(along):
-        copies[s].wait()
-        i = lax.rem(x - s + along, along)
-        for k in range(column):
-            for c in range(CAP):
-                start = pl.multiple_of(ask_ref[s, c, x * column + k] * BLK, BLK)
-                out_ref[i, k * CAP + c] = slabs_ref[k, :, pl.ds(start, BLK)]
 
 
 def tile_copies(adj_ref, adj, sems, step):
@@ -126,7 +118,20 @@
 
 
 def aggregate_kernel(
-    dst_hbm, counts_hbm, fetched_ref, adj_ref, agg_ref, inv_hbm, dst_ref, counts_ref, inv, adj, sems, small
+    dst_hbm,
+    counts_hbm,
+    fetched_hbm,
+    adj_ref,
+    agg_ref,
+    inv_hbm,
+    dst_ref,
+    counts_ref,
+    fetched_ref,
+    inv,
+    acc_ref,
+    adj,
+    sems,
+    small,
 ):
     along, slots, rows, _ = fetched_ref.shape
     per_row = slots - CAP
@@ -134,6 +139,8 @@
     step_rows = chunk * BLK
     dst_copy = pltpu.make_async_copy(dst_hbm, dst_ref, small.at[0])
     counts_copy = pltpu.make_async_copy(counts_hbm, counts_ref, small.at[1])
+    fetched_copy = pltpu.make_async_copy(fetched_hbm, fetched_ref, small.at[3])
+    fetched_copy.start()
     dst_copy.start()
     counts_copy.start()
     for copy in tile_copies(adj_ref, adj, sems, step_rows):
@@ -143,29 +150,32 @@
     chunks = per_row // chunk
     dst_copy.wait()
     counts_copy.wait()
-
-    def step(k, acc):
-        columns = []
+    fetched_copy.wait()
+
+    acc_ref[...] = jnp.zeros_like(acc_ref)
+    ones = jnp.ones((rows, BLK), bf16)
+
+    def step(k, carry):
+        wait_tiles(adj_ref, adj, sems, step_rows, k)
+        products = []
+        for i in range(chunk):
+            block = fetched_ref[k // chunks, (k % chunks) * chunk + i]
+            start = pl.multiple_of((k * chunk + i) * BLK, BLK)
+            products.append(jnp.dot(jnp.concatenate([block, ones], axis=0), adj[pl.ds(start, BLK), :], preferred_element_type=f32))
         for i in range(chunk):
             q = k * (chunk // CAP) + i // CAP
             live = (i % CAP) < counts_ref[0, q]
             dst = jnp.where(live, dst_ref[i % CAP, q], NB)
-            block = fetched_ref[k // chunks, (k % chunks) * chunk + i]
-            pieces = [jnp.where(dst == n, block, zero) for n in range(NB)]
-            pieces.append((row_ids == dst).astype(f32).astype(bf16))
-            columns.append(jnp.concatenate(pieces, axis=0))
-        lhs = jnp.concatenate(columns, axis=1)
-        wait_tiles(adj_ref, adj, sems, step_rows, k)
-        weights = adj[pl.ds(pl.multiple_of(k * step_rows, step_rows), step_rows), :]
-        return acc + jnp.dot(lhs, weights, preferred_element_type=f32)
-
-    acc = lax.fori_loop(0, along * chunks, step, jnp.zeros((NB * rows + 16, BLK), f32))
-    inverse = 1.0 / jnp.maximum(acc[NB * rows : NB * rows + NB], 1.0)
-    inv[...] = inverse
+            acc_ref[dst] += products[i][0 : rows + 8]
+        return carry
+
+    lax.fori_loop(0, along * chunks, step, 0)
+    for n in range(NB):
+        inv[n : n + 1] = 1.0 / jnp.maximum(acc_ref[n, rows : rows + 1], 1.0)
     inv_copy = pltpu.make_async_copy(inv, inv_hbm, small.at[2])
     inv_copy.start()
     for n in range(NB):
-        part = acc[n * rows : (n + 1) * rows] * inverse[n : n + 1]
+        part = acc_ref[n, 0:rows] * inv[n : n + 1]
         agg_ref[:, n * BLK : (n + 1) * BLK] = part.astype(bf16)
     inv_copy.wait()
 
@@ -176,8 +186,6 @@
     inv_hbm,
     agg_hbm,
     bundle_hbm,
-    w_self_ref,
-    w_neigh_ref,
     adj_ref,
     out_ref,
     self_ref,
@@ -194,8 +202,7 @@
     small,
 ):
     hidden, slab = agg_ref.shape
-    rows = w_self_ref.shape[0]
-    tiles = grads_ref.shape[0]
+    tiles, rows, _ = grads_ref.shape
     chunk = chunk_of(tiles)
     step_rows = chunk * BLK
     copies = [
@@ -210,11 +217,16 @@
             )
         )
     ]
-    for copy in copies + tile_copies(adj_ref, adj, sems, step_rows):
+    for copy in copies:
         copy.start()
     for copy in copies:
         copy.wait()
+    for copy in tile_copies(adj_ref, adj, sems, step_rows):
+        copy.start()
     weights = 2 * slab
+    first = pl.multiple_of(lax.axis_index("feat") * rows, rows)
+    w_self = bundle_ref[pl.ds(first, rows), weights : weights + hidden]
+    w_neigh = bundle_ref[pl.ds(first, rows), weights + hidden : weights + 2 * hidden]
     tail = bundle_ref[:, weights + 2 * hidden : weights + 2 * hidden + BLK].astype(f32)
     bias = tail[:, 0:1] + tail[:, 1:2] + tail[:, 2:3]
     w_self_all = bundle_ref[:, weights : weights + hidden]
@@ -237,13 +249,12 @@
         out_all[:, columns] = silu.astype(bf16)
         cotangent = bundle_ref[:, slab + start : slab + start + width].astype(f32)
         d_preact = (cotangent * (s + silu * (1.0 - s))).astype(bf16)
-        self_ref[:, columns] = jnp.dot(w_self_ref[...], d_preact, preferred_element_type=f32)
-        neigh = jnp.dot(w_neigh_ref[...], d_preact, preferred_element_type=f32)
+        self_ref[:, columns] = jnp.dot(w_self, d_preact, preferred_element_type=f32)
+        neigh = jnp.dot(w_neigh, d_preact, preferred_element_type=f32)
         for half in range(width // BLK):
             n = start // BLK + half
             part = neigh[:, half * BLK : (half + 1) * BLK] * inv_ref[n : n + 1]
             scaled[n] = part.astype(bf16)
-    first = pl.multiple_of(lax.axis_index("feat") * rows, rows)
     out_ref[...] = out_all[pl.ds(first, rows), :]
 
     zero = jnp.zeros((rows, BLK), bf16)
@@ -266,26 +277,24 @@
     lax.fori_loop(0, tiles // chunk, step, 0)
 
 
-def sum_kernel(ids_ref, grads_ref, self_hbm, out_ref, self_ref, sem):
+def sum_kernel(ids_ref, grads_ref, self_hbm, out_ref, self_ref, sums, sem):
     self_copy = pltpu.make_async_copy(self_hbm, self_ref, sem)
     self_copy.start()
     tiles, rows, _ = grads_ref.shape
     along = ids_ref.shape[0]
     column = tiles // (along * CAP)
-
-    def step(q, sums):
+    sums[...] = jnp.zeros_like(sums)
+    for q in range(tiles // CAP):
         for c in range(CAP):
             block = grads_ref[q * CAP + c].astype(f32)
-            asked = ids_ref[q // column, c, q % column]
-            sums = [total + jnp.where(asked == n, block, 0.0) for n, total in enumerate(sums)]
-        return tuple(sums)
-
-    start = (jnp.zeros((rows, BLK), f32),) * NB
-    sums = lax.fori_loop(0, tiles // CAP, step, start, unroll=2)
+            sums[c, ids_ref[q // column, c, q % column]] += block
     self_copy.wait()
     for n in range(NB):
         columns = slice(n * BLK, (n + 1) * BLK)
-        out_ref[:, columns] = self_ref[:, columns] + sums[n]
+        total = self_ref[:, columns]
+        for c in range(CAP):
+            total += sums[c, n]
+        out_ref[:, columns] = total
 
 
 def params(limit=VMEM_LIMIT):
@@ -296,19 +305,12 @@
     return jax.ShapeDtypeStruct(dims, dtype)
 
 
-def per_device(feats, w_self, w_neigh, bias, cotangent, block_ids, req_counts, tile_dst, adjacency):
-    along, column = lax.axis_size("x"), lax.axis_size("z")
-    graph_parts = along * column
+def prepare(block_ids, bias, feats, cotangent, w_self, w_neigh, receivers):
+    rows, slab = feats.shape
     hidden = w_self.shape[1]
-    rows, slab = feats.shape
-    tiles = graph_parts * CAP
-    per_row = column * CAP
-    adj = adjacency.reshape(tiles * BLK, BLK)
-    dst = tile_dst[0].T
+    graph_parts = block_ids.shape[1]
     width = 2 * slab + 2 * hidden + BLK
-    receivers = lax.axis_size("feat")
-
-    packed, ask, bundle = pl.pallas_call(
+    return pl.pallas_call(
         prepare_kernel,
         out_shape=(
             shape((rows, slab + CAP * BLK), bf16),
@@ -327,60 +329,63 @@
         ],
         compiler_params=params(66_800_000),
         name="prepare",
-    )(block_ids[0].T, bias.reshape(1, rows), feats, cotangent, w_self, w_neigh)
-    bundle = lax.all_to_all(bundle, "feat", 0, 0).reshape(hidden, width)
-    asked = [ask] + [
-        lax.ppermute(ask, "x", [(i, (i + s) % along) for i in range(along)])
-        for s in range(1, along)
-    ]
-    slabs = lax.all_gather(packed, "z", axis=0)
-    picked = pl.pallas_call(
+    )(block_ids, bias, feats, cotangent, w_self, w_neigh)
+
+
+def select(asked, slabs, along):
+    column, rows, _ = slabs.shape
+    return pl.pallas_call(
         select_kernel,
-        out_shape=shape((along, per_row + CAP, rows, BLK), bf16),
-        in_specs=[HBM] * along + [VMEM],
+        out_shape=shape((along, column * CAP + CAP, rows, BLK), bf16),
+        in_specs=[SMEM, VMEM],
         out_specs=VMEM,
-        scratch_shapes=[
-            pltpu.SMEM((along, CAP, BLK), jnp.int32),
-            pltpu.SemaphoreType.DMA((along,)),
-        ],
         compiler_params=params(),
         name="select_blocks",
-    )(*asked, slabs)
-    picked, bundle = lax.optimization_barrier((picked, bundle))
-    fetched = lax.all_to_all(picked, "x", 0, 0)
-    steps = along * per_row // chunk_of(per_row)
-    agg, inverse = pl.pallas_call(
+    )(asked, slabs)
+
+
+def aggregate(dst, counts, fetched, adj):
+    along, slots, rows, _ = fetched.shape
+    tiles = along * (slots - CAP)
+    steps = tiles // chunk_of(slots - CAP)
+    return pl.pallas_call(
         aggregate_kernel,
-        out_shape=(shape((rows, slab), bf16), shape((NB, BLK), f32)),
-        in_specs=[HBM, HBM, VMEM, HBM],
+        out_shape=(shape((rows, NB * BLK), bf16), shape((NB, BLK), f32)),
+        in_specs=[HBM] * 4,
         out_specs=(VMEM, HBM),
         scratch_shapes=[
-            pltpu.SMEM((CAP, graph_parts), jnp.int32),
-            pltpu.SMEM((1, graph_parts), jnp.int32),
+            pltpu.SMEM(dst.shape, jnp.int32),
+            pltpu.SMEM(counts.shape, jnp.int32),
+            pltpu.VMEM(fetched.shape, bf16),
             pltpu.VMEM((NB, BLK), f32),
+            pltpu.VMEM((NB + 1, rows + 8, BLK), f32),
             pltpu.VMEM((tiles * BLK, BLK), bf16),
             pltpu.SemaphoreType.DMA((steps,)),
-            pltpu.SemaphoreType.DMA((3,)),
+            pltpu.SemaphoreType.DMA((4,)),
         ],
         compiler_params=params(66_400_000),
         name="aggregate",
-    )(dst, req_counts, fetched, adj)
-    agg_all = lax.all_gather(agg, "feat", axis=0, tiled=True)
-    output, self_grad, grads = pl.pallas_call(
+    )(dst, counts, fetched, adj)
+
+
+def update(dst, counts, inverse, agg, bundle, adj, rows):
+    hidden, slab = agg.shape
+    tiles = adj.shape[0] // BLK
+    return pl.pallas_call(
         update_kernel,
         out_shape=(
             shape((rows, slab), bf16),
             shape((rows, slab), f32),
             shape((tiles, rows, BLK), bf16),
         ),
-        in_specs=[HBM] * 5 + [VMEM] * 2 + [HBM],
+        in_specs=[HBM] * 6,
         out_specs=(VMEM,) * 3,
         scratch_shapes=[
-            pltpu.SMEM((CAP, graph_parts), jnp.int32),
-            pltpu.SMEM((1, graph_parts), jnp.int32),
+            pltpu.SMEM(dst.shape, jnp.int32),
+            pltpu.SMEM(counts.shape, jnp.int32),
             pltpu.VMEM((NB, BLK), f32),
             pltpu.VMEM((hidden, slab), bf16),
-            pltpu.VMEM((hidden, width), bf16),
+            pltpu.VMEM(bundle.shape, bf16),
             pltpu.VMEM((hidden, slab), bf16),
             pltpu.VMEM((NB, rows, BLK), bf16),
             pltpu.VMEM((tiles * BLK, BLK), bf16),
@@ -389,24 +394,57 @@
         ],
         compiler_params=params(66_800_000),
         name="update",
-    )(dst, req_counts, inverse, agg_all, bundle, w_self, w_neigh, adj)
+    )(dst, counts, inverse, agg, bundle, adj)
+
+
+def sum_returned(ids, returned, self_grad):
+    return pl.pallas_call(
+        sum_kernel,
+        out_shape=shape(self_grad.shape, f32),
+        in_specs=[SMEM, VMEM, HBM],
+        out_specs=VMEM,
+        scratch_shapes=[
+            pltpu.VMEM(self_grad.shape, f32),
+            pltpu.VMEM((CAP, NB, returned.shape[1], BLK), f32),
+            pltpu.SemaphoreType.DMA,
+        ],
+        compiler_params=params(),
+        name="sum_returned",
+    )(ids, returned, self_grad)
+
+
+def per_device(feats, w_self, w_neigh, bias, cotangent, block_ids, req_counts, tile_dst, adjacency):
+    along, column = lax.axis_size("x"), lax.axis_size("z")
+    graph_parts = along * column
+    hidden = w_self.shape[1]
+    rows, slab = feats.shape
+    tiles = graph_parts * CAP
+    per_row = column * CAP
+    adj = adjacency.reshape(tiles * BLK, BLK)
+    dst = tile_dst[0].T
+    receivers = lax.axis_size("feat")
+
+    packed, ask, bundle = prepare(
+        block_ids[0].T, bias.reshape(1, rows), feats, cotangent, w_self, w_neigh, receivers
+    )
+    bundle = lax.all_to_all(bundle, "feat", 0, 0).reshape(hidden, -1)
+    asked = lax.all_gather(ask, "x", axis=0)
+    slabs = lax.all_gather(packed, "z", axis=0)
+    picked = select(asked, slabs, along)
+    picked, bundle = lax.optimization_barrier((picked, bundle))
+    fetched = lax.all_to_all(picked, "x", 0, 0)
+    agg, inverse = aggregate(dst, req_counts, fetched, adj)
+    agg_all = lax.all_gather(agg, "feat", axis=0, tiled=True)
+    output, self_grad, grads = update(
+        dst, req_counts, inverse, agg_all, bundle, adj, rows
+    )
     returned = lax.all_to_all(
         grads.reshape(graph_parts, CAP, rows, BLK), ("x", "z"), 0, 0
     ).reshape(tiles, rows, BLK)
     me = lax.axis_index("x") * column + lax.axis_index("z")
-    ids = lax.dynamic_slice(
-        fetched, (0, per_row, 0, me), (along, CAP, rows, 1)
-    )
+    ids = lax.dynamic_slice(fetched, (0, per_row, 0, me), (along, CAP, rows, 1))
     ids = ids.reshape(along, CAP, rows).astype(jnp.int32)
-    feat_grad = pl.pallas_call(
-        sum_kernel,
-        out_shape=shape((rows, slab), f32),
-        in_specs=[SMEM, VMEM, HBM],
-        out_specs=VMEM,
-        scratch_shapes=[pltpu.VMEM((rows, slab), f32), pltpu.SemaphoreType.DMA],
-        compiler_params=params(66_500_000),
-        name="sum_returned",
-    )(ids, returned, self_grad)
+    feat_grad = sum_returned(ids, returned, self_grad)
     return (output, feat_grad)
 
 

time: 134 us -> 130 us (0.970)
  starting transfers between devices: 26.9 us -> 14.2 us
  blocking collectives: 62 us -> 74 us
  Pallas kernels: 21.8 us -> 17.8 us
    ppermute x3 -> x0, starting transfers between devices: 13.2 us -> none  [per_device(): lax.ppermute(ask, 'x', [(i, (i + s) % along) for i in range(along)])]
    all_gather x0 -> x1, blocking collectives: none -> 11.7 us  [per_device(): asked = lax.all_gather(ask, 'x', axis=0)]
    pallas_call x5, Pallas kernels: 21.8 us -> 17.8 us  [the longest x1 7.04 us: update(): pl.pallas_call(update_kernel, out_shape=(shape((rows, slab), bf16), shape...]
    all_to_all x1, blocking collectives: 9.9 us -> 12 us  [per_device(): fetched = lax.all_to_all(picked, 'x', 0, 0)]
    all_gather x1, blocking collectives: 31.9 us -> 30 us  [per_device(): slabs = lax.all_gather(packed, 'z', axis=0)]
  transfers between devices with their start and end apart: 5 -> 2, of which waited for: 1 -> 1; matrix products, arithmetic and copies ran while one was open for 1% -> 1% of each run, Pallas kernels for 1% -> 1%
where the time goes in v4:
time: 130 us; the launch traced here: 129 us
  blocking collectives  74 us (57%)
  waiting for transfers between devices  20 us (15%)
  Pallas kernels  17.8 us (14%)
  starting transfers between devices  14.2 us (11%)
    all_gather x1, blocking collectives, per_device(): slabs = lax.all_gather(packed, 'z', axis=0)  30 us
    all_gather x1, blocking collectives, per_device(): agg_all = lax.all_gather(agg, 'feat', axis=0, tiled=True)  20.2 us
    all_to_all x1, waiting for transfers between devices, per_device(): lax.all_to_all(grads.reshape(graph_parts, CAP, rows, BLK), ('x', 'z'), 0, 0)  20 us
    all_to_all x1, blocking collectives, per_device(): fetched = lax.all_to_all(picked, 'x', 0, 0)  12 us
    all_gather x1, blocking collectives, per_device(): asked = lax.all_gather(ask, 'x', axis=0)  11.7 us
    all_to_all x1, starting transfers between devices, per_device(): bundle = lax.all_to_all(bundle, 'feat', 0, 0).reshape(hidden, -1)  7.35 us
    pallas_call x1, Pallas kernels, update(): pl.pallas_call(update_kernel, out_shape=(shape((rows, slab), bf16), shape...  7.04 us
    all_to_all x1, starting transfers between devices, per_device(): lax.all_to_all(grads.reshape(graph_parts, CAP, rows, BLK), ('x', 'z'), 0, 0)  6.82 us
  transfers between devices with their start and end apart: 2, of which 1 were waited for; matrix products, arithmetic and copies ran while one was open for 1% of the time, Pallas kernels for 1%

profile of v4, /device:TPU:6, one launch (start us, length us, event | category | flops | bytes accessed | tf_op | source)
XLA Modules:
  0.0 128.6 jit_solution(18428384940757045670)
XLA Ops:
  0.6 2.8 %prepare.1 = (bf16[16,1280]{1,0:T(8,128)(2,1)}, s32[2,128]{1,0:T(2,128)}, bf16[16,16,2688]{2,1,0:T(8,128)(2,1)}) custom-call(s32[2,48]{1,0:T(2,128)} %bitcast.22, f32[1,16]{1,0:T(1,128)} %bitcast.23, bf16[16,1024]{1,0:T(8,128)(2,1)} %feats_hbm.1, bf16[16,1024]{1,0:T(8,128)(2,1)} %cot_hbm.1, bf16[16,256]{1,0:T(8,128)(2,1)} %w_self_hbm.1, ...), custom_call_target="tpu_custom_call" | custom-call | tf_op jit(solution)/shard_map/prepare/pallas_call | solution.py:313
  3.4 0.0 copy-start.3
  3.4 0.0 copy-start.2
  3.4 7.3 %all-to-all-start = ((bf16[16,16,2688]{2,1,0:T(8,128)(2,1)}), bf16[16,16,2688]{2,1,0:T(8,128)(2,1)S(1)}, u32[]{:S(2)}, u32[]{:S(2)}) async-start(bf16[16,16,2688]{2,1,0:T(8,128)(2,1)} %get-tuple-element.14), calls=%async_computation | async-start | bytes 2752512 | tf_op jit(solution)/shard_map/all_to_all | solution.py:430
  10.8 0.0 copy-done.3
  10.8 11.7 %all-gather.2.ask_ref = s32[4,2,128]{2,1,0:T(2,128)S(1)} all-gather(s32[1,2,128]{2,1,0:T(2,128)S(1)} %bitcast.21), channel_id=2, replica_groups=mesh['x'=4,'z'=12,'feat'=16] {'x'}, dimensions={0}, use_global_device_ids=true | all-gather | bytes 5120 | tf_op jit(solution)/shard_map/all_gather | solution.py:431
  22.5 0.0 copy-done.2
  22.5 30.0 %all-gather.1 = bf16[192,1280]{1,0:T(8,128)(2,1)S(1)} all-gather(bf16[16,1280]{1,0:T(8,128)(2,1)S(1)} %copy-done.2), channel_id=3, replica_groups=mesh['x'=4,'z'=12,'feat'=16] {'z'}, dimensions={0}, use_global_device_ids=true | all-gather | bytes 532480 | tf_op jit(solution)/shard_map/all_gather | solution.py:432
  52.5 0.9 select_blocks.1
  53.4 0.0 all-to-all-done
  53.4 0.0 copy-start.1
  53.4 12.0 %all_to_all.15.fetched_hbm = bf16[4,26,16,128]{3,2,1,0:T(8,128)(2,1)} all-to-all(bf16[4,26,16,128]{3,2,1,0:T(8,128)(2,1)S(1)} %select_blocks.1), channel_id=1, replica_groups=mesh['x'=4,'z'=12,'feat'=16] {'x'}, dimensions={0} | all-to-all | bytes 851968 | tf_op jit(solution)/shard_map/all_to_all | solution.py:435
  65.5 0.0 copy-done.1
  65.5 5.4 %aggregate.1 = (bf16[16,1024]{1,0:T(8,128)(2,1)}, f32[8,128]{1,0:T(8,128)}) custom-call(s32[2,48]{1,0:T(2,128)} %bitcast.19, s32[1,48]{1,0:T(1,128)} %counts_hbm.3, bf16[4,26,16,128]{3,2,1,0:T(8,128)(2,1)} %all_to_all.15.fetched_hbm, bf16[12288,128]{1,0:T(8,128)(2,1)} %bitcast.15), custom_call_target="tpu_custom_call" | custom-call | tf_op jit(solution)/shard_map/aggregate/pallas_call | solution.py:351
  70.8 20.2 %all_gather.19.agg_hbm = bf16[256,1024]{1,0:T(8,128)(2,1)} all-gather(bf16[16,1024]{1,0:T(8,128)(2,1)} %get-tuple-element.17), channel_id=1, replica_groups=mesh['x'=4,'z'=12,'feat'=16] {'feat'}, dimensions={0}, use_global_device_ids=true | all-gather | bytes 557056 | tf_op jit(solution)/shard_map/all_gather | solution.py:437
  91.0 7.0 %update.1 = (bf16[16,1024]{1,0:T(8,128)(2,1)}, f32[16,1024]{1,0:T(8,128)}, bf16[96,16,128]{2,1,0:T(8,128)(2,1)}) custom-call(s32[2,48]{1,0:T(2,128)} %bitcast.20, s32[1,48]{1,0:T(1,128)} %counts_hbm.3, f32[8,128]{1,0:T(8,128)} %get-tuple-element.16.inv_hbm, bf16[256,1024]{1,0:T(8,128)(2,1)} %all_gather.19.agg_hbm, bf16[256,2688]{1,0:T(8,128)(2,1)} %bitcast.17, ...), custom_call_target="tpu_custom_call" | custom-call | tf_op jit(solution)/shard_map/update/pallas_call | solution.py:374
  98.1 6.8 %all-to-all-start.2 = ((bf16[48,2,16,128]{3,2,1,0:T(8,128)(2,1)}), bf16[48,2,16,128]{3,2,1,0:T(8,128)(2,1)S(1)}, u32[]{:S(2)}, u32[]{:S(2)}) async-start(bf16[48,2,16,128]{3,2,1,0:T(8,128)(2,1)} %bitcast.18), calls=%async_computation.2 | async-start | bytes 786432 | tf_op jit(solution)/shard_map/all_to_all | solution.py:441
  104.9 1.1 convert_reduce_fusion.ids_ref
  106.0 20.0 %all-to-all-done.2 = bf16[48,2,16,128]{3,2,1,0:T(8,128)(2,1)S(1)} async-done(((bf16[48,2,16,128]{3,2,1,0:T(8,128)(2,1)}), bf16[48,2,16,128]{3,2,1,0:T(8,128)(2,1)S(1)}, u32[]{:S(2)}, u32[]{:S(2)}) %all-to-all-start.2) | async-done | bytes 393248 | tf_op jit(solution)/shard_map/all_to_all | solution.py:441
  126.0 0.0 copy-start
  126.0 0.8 copy-done
  126.8 1.8 %sum_returned.1 = f32[16,1024]{1,0:T(8,128)} custom-call(s32[4,2,16]{2,1,0:T(2,128)S(1)} %convert_reduce_fusion.ids_ref, bf16[96,16,128]{2,1,0:T(8,128)(2,1)S(1)} %bitcast.14, f32[16,1024]{1,0:T(8,128)S(1)} %copy-done), custom_call_target="tpu_custom_call" | custom-call | tf_op jit(solution)/shard_map/sum_returned/pallas_call | solution.py:401
Async XLA Ops:
  3.4 7.4 %copy-start.3 = (s32[2,128]{1,0:T(2,128)S(1)}, s32[2,128]{1,0:T(2,128)}, u32[]{:S(2)}) copy-start(s32[2,128]{1,0:T(2,128)} %get-tuple-element.12) | copy-start | bytes 3076
  3.4 19.1 %copy-start.2 = (bf16[16,1280]{1,0:T(8,128)(2,1)S(1)}, bf16[16,1280]{1,0:T(8,128)(2,1)}, u32[]{:S(2)}) copy-start(bf16[16,1280]{1,0:T(8,128)(2,1)} %get-tuple-element.13) | copy-start | bytes 122884
  3.4 50.0 %all-to-all-start = ((bf16[16,16,2688]{2,1,0:T(8,128)(2,1)}), bf16[16,16,2688]{2,1,0:T(8,128)(2,1)S(1)}, u32[]{:S(2)}, u32[]{:S(2)}) async-start(bf16[16,16,2688]{2,1,0:T(8,128)(2,1)} %get-tuple-element.14), calls=%async_computation | async-start | bytes 2752512 | tf_op jit(solution)/shard_map/all_to_all | solution.py:430
  53.4 12.1 %copy-start.1 = (bf16[16,16,2688]{2,1,0:T(8,128)(2,1)}, bf16[16,16,2688]{2,1,0:T(8,128)(2,1)S(1)}, u32[]{:S(2)}) copy-start(bf16[16,16,2688]{2,1,0:T(8,128)(2,1)S(1)} %all-to-all-done) | copy-start | bytes 4128772
  98.1 27.9 %all-to-all-start.2 = ((bf16[48,2,16,128]{3,2,1,0:T(8,128)(2,1)}), bf16[48,2,16,128]{3,2,1,0:T(8,128)(2,1)S(1)}, u32[]{:S(2)}, u32[]{:S(2)}) async-start(bf16[48,2,16,128]{3,2,1,0:T(8,128)(2,1)} %bitcast.18), calls=%async_computation.2 | async-start | bytes 786432 | tf_op jit(solution)/shard_map/all_to_all | solution.py:441
  126.0 0.8 copy-start

commit v5 on v4

v5 whole, which is shorter than its diff:
```python
import jax
import jax.numpy as jnp
from jax import lax
from jax.experimental import pallas as pl
from jax.experimental.pallas import tpu as pltpu
from jax.sharding import Mesh, PartitionSpec as P

BLK = 128
NB = 8
CAP = 2
VMEM_LIMIT = 24 * 1024 * 1024

SMEM = pl.BlockSpec(memory_space=pltpu.SMEM)
VMEM = pl.BlockSpec(memory_space=pltpu.VMEM)
HBM = pl.BlockSpec(memory_space=pltpu.HBM)

f32 = jnp.float32
bf16 = jnp.bfloat16


def chunk_of(tiles):
    return 8 if tiles % 8 == 0 else tiles


def prepare_kernel(
    ids_hbm,
    bias_hbm,
    feats_hbm,
    cot_hbm,
    w_self_hbm,
    w_neigh_hbm,
    slabs_hbm,
    ask_ref,
    first_ref,
    second_ref,
    slab_ref,
    ids_ref,
    bias_ref,
    sems,
    out_sems,
):
    rows, slab = feats_hbm.shape
    parts = ids_hbm.shape[1]
    hidden = w_self_hbm.shape[1]
    left, right = pl.ds(0, slab), pl.ds(slab, hidden)
    copies = [
        pltpu.make_async_copy(source, target, sems.at[i])
        for i, (source, target) in enumerate(
            (
                (feats_hbm, slab_ref),
                (bias_hbm, bias_ref),
                (ids_hbm, ids_ref),
                (feats_hbm, first_ref.at[:, left]),
                (w_self_hbm, first_ref.at[:, right]),
                (cot_hbm, second_ref.at[:, left]),
                (w_neigh_hbm, second_ref.at[:, right]),
            )
        )
    ]
    for copy in copies:
        copy.start()
    copies[0].wait()
    out_copies = [
        pltpu.make_async_copy(slab_ref, slabs_hbm.at[i], out_sems.at[i])
        for i in range(slabs_hbm.shape[0])
    ]
    for copy in out_copies:
        copy.start()
    copies[1].wait()
    wide = jnp.broadcast_to(bias_ref[...], (rows, rows))
    place = lax.broadcasted_iota(jnp.int32, (rows, rows), 0)
    place = place == lax.broadcasted_iota(jnp.int32, (rows, rows), 1)
    bias = jnp.sum(jnp.where(place, wide, 0.0), axis=1, keepdims=True)
    high = bias.astype(bf16).astype(f32)
    middle = (bias - high).astype(bf16).astype(f32)
    low = bias - high - middle
    lane = lax.broadcasted_iota(jnp.int32, (rows, BLK), 1)
    terms = jnp.where(lane == 0, high, jnp.where(lane == 1, middle, jnp.where(lane == 2, low, 0.0)))
    second_ref[:, slab + hidden :] = terms.astype(bf16)
    copies[2].wait()
    ask_ref[...] = jnp.zeros_like(ask_ref)
    ask_ref[:, 0:parts] = ids_ref[...]
    for copy in copies[3:] + out_copies:
        copy.wait()


def tile_copies(adj_ref, adj, sems, step):
    return [
        pltpu.make_async_copy(
            adj_ref.at[pl.ds(k * step, step)], adj.at[pl.ds(k * step, step)], sems.at[k]
        )
        for k in range(adj_ref.shape[0] // step)
    ]


def wait_tiles(adj_ref, adj, sems, step, k):
    part = pl.ds(pl.multiple_of(k * step, step), step)
    pltpu.make_async_copy(adj_ref.at[part], adj.at[part], sems.at[k]).wait()


def aggregate_kernel(
    dst_hbm,
    counts_hbm,
    ids_hbm,
    slabs_hbm,
    adj_ref,
    agg_ref,
    inv_hbm,
    dst_ref,
    counts_ref,
    ids_ref,
    slabs_ref,
    inv,
    acc_ref,
    adj,
    sems,
    slab_sems,
    small,
):
    parts, rows, _ = slabs_ref.shape
    chunk = chunk_of(parts * CAP)
    step_rows = chunk * BLK
    step_parts = chunk // CAP
    small_copies = [
        pltpu.make_async_copy(source, target, small.at[i])
        for i, (source, target) in enumerate(
            ((dst_hbm, dst_ref), (counts_hbm, counts_ref), (ids_hbm, ids_ref))
        )
    ]
    for copy in small_copies:
        copy.start()
    for slab_copy, tile_copy in zip(
        tile_copies(slabs_hbm, slabs_ref, slab_sems, step_parts),
        tile_copies(adj_ref, adj, sems, step_rows),
    ):
        slab_copy.start()
        tile_copy.start()
    acc_ref[...] = jnp.zeros_like(acc_ref)
    ones = jnp.ones((rows, BLK), bf16)
    for copy in small_copies:
        copy.wait()

    def step(k, carry):
        wait_tiles(slabs_hbm, slabs_ref, slab_sems, step_parts, k)
        wait_tiles(adj_ref, adj, sems, step_rows, k)
        products = []
        for i in range(chunk):
            q = k * step_parts + i // CAP
            column = pl.multiple_of(ids_ref[i % CAP, q] * BLK, BLK)
            block = slabs_ref[q, :, pl.ds(column, BLK)]
            start = pl.multiple_of((k * chunk + i) * BLK, BLK)
            products.append(
                jnp.dot(
                    jnp.concatenate([block, ones], axis=0),
                    adj[pl.ds(start, BLK), :],
                    preferred_element_type=f32,
                )
            )
        for i in range(chunk):
            q = k * step_parts + i // CAP
            live = (i % CAP) < counts_ref[0, q]
            dst = jnp.where(live, dst_ref[i % CAP, q], NB)
            acc_ref[dst] += products[i][0 : rows + 8]
        return carry

    lax.fori_loop(0, parts * CAP // chunk, step, 0)
    for n in range(NB):
        inv[n : n + 1] = 1.0 / jnp.maximum(acc_ref[n, rows : rows + 1], 1.0)
    inv_copy = pltpu.make_async_copy(inv, inv_hbm, small.at[3])
    inv_copy.start()
    for n in range(NB):
        part = acc_ref[n, 0:rows] * inv[n : n + 1]
        agg_ref[:, n * BLK : (n + 1) * BLK] = part.astype(bf16)
    inv_copy.wait()


def update_kernel(
    dst_hbm,
    counts_hbm,
    inv_hbm,
    agg_hbm,
    first_hbm,
    second_hbm,
    adj_ref,
    out_ref,
    self_ref,
    grads_ref,
    dst_ref,
    counts_ref,
    inv_ref,
    agg_ref,
    first_ref,
    second_ref,
    out_all,
    scaled,
    adj,
    sems,
    small,
):
    hidden, slab = agg_ref.shape
    tiles, rows, _ = grads_ref.shape
    chunk = chunk_of(tiles)
    step_rows = chunk * BLK
    copies = [
        pltpu.make_async_copy(source, target, small.at[i])
        for i, (source, target) in enumerate(
            (
                (first_hbm, first_ref),
                (second_hbm, second_ref),
                (agg_hbm, agg_ref),
                (inv_hbm, inv_ref),
                (dst_hbm, dst_ref),
                (counts_hbm, counts_ref),
            )
        )
    ]
    for copy in copies:
        copy.start()
    for copy in copies:
        copy.wait()
    for copy in tile_copies(adj_ref, adj, sems, step_rows):
        copy.start()
    first = pl.multiple_of(lax.axis_index("feat") * rows, rows)
    w_self = first_ref[pl.ds(first, rows), slab:]
    w_neigh = second_ref[pl.ds(first, rows), slab : slab + hidden]
    tail = second_ref[:, slab + hidden :].astype(f32)
    bias = tail[:, 0:1] + tail[:, 1:2] + tail[:, 2:3]
    w_self_all = first_ref[:, slab:]
    w_neigh_all = second_ref[:, slab : slab + hidden]
    contract_rows = (((0,), (0,)), ((), ()))
    width = 2 * BLK
    for start in range(0, slab, width):
        columns = slice(start, start + width)
        preact = (
            lax.dot_general(
                w_self_all, first_ref[:, columns], contract_rows, preferred_element_type=f32
            )
            + lax.dot_general(
                w_neigh_all, agg_ref[:, columns], contract_rows, preferred_element_type=f32
            )
            + bias
        )
        s = 1.0 / (1.0 + jnp.exp(-preact))
        silu = preact * s
        out_all[:, columns] = silu.astype(bf16)
        cotangent = second_ref[:, columns].astype(f32)
        d_preact = (cotangent * (s + silu * (1.0 - s))).astype(bf16)
        self_ref[:, columns] = jnp.dot(w_self, d_preact, preferred_element_type=f32)
        neigh = jnp.dot(w_neigh, d_preact, preferred_element_type=f32)
        for half in range(width // BLK):
            n = start // BLK + half
            part = neigh[:, half * BLK : (half + 1) * BLK] * inv_ref[n : n + 1]
            scaled[n] = part.astype(bf16)
    out_ref[...] = out_all[pl.ds(first, rows), :]

    zero = jnp.zeros((rows, BLK), bf16)
    contract_columns = (((1,), (1,)), ((), ()))

    def step(k, carry):
        wait_tiles(adj_ref, adj, sems, step_rows, k)
        for i in range(chunk):
            t = k * chunk + i
            q = k * (chunk // CAP) + i // CAP
            live = (i % CAP) < counts_ref[0, q]
            chosen = jnp.where(live, scaled[dst_ref[i % CAP, q]], zero)
            start = pl.multiple_of(t * BLK, BLK)
            grads = lax.dot_general(
                chosen, adj[pl.ds(start, BLK), :], contract_columns, preferred_element_type=f32
            )
            grads_ref[t] = grads.astype(bf16)
        return carry

    lax.fori_loop(0, tiles // chunk, step, 0)


def sum_kernel(ids_ref, grads_ref, self_hbm, out_ref, self_ref, sums, sem):
    self_copy = pltpu.make_async_copy(self_hbm, self_ref, sem)
    self_copy.start()
    tiles, rows, _ = grads_ref.shape
    column = lax.axis_size("z")
    along = tiles // (column * CAP)
    me = lax.axis_index("x") * column + lax.axis_index("z")
    sums[...] = jnp.zeros_like(sums)
    for q in range(tiles // CAP):
        for c in range(CAP):
            block = grads_ref[q * CAP + c].astype(f32)
            row = ((q % column) * along + q // column) * CAP + c
            sums[c, ids_ref[row, me]] += block
    self_copy.wait()
    for n in range(NB):
        columns = slice(n * BLK, (n + 1) * BLK)
        total = self_ref[:, columns]
        for c in range(CAP):
            total += sums[c, n]
        out_ref[:, columns] = total


def params(limit=VMEM_LIMIT):
    return pltpu.CompilerParams(vmem_limit_bytes=limit)


def shape(dims, dtype):
    return jax.ShapeDtypeStruct(dims, dtype)


def prepare(block_ids, bias, feats, cotangent, w_self, w_neigh):
    rows, slab = feats.shape
    hidden = w_self.shape[1]
    parts = block_ids.shape[1]
    return pl.pallas_call(
        prepare_kernel,
        out_shape=(
            shape((parts, rows, slab), bf16),
            shape((CAP, BLK), jnp.int32),
            shape((rows, slab + hidden), bf16),
            shape((rows, slab + hidden + BLK), bf16),
        ),
        in_specs=[HBM] * 6,
        out_specs=(HBM, VMEM, VMEM, VMEM),
        scratch_shapes=[
            pltpu.VMEM((rows, slab), bf16),
            pltpu.VMEM((CAP, parts), jnp.int32),
            pltpu.VMEM((1, rows), f32),
            pltpu.SemaphoreType.DMA((7,)),
            pltpu.SemaphoreType.DMA((parts,)),
        ],
        compiler_params=params(66_800_000),
        name="prepare",
    )(block_ids, bias, feats, cotangent, w_self, w_neigh)


def aggregate(dst, counts, block_ids, slabs, adj):
    parts, rows, _ = slabs.shape
    tiles = parts * CAP
    steps = tiles // chunk_of(tiles)
    return pl.pallas_call(
        aggregate_kernel,
        out_shape=(shape((rows, NB * BLK), bf16), shape((NB, BLK), f32)),
        in_specs=[HBM] * 5,
        out_specs=(VMEM, HBM),
        scratch_shapes=[
            pltpu.SMEM(dst.shape, jnp.int32),
            pltpu.SMEM(counts.shape, jnp.int32),
            pltpu.SMEM(dst.shape, jnp.int32),
            pltpu.VMEM(slabs.shape, bf16),
            pltpu.VMEM((NB, BLK), f32),
            pltpu.VMEM((NB + 1, rows + 8, BLK), f32),
            pltpu.VMEM((tiles * BLK, BLK), bf16),
            pltpu.SemaphoreType.DMA((steps,)),
            pltpu.SemaphoreType.DMA((steps,)),
            pltpu.SemaphoreType.DMA((4,)),
        ],
        compiler_params=params(66_800_000),
        name="aggregate",
    )(dst, counts, block_ids, slabs, adj)


def update(dst, counts, inverse, agg, first, second, adj, rows):
    hidden, slab = agg.shape
    tiles = adj.shape[0] // BLK
    return pl.pallas_call(
        update_kernel,
        out_shape=(
            shape((rows, slab), bf16),
            shape((rows, slab), f32),
            shape((tiles, rows, BLK), bf16),
        ),
        in_specs=[HBM] * 7,
        out_specs=(VMEM,) * 3,
        scratch_shapes=[
            pltpu.SMEM(dst.shape, jnp.int32),
            pltpu.SMEM(counts.shape, jnp.int32),
            pltpu.VMEM((NB, BLK), f32),
            pltpu.VMEM((hidden, slab), bf16),
            pltpu.VMEM(first.shape, bf16),
            pltpu.VMEM(second.shape, bf16),
            pltpu.VMEM((hidden, slab), bf16),
            pltpu.VMEM((NB, rows, BLK), bf16),
            pltpu.VMEM((tiles * BLK, BLK), bf16),
            pltpu.SemaphoreType.DMA((tiles // chunk_of(tiles),)),
            pltpu.SemaphoreType.DMA((6,)),
        ],
        compiler_params=params(66_800_000),
        name="update",
    )(dst, counts, inverse, agg, first, second, adj)


def sum_returned(ids, returned, self_grad):
    return pl.pallas_call(
        sum_kernel,
        out_shape=shape(self_grad.shape, f32),
        in_specs=[SMEM, VMEM, HBM],
        out_specs=VMEM,
        scratch_shapes=[
            pltpu.VMEM(self_grad.shape, f32),
            pltpu.VMEM((CAP, NB, returned.shape[1], BLK), f32),
            pltpu.SemaphoreType.DMA,
        ],
        compiler_params=params(),
        name="sum_returned",
    )(ids, returned, self_grad)


def per_device(feats, w_self, w_neigh, bias, cotangent, block_ids, req_counts, tile_dst, adjacency):
    graph_parts = lax.axis_size("x") * lax.axis_size("z")
    rows, slab = feats.shape
    tiles = graph_parts * CAP
    adj = adjacency.reshape(tiles * BLK, BLK)
    dst = tile_dst[0].T
    own_ids = block_ids[0].T

    slabs, ask, first, second = prepare(
        own_ids, bias.reshape(1, rows), feats, cotangent, w_self, w_neigh
    )
    slabs = lax.all_to_all(slabs, ("x", "z"), 0, 0)
    first = lax.all_gather(first, "feat", axis=0, tiled=True)
    second = lax.all_gather(second, "feat", axis=0, tiled=True)
    slabs, first, second = lax.optimization_barrier((slabs, first, second))
    agg, inverse = aggregate(dst, req_counts, own_ids, slabs, adj)
    agg_all = lax.all_gather(agg, "feat", axis=0, tiled=True)
    output, self_grad, grads = update(
        dst, req_counts, inverse, agg_all, first, second, adj, rows
    )
    returned = lax.all_to_all(
        grads.reshape(graph_parts, CAP, rows, BLK), ("x", "z"), 0, 0
    ).reshape(tiles, rows, BLK)
    ids = lax.all_gather(ask, "x", axis=0, tiled=True)
    ids = lax.all_gather(ids, "z", axis=0, tiled=True)
    feat_grad = sum_returned(ids, returned, self_grad)
    return (output, feat_grad)


def solution(mesh):
    graph, feat = mesh.devices.shape
    along = 4 if graph % 12 == 0 else 2
    mesh = Mesh(mesh.devices.reshape(along, graph // along, feat), ("x", "z", "feat"))
    graph = ("x", "z")
    in_specs = (
        P("feat", graph),
        P("feat", None),
        P("feat", None),
        P("feat"),
        P("feat", graph),
        P(graph, None, None),
        P(graph, None),
        P(graph, None, None),
        P(graph, None, None, None, None),
    )
    out_specs = (P("feat", graph), P("feat", graph))
    return jax.shard_map(
        per_device, mesh=mesh, in_specs=in_specs, out_specs=out_specs, check_vma=False
    )
```

time: 130 us -> 155 us (1.19)
  blocking collectives: 74 us -> 91.1 us
  starting transfers between devices: 14.2 us -> 24.8 us
    all_gather x2 -> x4, blocking collectives: 41.7 us -> 70.4 us  [the longest x1 24.6 us: per_device(): ids = lax.all_gather(ids, 'z', axis=0, tiled=True)]
    all_to_all x1, waiting for transfers between devices: 20 us -> 0.01 us  [per_device(): lax.all_to_all(grads.reshape(graph_parts, CAP, rows, BLK), ('x', 'z'), 0, 0)]
    all_to_all x1, waiting for transfers between devices: 0.01 us -> 19.4 us  [per_device(): slabs = lax.all_to_all(slabs, ('x', 'z'), 0, 0)]
    all_to_all x1 -> x0, blocking collectives: 12 us -> none  [per_device(): fetched = lax.all_to_all(picked, 'x', 0, 0)]
    all_to_all x1, starting transfers between devices: 7.35 us -> 18.8 us  [per_device(): slabs = lax.all_to_all(slabs, ('x', 'z'), 0, 0)]
    pallas_call x2 -> x1, Pallas kernels: 3.62 us -> 3.04 us  [prepare(): pl.pallas_call(prepare_kernel, out_shape=(shape((parts, rows, slab), bf16...]
  transfers between devices with their start and end apart: 2 -> 2, of which waited for: 1 -> 1; matrix products, arithmetic and copies ran while one was open for 1% -> 0% of each run, Pallas kernels for 1% -> 0%
where the time goes in v5:
time: 155 us; the launch traced here: 154 us
  blocking collectives  91.1 us (59%)
  starting transfers between devices  24.8 us (16%)
  waiting for transfers between devices  19.4 us (13%)
  Pallas kernels  17.4 us (11%)
    all_gather x1, blocking collectives, per_device(): ids = lax.all_gather(ids, 'z', axis=0, tiled=True)  24.6 us
    all_gather x1, blocking collectives, per_device(): first = lax.all_gather(first, 'feat', axis=0, tiled=True)  20.8 us
    all_gather x1, blocking collectives, per_device(): agg_all = lax.all_gather(agg, 'feat', axis=0, tiled=True)  20.7 us
    all_to_all x1, waiting for transfers between devices, per_device(): slabs = lax.all_to_all(slabs, ('x', 'z'), 0, 0)  19.4 us
    all_to_all x1, starting transfers between devices, per_device(): slabs = lax.all_to_all(slabs, ('x', 'z'), 0, 0)  18.8 us
    all_gather x1, blocking collectives, per_device(): second = lax.all_gather(second, 'feat', axis=0, tiled=True)  18.3 us
    pallas_call x1, Pallas kernels, update(): pl.pallas_call(update_kernel, out_shape=(shape((rows, slab), bf16), shape...  7.05 us
    all_gather x1, blocking collectives, per_device(): ids = lax.all_gather(ask, 'x', axis=0, tiled=True)  6.8 us
  transfers between devices with their start and end apart: 2, of which 1 were waited for; matrix products, arithmetic and copies ran while one was open for 0% of the time, Pallas kernels for 0%

profile of v5, /device:TPU:6, one launch (start us, length us, event | category | flops | bytes accessed | tf_op | source)
XLA Modules:
  0.0 154.3 jit_solution(8597429745454884983)
XLA Ops:
  0.6 3.0 %prepare.1 = (bf16[48,16,1024]{2,1,0:T(8,128)(2,1)}, s32[2,128]{1,0:T(2,128)}, bf16[16,1280]{1,0:T(8,128)(2,1)}, bf16[16,1408]{1,0:T(8,128)(2,1)}) custom-call(s32[2,48]{1,0:T(2,128)} %bitcast.19, f32[1,16]{1,0:T(1,128)} %bitcast.22, bf16[16,1024]{1,0:T(8,128)(2,1)} %feats_hbm.1, bf16[16,1024]{1,0:T(8,128)(2,1)} %cot_hbm.1, bf16[16,256]{1,0:T(8,128)(2,1)} %w_self_hbm.1, ...), custom_call_target="tpu_custom_call" | custom-call | tf_op jit(solution)/shard_map/prepare/pallas_call | solution.py:310
  3.7 0.0 copy-start.2
  3.7 0.0 copy-start.1
  3.7 18.8 %all-to-all-start = ((bf16[48,16,1024]{2,1,0:T(8,128)(2,1)}), bf16[48,16,1024]{2,1,0:T(8,128)(2,1)}, u32[]{:S(2)}, u32[]{:S(2)}) async-start(bf16[48,16,1024]{2,1,0:T(8,128)(2,1)} %get-tuple-element.14), calls=%async_computation | async-start | bytes 3145728 | tf_op jit(solution)/shard_map/all_to_all | solution.py:415
  22.5 0.0 copy-done.2
  22.5 20.8 %all_gather.15.first_hbm = bf16[256,1280]{1,0:T(8,128)(2,1)} all-gather(bf16[16,1280]{1,0:T(8,128)(2,1)S(1)} %copy-done.2), channel_id=1, replica_groups=mesh['x'=4,'z'=12,'feat'=16] {'feat'}, dimensions={0}, use_global_device_ids=true | all-gather | bytes 696320 | tf_op jit(solution)/shard_map/all_gather | solution.py:416
  43.3 0.0 copy-done.1
  43.3 18.3 %all_gather.16.second_hbm = bf16[256,1408]{1,0:T(8,128)(2,1)} all-gather(bf16[16,1408]{1,0:T(8,128)(2,1)S(1)} %copy-done.1), channel_id=1, replica_groups=mesh['x'=4,'z'=12,'feat'=16] {'feat'}, dimensions={0}, use_global_device_ids=true | all-gather | bytes 765952 | tf_op jit(solution)/shard_map/all_gather | solution.py:417
  61.6 19.4 %all-to-all-done.slabs_hbm = bf16[48,16,1024]{2,1,0:T(8,128)(2,1)} async-done(((bf16[48,16,1024]{2,1,0:T(8,128)(2,1)}), bf16[48,16,1024]{2,1,0:T(8,128)(2,1)}, u32[]{:S(2)}, u32[]{:S(2)}) %all-to-all-start) | async-done | bytes 1572896 | tf_op jit(solution)/shard_map/all_to_all | solution.py:415
  81.0 4.8 %aggregate.1 = (bf16[16,1024]{1,0:T(8,128)(2,1)}, f32[8,128]{1,0:T(8,128)}) custom-call(s32[2,48]{1,0:T(2,128)} %bitcast.17, s32[1,48]{1,0:T(1,128)} %counts_hbm.3, s32[2,48]{1,0:T(2,128)} %bitcast.20, bf16[48,16,1024]{2,1,0:T(8,128)(2,1)} %all-to-all-done.slabs_hbm, bf16[12288,128]{1,0:T(8,128)(2,1)} %bitcast.13), custom_call_target="tpu_custom_call" | custom-call | tf_op jit(solution)/shard_map/aggregate/pallas_call | solution.py:336
  85.8 20.7 %all_gather.17.agg_hbm = bf16[256,1024]{1,0:T(8,128)(2,1)} all-gather(bf16[16,1024]{1,0:T(8,128)(2,1)} %get-tuple-element.19), channel_id=1, replica_groups=mesh['x'=4,'z'=12,'feat'=16] {'feat'}, dimensions={0}, use_global_device_ids=true | all-gather | bytes 557056 | tf_op jit(solution)/shard_map/all_gather | solution.py:420
  106.4 0.0 copy-start.3
  106.4 7.0 %update.1 = (bf16[16,1024]{1,0:T(8,128)(2,1)}, f32[16,1024]{1,0:T(8,128)}, bf16[96,16,128]{2,1,0:T(8,128)(2,1)}) custom-call(s32[2,48]{1,0:T(2,128)} %bitcast.18, s32[1,48]{1,0:T(1,128)} %counts_hbm.3, f32[8,128]{1,0:T(8,128)} %get-tuple-element.18.inv_hbm, bf16[256,1024]{1,0:T(8,128)(2,1)} %all_gather.17.agg_hbm, bf16[256,1280]{1,0:T(8,128)(2,1)} %all_gather.15.first_hbm, ...), custom_call_target="tpu_custom_call" | custom-call | tf_op jit(solution)/shard_map/update/pallas_call | solution.py:361
  113.5 6.0 %all-to-all-start.1 = ((bf16[48,2,16,128]{3,2,1,0:T(8,128)(2,1)}), bf16[48,2,16,128]{3,2,1,0:T(8,128)(2,1)S(1)}, u32[]{:S(2)}, u32[]{:S(2)}) async-start(bf16[48,2,16,128]{3,2,1,0:T(8,128)(2,1)} %bitcast.15), calls=%async_computation.1 | async-start | bytes 786432 | tf_op jit(solution)/shard_map/all_to_all | solution.py:424
  119.5 0.0 copy-done.3
  119.5 6.8 %all-gather = s32[4,2,128]{2,1,0:T(2,128)S(1)} all-gather(s32[1,2,128]{2,1,0:T(2,128)S(1)} %bitcast.21), channel_id=1, replica_groups=mesh['x'=4,'z'=12,'feat'=16] {'x'}, dimensions={0}, use_global_device_ids=true | all-gather | bytes 5120 | tf_op jit(solution)/shard_map/all_gather | solution.py:427
  126.3 24.6 %all_gather.19.ids_ref = s32[96,128]{1,0:T(8,128)S(1)} all-gather(s32[8,128]{1,0:T(8,128)S(1)} %bitcast.16), channel_id=1, replica_groups=mesh['x'=4,'z'=12,'feat'=16] {'z'}, dimensions={0}, use_global_device_ids=true | all-gather | bytes 53248 | tf_op jit(solution)/shard_map/all_gather | solution.py:428
  150.9 0.0 all-to-all-done.1
  150.9 0.0 copy-start
  150.9 0.8 copy-done
  151.7 2.5 %sum_returned.1 = f32[16,1024]{1,0:T(8,128)} custom-call(s32[96,128]{1,0:T(8,128)S(1)} %all_gather.19.ids_ref, bf16[96,16,128]{2,1,0:T(8,128)(2,1)S(1)} %bitcast.12, f32[16,1024]{1,0:T(8,128)S(1)} %copy-done), custom_call_target="tpu_custom_call" | custom-call | tf_op jit(solution)/shard_map/sum_returned/pallas_call | solution.py:389
Async XLA Ops:
  3.7 18.8 %copy-start.2 = (bf16[16,1280]{1,0:T(8,128)(2,1)S(1)}, bf16[16,1280]{1,0:T(8,128)(2,1)}, u32[]{:S(2)}) copy-start(bf16[16,1280]{1,0:T(8,128)(2,1)} %get-tuple-element.15) | copy-start | bytes 122884
  3.7 39.6 %copy-start.1 = (bf16[16,1408]{1,0:T(8,128)(2,1)S(1)}, bf16[16,1408]{1,0:T(8,128)(2,1)}, u32[]{:S(2)}) copy-start(bf16[16,1408]{1,0:T(8,128)(2,1)} %get-tuple-element.16) | copy-start | bytes 135172
  3.7 77.3 %all-to-all-start = ((bf16[48,16,1024]{2,1,0:T(8,128)(2,1)}), bf16[48,16,1024]{2,1,0:T(8,128)(2,1)}, u32[]{:S(2)}, u32[]{:S(2)}) async-start(bf16[48,16,1024]{2,1,0:T(8,128)(2,1)} %get-tuple-element.14), calls=%async_computation | async-start | bytes 3145728 | tf_op jit(solution)/shard_map/all_to_all | solution.py:415
  106.4 13.1 %copy-start.3 = (s32[2,128]{1,0:T(2,128)S(1)}, s32[2,128]{1,0:T(2,128)}, u32[]{:S(2)}) copy-start(s32[2,128]{1,0:T(2,128)} %get-tuple-element.23) | copy-start | bytes 3076
  113.5 37.4 %all-to-all-start.1 = ((bf16[48,2,16,128]{3,2,1,0:T(8,128)(2,1)}), bf16[48,2,16,128]{3,2,1,0:T(8,128)(2,1)S(1)}, u32[]{:S(2)}, u32[]{:S(2)}) async-start(bf16[48,2,16,128]{3,2,1,0:T(8,128)(2,1)} %bitcast.15), calls=%async_computation.1 | async-start | bytes 786432 | tf_op jit(solution)/shard_map/all_to_all | solution.py:424
  150.9 0.8 copy-start

commit v6 on v4

--- a/solution.py
+++ b/solution.py
@@ -19,7 +19,7 @@
 
 
 def chunk_of(tiles):
-    return 8 if tiles % 8 == 0 else tiles
+    return 48 if tiles % 48 == 0 else (24 if tiles % 24 == 0 else tiles)
 
 
 def prepare_kernel(
@@ -103,65 +103,41 @@
             out_ref[i, column * CAP + c] = plane.astype(bf16)
 
 
-def tile_copies(adj_ref, adj, sems, step):
-    return [
-        pltpu.make_async_copy(
-            adj_ref.at[pl.ds(k * step, step)], adj.at[pl.ds(k * step, step)], sems.at[k]
-        )
-        for k in range(adj_ref.shape[0] // step)
-    ]
-
-
-def wait_tiles(adj_ref, adj, sems, step, k):
-    part = pl.ds(pl.multiple_of(k * step, step), step)
-    pltpu.make_async_copy(adj_ref.at[part], adj.at[part], sems.at[k]).wait()
-
-
 def aggregate_kernel(
     dst_hbm,
     counts_hbm,
-    fetched_hbm,
+    fetched_ref,
     adj_ref,
     agg_ref,
     inv_hbm,
     dst_ref,
     counts_ref,
-    fetched_ref,
     inv,
     acc_ref,
-    adj,
-    sems,
     small,
 ):
     along, slots, rows, _ = fetched_ref.shape
     per_row = slots - CAP
     chunk = chunk_of(per_row)
-    step_rows = chunk * BLK
     dst_copy = pltpu.make_async_copy(dst_hbm, dst_ref, small.at[0])
     counts_copy = pltpu.make_async_copy(counts_hbm, counts_ref, small.at[1])
-    fetched_copy = pltpu.make_async_copy(fetched_hbm, fetched_ref, small.at[3])
-    fetched_copy.start()
     dst_copy.start()
     counts_copy.start()
-    for copy in tile_copies(adj_ref, adj, sems, step_rows):
-        copy.start()
     row_ids = lax.broadcasted_iota(jnp.int32, (16, BLK), 0)
     zero = jnp.zeros((rows, BLK), bf16)
     chunks = per_row // chunk
     dst_copy.wait()
     counts_copy.wait()
-    fetched_copy.wait()
 
     acc_ref[...] = jnp.zeros_like(acc_ref)
     ones = jnp.ones((rows, BLK), bf16)
 
     def step(k, carry):
-        wait_tiles(adj_ref, adj, sems, step_rows, k)
         products = []
         for i in range(chunk):
             block = fetched_ref[k // chunks, (k % chunks) * chunk + i]
             start = pl.multiple_of((k * chunk + i) * BLK, BLK)
-            products.append(jnp.dot(jnp.concatenate([block, ones], axis=0), adj[pl.ds(start, BLK), :], preferred_element_type=f32))
+            products.append(jnp.dot(jnp.concatenate([block, ones], axis=0), adj_ref[pl.ds(start, BLK), :], preferred_element_type=f32))
         for i in range(chunk):
             q = k * (chunk // CAP) + i // CAP
             live = (i % CAP) < counts_ref[0, q]
@@ -184,7 +160,7 @@
     dst_hbm,
     counts_hbm,
     inv_hbm,
-    agg_hbm,
+    agg_ref,
     bundle_hbm,
     adj_ref,
     out_ref,
@@ -193,24 +169,19 @@
     dst_ref,
     counts_ref,
     inv_ref,
-    agg_ref,
     bundle_ref,
     out_all,
     scaled,
-    adj,
-    sems,
     small,
 ):
     hidden, slab = agg_ref.shape
     tiles, rows, _ = grads_ref.shape
     chunk = chunk_of(tiles)
-    step_rows = chunk * BLK
     copies = [
         pltpu.make_async_copy(source, target, small.at[i])
         for i, (source, target) in enumerate(
             (
                 (bundle_hbm, bundle_ref),
-                (agg_hbm, agg_ref),
                 (inv_hbm, inv_ref),
                 (dst_hbm, dst_ref),
                 (counts_hbm, counts_ref),
@@ -221,8 +192,6 @@
         copy.start()
     for copy in copies:
         copy.wait()
-    for copy in tile_copies(adj_ref, adj, sems, step_rows):
-        copy.start()
     weights = 2 * slab
     first = pl.multiple_of(lax.axis_index("feat") * rows, rows)
     w_self = bundle_ref[pl.ds(first, rows), weights : weights + hidden]
@@ -232,7 +201,7 @@
     w_self_all = bundle_ref[:, weights : weights + hidden]
     w_neigh_all = bundle_ref[:, weights + hidden : weights + 2 * hidden]
     contract_rows = (((0,), (0,)), ((), ()))
-    width = 2 * BLK
+    width = 8 * BLK
     for start in range(0, slab, width):
         columns = slice(start, start + width)
         preact = (
@@ -261,7 +230,6 @@
     contract_columns = (((1,), (1,)), ((), ()))
 
     def step(k, carry):
-        wait_tiles(adj_ref, adj, sems, step_rows, k)
         for i in range(chunk):
             t = k * chunk + i
             q = k * (chunk // CAP) + i // CAP
@@ -269,7 +237,7 @@
             chosen = jnp.where(live, scaled[dst_ref[i % CAP, q]], zero)
             start = pl.multiple_of(t * BLK, BLK)
             grads = lax.dot_general(
-                chosen, adj[pl.ds(start, BLK), :], contract_columns, preferred_element_type=f32
+                chosen, adj_ref[pl.ds(start, BLK), :], contract_columns, preferred_element_type=f32
             )
             grads_ref[t] = grads.astype(bf16)
         return carry
@@ -347,23 +315,19 @@
 def aggregate(dst, counts, fetched, adj):
     along, slots, rows, _ = fetched.shape
     tiles = along * (slots - CAP)
-    steps = tiles // chunk_of(slots - CAP)
     return pl.pallas_call(
         aggregate_kernel,
         out_shape=(shape((rows, NB * BLK), bf16), shape((NB, BLK), f32)),
-        in_specs=[HBM] * 4,
+        in_specs=[HBM, HBM, VMEM, VMEM],
         out_specs=(VMEM, HBM),
         scratch_shapes=[
             pltpu.SMEM(dst.shape, jnp.int32),
             pltpu.SMEM(counts.shape, jnp.int32),
-            pltpu.VMEM(fetched.shape, bf16),
             pltpu.VMEM((NB, BLK), f32),
             pltpu.VMEM((NB + 1, rows + 8, BLK), f32),
-            pltpu.VMEM((tiles * BLK, BLK), bf16),
-            pltpu.SemaphoreType.DMA((steps,)),
-            pltpu.SemaphoreType.DMA((4,)),
+            pltpu.SemaphoreType.DMA((3,)),
         ],
-        compiler_params=params(66_400_000),
+        compiler_params=params(),
         name="aggregate",
     )(dst, counts, fetched, adj)
 
@@ -378,21 +342,18 @@
             shape((rows, slab), f32),
             shape((tiles, rows, BLK), bf16),
         ),
-        in_specs=[HBM] * 6,
+        in_specs=[HBM] * 3 + [VMEM, HBM, VMEM],
         out_specs=(VMEM,) * 3,
         scratch_shapes=[
             pltpu.SMEM(dst.shape, jnp.int32),
             pltpu.SMEM(counts.shape, jnp.int32),
             pltpu.VMEM((NB, BLK), f32),
-            pltpu.VMEM((hidden, slab), bf16),
             pltpu.VMEM(bundle.shape, bf16),
             pltpu.VMEM((hidden, slab), bf16),
             pltpu.VMEM((NB, rows, BLK), bf16),
-            pltpu.VMEM((tiles * BLK, BLK), bf16),
-            pltpu.SemaphoreType.DMA((tiles // chunk_of(tiles),)),
-            pltpu.SemaphoreType.DMA((5,)),
+            pltpu.SemaphoreType.DMA((4,)),
         ],
-        compiler_params=params(66_800_000),
+        compiler_params=params(),
         name="update",
     )(dst, counts, inverse, agg, bundle, adj)
 

time: 130 us -> 123 us (0.946)
  Pallas kernels: 17.8 us -> 12.3 us
    pallas_call x1, Pallas kernels: 5.36 us -> 1.93 us  [aggregate(): pl.pallas_call(aggregate_kernel, out_shape=(shape((rows, NB * BLK), bf16)...]
    pallas_call x1, Pallas kernels: 7.04 us -> 5.02 us  [update(): pl.pallas_call(update_kernel, out_shape=(shape((rows, slab), bf16), shape...]
    all_gather x1, blocking collectives: 20.2 us -> 18.8 us  [per_device(): agg_all = lax.all_gather(agg, 'feat', axis=0, tiled=True)]
where the time goes in v6:
time: 123 us
  blocking collectives  73.6 us (60%)
  waiting for transfers between devices  20.3 us (17%)
  starting transfers between devices  13.9 us (11%)
  Pallas kernels  12.3 us (10%)
    all_gather x1, blocking collectives, per_device(): slabs = lax.all_gather(packed, 'z', axis=0)  29.6 us
    all_to_all x1, waiting for transfers between devices, per_device(): lax.all_to_all(grads.reshape(graph_parts, CAP, rows, BLK), ('x', 'z'), 0, 0)  20.3 us
    all_gather x1, blocking collectives, per_device(): agg_all = lax.all_gather(agg, 'feat', axis=0, tiled=True)  18.8 us
    all_gather x1, blocking collectives, per_device(): asked = lax.all_gather(ask, 'x', axis=0)  12.6 us
    all_to_all x1, blocking collectives, per_device(): fetched = lax.all_to_all(picked, 'x', 0, 0)  12.5 us
    all_to_all x1, starting transfers between devices, per_device(): bundle = lax.all_to_all(bundle, 'feat', 0, 0).reshape(hidden, -1)  7.53 us
    all_to_all x1, starting transfers between devices, per_device(): lax.all_to_all(grads.reshape(graph_parts, CAP, rows, BLK), ('x', 'z'), 0, 0)  6.39 us
    pallas_call x1, Pallas kernels, update(): pl.pallas_call(update_kernel, out_shape=(shape((rows, slab), bf16), shape...  5.02 us
  transfers between devices with their start and end apart: 2, of which 1 were waited for; matrix products, arithmetic and copies ran while one was open for 1% of the time, Pallas kernels for 1%

profile of v6, /device:TPU:6, one launch (start us, length us, event | category | flops | bytes accessed | tf_op | source)
XLA Modules:
  0.0 122.7 jit_solution(12622093930328595670)
XLA Ops:
  0.6 2.8 %prepare.1 = (bf16[16,1280]{1,0:T(8,128)(2,1)}, s32[2,128]{1,0:T(2,128)}, bf16[16,16,2688]{2,1,0:T(8,128)(2,1)}) custom-call(s32[2,48]{1,0:T(2,128)} %bitcast.20, f32[1,16]{1,0:T(1,128)} %bitcast.21, bf16[16,1024]{1,0:T(8,128)(2,1)} %feats_hbm.1, bf16[16,1024]{1,0:T(8,128)(2,1)} %cot_hbm.1, bf16[16,256]{1,0:T(8,128)(2,1)} %w_self_hbm.1, ...), custom_call_target="tpu_custom_call" | custom-call | tf_op jit(solution)/shard_map/prepare/pallas_call | solution.py:281
  3.4 0.0 copy-start
  3.4 7.5 %all-to-all-start = ((bf16[16,16,2688]{2,1,0:T(8,128)(2,1)}), bf16[16,16,2688]{2,1,0:T(8,128)(2,1)}, u32[]{:S(2)}, u32[]{:S(2)}) async-start(bf16[16,16,2688]{2,1,0:T(8,128)(2,1)} %get-tuple-element.14), calls=%async_computation | async-start | bytes 2752512 | tf_op jit(solution)/shard_map/all_to_all | solution.py:391
  10.9 0.0 copy-start.3
  11.0 0.0 copy-start.4
  11.0 12.6 %all-gather.2.ask_ref = s32[4,2,128]{2,1,0:T(2,128)S(1)} all-gather(s32[1,2,128]{2,1,0:T(2,128)} %bitcast.19), channel_id=2, replica_groups=mesh['x'=4,'z'=12,'feat'=16] {'x'}, dimensions={0}, use_global_device_ids=true | all-gather | bytes 5120 | tf_op jit(solution)/shard_map/all_gather | solution.py:392
  23.6 29.6 %all-gather.1 = bf16[192,1280]{1,0:T(8,128)(2,1)S(1)} all-gather(bf16[16,1280]{1,0:T(8,128)(2,1)} %get-tuple-element.13), channel_id=3, replica_groups=mesh['x'=4,'z'=12,'feat'=16] {'z'}, dimensions={0}, use_global_device_ids=true | all-gather | bytes 532480 | tf_op jit(solution)/shard_map/all_gather | solution.py:393
  53.2 0.9 select_blocks.1
  54.1 0.0 copy-start.2
  54.1 0.8 copy-done.2
  54.8 0.0 all-to-all-done
  54.8 12.5 %all_to_all.15.fetched_ref = bf16[4,26,16,128]{3,2,1,0:T(8,128)(2,1)S(1)} all-to-all(bf16[4,26,16,128]{3,2,1,0:T(8,128)(2,1)} %copy-done.2), channel_id=1, replica_groups=mesh['x'=4,'z'=12,'feat'=16] {'x'}, dimensions={0} | all-to-all | bytes 851968 | tf_op jit(solution)/shard_map/all_to_all | solution.py:396
  67.3 0.0 copy-start.1
  67.3 0.0 copy-done
  67.3 0.0 copy-done.3
  67.3 0.0 copy-done.4
  67.3 1.9 %aggregate.1 = (bf16[16,1024]{1,0:T(8,128)(2,1)S(1)}, f32[8,128]{1,0:T(8,128)S(1)}) custom-call(s32[2,48]{1,0:T(2,128)S(1)} %bitcast.17, s32[1,48]{1,0:T(1,128)S(1)} %copy-done.4, bf16[4,26,16,128]{3,2,1,0:T(8,128)(2,1)S(1)} %all_to_all.15.fetched_ref, bf16[12288,128]{1,0:T(8,128)(2,1)S(1)} %bitcast.13), custom_call_target="tpu_custom_call" | custom-call | tf_op jit(solution)/shard_map/aggregate/pallas_call | solution.py:318
  69.3 0.0 copy-done.1
  69.3 18.8 %all_gather.19.agg_ref = bf16[256,1024]{1,0:T(8,128)(2,1)S(1)} all-gather(bf16[16,1024]{1,0:T(8,128)(2,1)S(1)} %get-tuple-element.17), channel_id=1, replica_groups=mesh['x'=4,'z'=12,'feat'=16] {'feat'}, dimensions={0}, use_global_device_ids=true | all-gather | bytes 557056 | tf_op jit(solution)/shard_map/all_gather | solution.py:398
  88.1 5.0 %update.1 = (bf16[16,1024]{1,0:T(8,128)(2,1)}, f32[16,1024]{1,0:T(8,128)S(1)}, bf16[96,16,128]{2,1,0:T(8,128)(2,1)}) custom-call(s32[2,48]{1,0:T(2,128)S(1)} %bitcast.18, s32[1,48]{1,0:T(1,128)S(1)} %copy-done.4, f32[8,128]{1,0:T(8,128)S(1)} %get-tuple-element.16.inv_hbm, bf16[256,1024]{1,0:T(8,128)(2,1)S(1)} %all_gather.19.agg_ref, ...), custom_call_target="tpu_custom_call" | custom-call | tf_op jit(solution)/shard_map/update/pallas_call | solution.py:338
  93.2 6.4 %all-to-all-start.2 = ((bf16[48,2,16,128]{3,2,1,0:T(8,128)(2,1)}), bf16[48,2,16,128]{3,2,1,0:T(8,128)(2,1)S(1)}, u32[]{:S(2)}, u32[]{:S(2)}) async-start(bf16[48,2,16,128]{3,2,1,0:T(8,128)(2,1)} %bitcast.10), calls=%async_computation.2 | async-start | bytes 786432 | tf_op jit(solution)/shard_map/all_to_all | solution.py:402
  99.6 1.1 convert_reduce_fusion.ids_ref
  100.6 20.3 %all-to-all-done.2 = bf16[48,2,16,128]{3,2,1,0:T(8,128)(2,1)S(1)} async-done(((bf16[48,2,16,128]{3,2,1,0:T(8,128)(2,1)}), bf16[48,2,16,128]{3,2,1,0:T(8,128)(2,1)S(1)}, u32[]{:S(2)}, u32[]{:S(2)}) %all-to-all-start.2) | async-done | bytes 393248 | tf_op jit(solution)/shard_map/all_to_all | solution.py:402
  120.9 1.8 %sum_returned.1 = f32[16,1024]{1,0:T(8,128)} custom-call(s32[4,2,16]{2,1,0:T(2,128)S(1)} %convert_reduce_fusion.ids_ref, bf16[96,16,128]{2,1,0:T(8,128)(2,1)S(1)} %bitcast.16, f32[16,1024]{1,0:T(8,128)S(1)} %get-tuple-element.21.self_hbm), custom_call_target="tpu_custom_call" | custom-call | tf_op jit(solution)/shard_map/sum_returned/pallas_call | solution.py:362
Async XLA Ops:
  3.4 63.9 %copy-start = (bf16[1,48,2,128,128]{4,3,2,1,0:T(8,128)(2,1)S(1)}, bf16[1,48,2,128,128]{4,3,2,1,0:T(8,128)(2,1)}, u32[]{:S(2)}) copy-start(bf16[1,48,2,128,128]{4,3,2,1,0:T(8,128)(2,1)} %param.17) | copy-start | bytes 9437188
  3.4 51.4 %all-to-all-start = ((bf16[16,16,2688]{2,1,0:T(8,128)(2,1)}), bf16[16,16,2688]{2,1,0:T(8,128)(2,1)}, u32[]{:S(2)}, u32[]{:S(2)}) async-start(bf16[16,16,2688]{2,1,0:T(8,128)(2,1)} %get-tuple-element.14), calls=%async_computation | async-start | bytes 2752512 | tf_op jit(solution)/shard_map/all_to_all | solution.py:391
  10.9 56.4 %copy-start.3 = (s32[1,48,2]{1,2,0:T(2,128)S(1)}, s32[1,48,2]{1,2,0:T(2,128)}, u32[]{:S(2)}) copy-start(s32[1,48,2]{1,2,0:T(2,128)} %param.16) | copy-start | bytes 1156
  11.0 56.4 %copy-start.4 = (s32[1,48]{1,0:T(1,128)S(1)}, s32[1,48]{1,0:T(1,128)}, u32[]{:S(2)}) copy-start(s32[1,48]{1,0:T(1,128)} %counts_hbm.3) | copy-start | bytes 580
  54.1 0.8 copy-start.2
  67.3 2.0 %copy-start.1 = (bf16[4,26,16,128]{3,2,1,0:T(8,128)(2,1)}, bf16[4,26,16,128]{3,2,1,0:T(8,128)(2,1)S(1)}, u32[]{:S(2)}) copy-start(bf16[4,26,16,128]{3,2,1,0:T(8,128)(2,1)S(1)} %all_to_all.15.fetched_ref) | copy-start | bytes 1277956
  93.2 27.8 %all-to-all-start.2 = ((bf16[48,2,16,128]{3,2,1,0:T(8,128)(2,1)}), bf16[48,2,16,128]{3,2,1,0:T(8,128)(2,1)S(1)}, u32[]{:S(2)}, u32[]{:S(2)}) async-start(bf16[48,2,16,128]{3,2,1,0:T(8,128)(2,1)} %bitcast.10), calls=%async_computation.2 | async-start | bytes 786432 | tf_op jit(solution)/shard_map/all_to_all | solution.py:402

commit v7 on v6

--- a/solution.py
+++ b/solution.py
@@ -29,11 +29,10 @@
     cot_hbm,
     w_self_hbm,
     w_neigh_hbm,
+    slabs_hbm,
+    ask_ref,
+    bundle_ref,
     slab_ref,
-    ask_ref,
-    out_hbm,
-    bundle_ref,
-    pad,
     ids_ref,
     bias_ref,
     sems,
@@ -42,27 +41,39 @@
     rows, slab = feats_hbm.shape
     parts = ids_hbm.shape[1]
     hidden = w_self_hbm.shape[1]
-    ends = (0, slab, 2 * slab, 2 * slab + hidden, 2 * slab + 2 * hidden)
-    pieces = [bundle_ref.at[:, pl.ds(i, j - i)] for i, j in zip(ends, ends[1:])]
-    sources = (ids_hbm, bias_hbm, feats_hbm, feats_hbm, cot_hbm, w_self_hbm, w_neigh_hbm)
-    targets = [ids_ref, bias_ref, slab_ref.at[:, pl.ds(0, slab)]] + pieces
+    ends = (slab, slab + hidden, slab + 2 * hidden, slab + 2 * hidden + BLK)
     copies = [
         pltpu.make_async_copy(source, target, sems.at[i])
-        for i, (source, target) in enumerate(zip(sources, targets))
+        for i, (source, target) in enumerate(
+            (
+                (ids_hbm, ids_ref),
+                (feats_hbm, slab_ref.at[:, pl.ds(0, slab)]),
+                (bias_hbm, bias_ref),
+                (feats_hbm, bundle_ref.at[:, pl.ds(0, slab)]),
+                (w_self_hbm, bundle_ref.at[:, pl.ds(ends[0], hidden)]),
+                (w_neigh_hbm, bundle_ref.at[:, pl.ds(ends[1], hidden)]),
+                (cot_hbm.at[:, pl.ds(0, BLK)], bundle_ref.at[:, pl.ds(ends[3], BLK)]),
+            )
+        )
     ]
     for copy in copies:
         copy.start()
-    pad[...] = jnp.zeros_like(pad)
+    ask_ref[...] = jnp.zeros_like(ask_ref)
     copies[0].wait()
-    pad[0:CAP, 0:parts] = ids_ref[...]
-    ask_ref[...] = pad[0:CAP, :]
-    row = lax.broadcasted_iota(jnp.int32, (rows, BLK), 0)
-    mine = row == lax.axis_index("z")
+    ask_ref[:, 0:parts] = ids_ref[...]
+    mine = lax.broadcasted_iota(jnp.int32, (rows, BLK), 0) == lax.axis_index("z")
     for c in range(CAP):
-        ids = jnp.broadcast_to(pad[c : c + 1, :], (rows, BLK))
+        ids = jnp.broadcast_to(ask_ref[c : c + 1, :], (rows, BLK))
         plane = jnp.where(mine, ids, 0).astype(f32).astype(bf16)
         slab_ref[:, slab + c * BLK : slab + (c + 1) * BLK] = plane
     copies[1].wait()
+    out_copies = [
+        pltpu.make_async_copy(slab_ref, slabs_hbm.at[i], out_sems.at[i])
+        for i in range(slabs_hbm.shape[0])
+    ]
+    for copy in out_copies:
+        copy.start()
+    copies[2].wait()
     wide = jnp.broadcast_to(bias_ref[...], (rows, rows))
     place = lax.broadcasted_iota(jnp.int32, (rows, rows), 0)
     place = place == lax.broadcasted_iota(jnp.int32, (rows, rows), 1)
@@ -72,16 +83,8 @@
     low = bias - high - middle
     lane = lax.broadcasted_iota(jnp.int32, (rows, BLK), 1)
     terms = jnp.where(lane == 0, high, jnp.where(lane == 1, middle, jnp.where(lane == 2, low, 0.0)))
-    bundle_ref[:, ends[-1] :] = terms.astype(bf16)
-    for copy in copies[2:]:
-        copy.wait()
-    copies = [
-        pltpu.make_async_copy(bundle_ref, out_hbm.at[i], out_sems.at[i])
-        for i in range(out_hbm.shape[0])
-    ]
-    for copy in copies:
-        copy.start()
-    for copy in copies:
+    bundle_ref[:, ends[2] : ends[3]] = terms.astype(bf16)
+    for copy in copies[3:] + out_copies:
         copy.wait()
 
 
@@ -106,6 +109,7 @@
 def aggregate_kernel(
     dst_hbm,
     counts_hbm,
+    cot_hbm,
     fetched_ref,
     adj_ref,
     agg_ref,
@@ -123,6 +127,11 @@
     counts_copy = pltpu.make_async_copy(counts_hbm, counts_ref, small.at[1])
     dst_copy.start()
     counts_copy.start()
+    slab = NB * BLK
+    cot_copy = pltpu.make_async_copy(
+        cot_hbm.at[:, pl.ds(BLK, slab - BLK)], agg_ref.at[:, pl.ds(slab, slab - BLK)], small.at[3]
+    )
+    cot_copy.start()
     row_ids = lax.broadcasted_iota(jnp.int32, (16, BLK), 0)
     zero = jnp.zeros((rows, BLK), bf16)
     chunks = per_row // chunk
@@ -154,6 +163,7 @@
         part = acc_ref[n, 0:rows] * inv[n : n + 1]
         agg_ref[:, n * BLK : (n + 1) * BLK] = part.astype(bf16)
     inv_copy.wait()
+    cot_copy.wait()
 
 
 def update_kernel(
@@ -174,7 +184,8 @@
     scaled,
     small,
 ):
-    hidden, slab = agg_ref.shape
+    hidden = agg_ref.shape[0]
+    slab = NB * BLK
     tiles, rows, _ = grads_ref.shape
     chunk = chunk_of(tiles)
     copies = [
@@ -192,7 +203,7 @@
         copy.start()
     for copy in copies:
         copy.wait()
-    weights = 2 * slab
+    weights = slab
     first = pl.multiple_of(lax.axis_index("feat") * rows, rows)
     w_self = bundle_ref[pl.ds(first, rows), weights : weights + hidden]
     w_neigh = bundle_ref[pl.ds(first, rows), weights + hidden : weights + 2 * hidden]
@@ -201,7 +212,7 @@
     w_self_all = bundle_ref[:, weights : weights + hidden]
     w_neigh_all = bundle_ref[:, weights + hidden : weights + 2 * hidden]
     contract_rows = (((0,), (0,)), ((), ()))
-    width = 8 * BLK
+    width = slab
     for start in range(0, slab, width):
         columns = slice(start, start + width)
         preact = (
@@ -216,7 +227,9 @@
         s = 1.0 / (1.0 + jnp.exp(-preact))
         silu = preact * s
         out_all[:, columns] = silu.astype(bf16)
-        cotangent = bundle_ref[:, slab + start : slab + start + width].astype(f32)
+        cotangent = jnp.concatenate(
+            [bundle_ref[:, weights + 2 * hidden + BLK :], agg_ref[:, slab:]], axis=1
+        ).astype(f32)
         d_preact = (cotangent * (s + silu * (1.0 - s))).astype(bf16)
         self_ref[:, columns] = jnp.dot(w_self, d_preact, preferred_element_type=f32)
         neigh = jnp.dot(w_neigh, d_preact, preferred_element_type=f32)
@@ -276,21 +289,18 @@
 def prepare(block_ids, bias, feats, cotangent, w_self, w_neigh, receivers):
     rows, slab = feats.shape
     hidden = w_self.shape[1]
-    graph_parts = block_ids.shape[1]
-    width = 2 * slab + 2 * hidden + BLK
     return pl.pallas_call(
         prepare_kernel,
         out_shape=(
-            shape((rows, slab + CAP * BLK), bf16),
+            shape((receivers, rows, slab + CAP * BLK), bf16),
             shape((CAP, BLK), jnp.int32),
-            shape((receivers, rows, width), bf16),
+            shape((rows, slab + 2 * hidden + 2 * BLK), bf16),
         ),
         in_specs=[HBM] * 6,
-        out_specs=(VMEM, VMEM, HBM),
+        out_specs=(HBM, VMEM, VMEM),
         scratch_shapes=[
-            pltpu.VMEM((rows, width), bf16),
-            pltpu.VMEM((8, BLK), jnp.int32),
-            pltpu.VMEM((CAP, graph_parts), jnp.int32),
+            pltpu.VMEM((rows, slab + CAP * BLK), bf16),
+            pltpu.VMEM(block_ids.shape, jnp.int32),
             pltpu.VMEM((1, rows), f32),
             pltpu.SemaphoreType.DMA((7,)),
             pltpu.SemaphoreType.DMA((receivers,)),
@@ -312,28 +322,28 @@
     )(asked, slabs)
 
 
-def aggregate(dst, counts, fetched, adj):
+def aggregate(dst, counts, cotangent, fetched, adj):
     along, slots, rows, _ = fetched.shape
     tiles = along * (slots - CAP)
     return pl.pallas_call(
         aggregate_kernel,
-        out_shape=(shape((rows, NB * BLK), bf16), shape((NB, BLK), f32)),
-        in_specs=[HBM, HBM, VMEM, VMEM],
+        out_shape=(shape((rows, (2 * NB - 1) * BLK), bf16), shape((NB, BLK), f32)),
+        in_specs=[HBM, HBM, HBM, VMEM, VMEM],
         out_specs=(VMEM, HBM),
         scratch_shapes=[
             pltpu.SMEM(dst.shape, jnp.int32),
             pltpu.SMEM(counts.shape, jnp.int32),
             pltpu.VMEM((NB, BLK), f32),
             pltpu.VMEM((NB + 1, rows + 8, BLK), f32),
-            pltpu.SemaphoreType.DMA((3,)),
+            pltpu.SemaphoreType.DMA((4,)),
         ],
         compiler_params=params(),
         name="aggregate",
-    )(dst, counts, fetched, adj)
+    )(dst, counts, cotangent, fetched, adj)
 
 
 def update(dst, counts, inverse, agg, bundle, adj, rows):
-    hidden, slab = agg.shape
+    hidden, slab = agg.shape[0], NB * BLK
     tiles = adj.shape[0] // BLK
     return pl.pallas_call(
         update_kernel,
@@ -377,24 +387,22 @@
 def per_device(feats, w_self, w_neigh, bias, cotangent, block_ids, req_counts, tile_dst, adjacency):
     along, column = lax.axis_size("x"), lax.axis_size("z")
     graph_parts = along * column
-    hidden = w_self.shape[1]
     rows, slab = feats.shape
     tiles = graph_parts * CAP
     per_row = column * CAP
     adj = adjacency.reshape(tiles * BLK, BLK)
     dst = tile_dst[0].T
-    receivers = lax.axis_size("feat")
-
-    packed, ask, bundle = prepare(
-        block_ids[0].T, bias.reshape(1, rows), feats, cotangent, w_self, w_neigh, receivers
+
+    slabs, ask, bundle = prepare(
+        block_ids[0].T, bias.reshape(1, rows), feats, cotangent, w_self, w_neigh, column
     )
-    bundle = lax.all_to_all(bundle, "feat", 0, 0).reshape(hidden, -1)
+    slabs = lax.all_to_all(slabs, "z", 0, 0)
     asked = lax.all_gather(ask, "x", axis=0)
-    slabs = lax.all_gather(packed, "z", axis=0)
+    bundle = lax.all_gather(bundle, "feat", axis=0, tiled=True)
+    slabs, asked, bundle = lax.optimization_barrier((slabs, asked, bundle))
     picked = select(asked, slabs, along)
-    picked, bundle = lax.optimization_barrier((picked, bundle))
     fetched = lax.all_to_all(picked, "x", 0, 0)
-    agg, inverse = aggregate(dst, req_counts, fetched, adj)
+    agg, inverse = aggregate(dst, req_counts, cotangent, fetched, adj)
     agg_all = lax.all_gather(agg, "feat", axis=0, tiled=True)
     output, self_grad, grads = update(
         dst, req_counts, inverse, agg_all, bundle, adj, rows

time: 123 us -> 122 us (level)
  starting transfers between devices: 13.9 us -> 28.2 us
  blocking collectives: 73.6 us -> 59.3 us
    all_to_all x1, starting transfers between devices: 7.53 us -> 15.4 us  [per_device(): slabs = lax.all_to_all(slabs, 'z', 0, 0)]
    all_gather x1, blocking collectives: 29.6 us -> 21.7 us  [per_device(): bundle = lax.all_gather(bundle, 'feat', axis=0, tiled=True)]
    all_to_all x1, starting transfers between devices: 6.39 us -> 12.7 us  [per_device(): lax.all_to_all(grads.reshape(graph_parts, CAP, rows, BLK), ('x', 'z'), 0, 0)]
    all_gather x1, blocking collectives: 12.6 us -> 6.97 us  [per_device(): asked = lax.all_gather(ask, 'x', axis=0)]
    all_gather x1, blocking collectives: 18.8 us -> 17.6 us  [per_device(): agg_all = lax.all_gather(agg, 'feat', axis=0, tiled=True)]
  transfers between devices with their start and end apart: 2 -> 2, of which waited for: 1 -> 1; matrix products, arithmetic and copies ran while one was open for 1% -> 1% of each run, Pallas kernels for 1% -> 0%
where the time goes in v7:
time: 122 us; the launch traced here: 121 us
  blocking collectives  59.3 us (49%)
  starting transfers between devices  28.2 us (23%)
  waiting for transfers between devices  20 us (16%)
  Pallas kernels  11.9 us (10%)
    all_gather x1, blocking collectives, per_device(): bundle = lax.all_gather(bundle, 'feat', axis=0, tiled=True)  21.7 us
    all_to_all x1, waiting for transfers between devices, per_device(): lax.all_to_all(grads.reshape(graph_parts, CAP, rows, BLK), ('x', 'z'), 0, 0)  20 us
    all_gather x1, blocking collectives, per_device(): agg_all = lax.all_gather(agg, 'feat', axis=0, tiled=True)  17.6 us
    all_to_all x1, starting transfers between devices, per_device(): slabs = lax.all_to_all(slabs, 'z', 0, 0)  15.4 us
    all_to_all x1, blocking collectives, per_device(): fetched = lax.all_to_all(picked, 'x', 0, 0)  13 us
    all_to_all x1, starting transfers between devices, per_device(): lax.all_to_all(grads.reshape(graph_parts, CAP, rows, BLK), ('x', 'z'), 0, 0)  12.7 us
    all_gather x1, blocking collectives, per_device(): asked = lax.all_gather(ask, 'x', axis=0)  6.97 us
    pallas_call x1, Pallas kernels, update(): pl.pallas_call(update_kernel, out_shape=(shape((rows, slab), bf16), shape...  4.42 us
  transfers between devices with their start and end apart: 2, of which 1 were waited for; matrix products, arithmetic and copies ran while one was open for 1% of the time, Pallas kernels for 0%

profile of v7, /device:TPU:6, one launch (start us, length us, event | category | flops | bytes accessed | tf_op | source)
XLA Modules:
  0.0 121.2 jit_solution(2654627959546863700)
XLA Ops:
  0.6 0.0 copy-start.3
  0.6 0.0 copy-start.5
  0.7 0.0 copy-start.4
  0.7 2.4 %prepare.1 = (bf16[12,16,1280]{2,1,0:T(8,128)(2,1)}, s32[2,128]{1,0:T(2,128)}, bf16[16,1792]{1,0:T(8,128)(2,1)}) custom-call(s32[2,48]{1,0:T(2,128)} %bitcast.17, f32[1,16]{1,0:T(1,128)} %bitcast.18, bf16[16,1024]{1,0:T(8,128)(2,1)} %feats_hbm.1, bf16[16,1024]{1,0:T(8,128)(2,1)} %cot_hbm.3, bf16[16,256]{1,0:T(8,128)(2,1)} %w_self_hbm.1, ...), custom_call_target="tpu_custom_call" | custom-call | tf_op jit(solution)/shard_map/prepare/pallas_call | solution.py:292
  3.1 0.0 copy-start
  3.1 15.4 %all-to-all-start = ((bf16[12,16,1280]{2,1,0:T(8,128)(2,1)}), bf16[12,16,1280]{2,1,0:T(8,128)(2,1)}, u32[]{:S(2)}, u32[]{:S(2)}) async-start(bf16[12,16,1280]{2,1,0:T(8,128)(2,1)} %get-tuple-element.13), calls=%async_computation | async-start | bytes 983040 | tf_op jit(solution)/shard_map/all_to_all | solution.py:399
  18.5 7.0 %all-gather.1.ask_ref = s32[4,2,128]{2,1,0:T(2,128)S(1)} all-gather(s32[1,2,128]{2,1,0:T(2,128)} %bitcast.16), channel_id=2, replica_groups=mesh['x'=4,'z'=12,'feat'=16] {'x'}, dimensions={0}, use_global_device_ids=true | all-gather | bytes 5120 | tf_op jit(solution)/shard_map/all_gather | solution.py:400
  25.5 21.7 %all_gather.14.bundle_hbm = bf16[256,1792]{1,0:T(8,128)(2,1)} all-gather(bf16[16,1792]{1,0:T(8,128)(2,1)} %get-tuple-element.15), channel_id=1, replica_groups=mesh['x'=4,'z'=12,'feat'=16] {'feat'}, dimensions={0}, use_global_device_ids=true | all-gather | bytes 974848 | tf_op jit(solution)/shard_map/all_gather | solution.py:401
  47.2 0.0 all-to-all-done.slabs_ref
  47.2 0.0 copy-start.1
  47.2 1.4 %select_blocks.1 = bf16[4,26,16,128]{3,2,1,0:T(8,128)(2,1)S(1)} custom-call(s32[4,2,128]{2,1,0:T(2,128)S(1)} %all-gather.1.ask_ref, bf16[12,16,1280]{2,1,0:T(8,128)(2,1)} %all-to-all-done.slabs_ref), custom_call_target="tpu_custom_call" | custom-call | tf_op jit(solution)/shard_map/select_blocks/pallas_call | solution.py:315
  48.6 13.0 %all_to_all.15.fetched_ref = bf16[4,26,16,128]{3,2,1,0:T(8,128)(2,1)S(1)} all-to-all(bf16[4,26,16,128]{3,2,1,0:T(8,128)(2,1)S(1)} %select_blocks.1), channel_id=1, replica_groups=mesh['x'=4,'z'=12,'feat'=16] {'x'}, dimensions={0} | all-to-all | bytes 851968 | tf_op jit(solution)/shard_map/all_to_all | solution.py:404
  61.6 0.0 copy-start.2
  61.6 0.0 copy-done.3
  61.6 0.0 copy-done.5
  61.6 0.0 copy-done.4
  61.6 0.0 copy-done
  61.6 1.9 %aggregate.1 = (bf16[16,1920]{1,0:T(8,128)(2,1)S(1)}, f32[8,128]{1,0:T(8,128)S(1)}) custom-call(s32[2,48]{1,0:T(2,128)S(1)} %bitcast.14, s32[1,48]{1,0:T(1,128)S(1)} %copy-done.5, bf16[16,1024]{1,0:T(8,128)(2,1)S(1)} %copy-done.3, bf16[4,26,16,128]{3,2,1,0:T(8,128)(2,1)S(1)} %all_to_all.15.fetched_ref, bf16[12288,128]{1,0:T(8,128)(2,1)S(1)} %bitcast.11), custom_call_target="tpu_custom_call" | custom-call | tf_op jit(solution)/shard_map/aggregate/pallas_call | solution.py:328
  63.6 0.0 copy-done.2
  63.6 17.6 %all_gather.15.agg_ref = bf16[256,1920]{1,0:T(8,128)(2,1)S(1)} all-gather(bf16[16,1920]{1,0:T(8,128)(2,1)S(1)} %get-tuple-element.19), channel_id=1, replica_groups=mesh['x'=4,'z'=12,'feat'=16] {'feat'}, dimensions={0}, use_global_device_ids=true | all-gather | bytes 1044480 | tf_op jit(solution)/shard_map/all_gather | solution.py:406
  81.2 0.0 copy-done.1
  81.2 4.4 %update.1 = (bf16[16,1024]{1,0:T(8,128)(2,1)}, f32[16,1024]{1,0:T(8,128)S(1)}, bf16[96,16,128]{2,1,0:T(8,128)(2,1)}) custom-call(s32[2,48]{1,0:T(2,128)S(1)} %bitcast.15, s32[1,48]{1,0:T(1,128)S(1)} %copy-done.5, f32[8,128]{1,0:T(8,128)S(1)} %get-tuple-element.18.inv_hbm, bf16[256,1920]{1,0:T(8,128)(2,1)S(1)} %all_gather.15.agg_ref, ...), custom_call_target="tpu_custom_call" | custom-call | tf_op jit(solution)/shard_map/update/pallas_call | solution.py:348
  85.6 12.7 %all-to-all-start.2 = ((bf16[48,2,16,128]{3,2,1,0:T(8,128)(2,1)}), bf16[48,2,16,128]{3,2,1,0:T(8,128)(2,1)S(1)}, u32[]{:S(2)}, u32[]{:S(2)}) async-start(bf16[48,2,16,128]{3,2,1,0:T(8,128)(2,1)} %bitcast.8), calls=%async_computation.2 | async-start | bytes 786432 | tf_op jit(solution)/shard_map/all_to_all | solution.py:410
  98.4 1.1 convert_reduce_fusion.ids_ref
  99.4 20.0 %all-to-all-done.2 = bf16[48,2,16,128]{3,2,1,0:T(8,128)(2,1)S(1)} async-done(((bf16[48,2,16,128]{3,2,1,0:T(8,128)(2,1)}), bf16[48,2,16,128]{3,2,1,0:T(8,128)(2,1)S(1)}, u32[]{:S(2)}, u32[]{:S(2)}) %all-to-all-start.2) | async-done | bytes 393248 | tf_op jit(solution)/shard_map/all_to_all | solution.py:410
  119.4 1.8 %sum_returned.1 = f32[16,1024]{1,0:T(8,128)} custom-call(s32[4,2,16]{2,1,0:T(2,128)S(1)} %convert_reduce_fusion.ids_ref, bf16[96,16,128]{2,1,0:T(8,128)(2,1)S(1)} %bitcast.13, f32[16,1024]{1,0:T(8,128)S(1)} %get-tuple-element.23.self_hbm), custom_call_target="tpu_custom_call" | custom-call | tf_op jit(solution)/shard_map/sum_returned/pallas_call | solution.py:372
Async XLA Ops:
  0.6 61.0 %copy-start.3 = (bf16[16,1024]{1,0:T(8,128)(2,1)S(1)}, bf16[16,1024]{1,0:T(8,128)(2,1)}, u32[]{:S(2)}) copy-start(bf16[16,1024]{1,0:T(8,128)(2,1)} %cot_hbm.3) | copy-start | bytes 98308
  0.6 61.0 %copy-start.5 = (s32[1,48]{1,0:T(1,128)S(1)}, s32[1,48]{1,0:T(1,128)}, u32[]{:S(2)}) copy-start(s32[1,48]{1,0:T(1,128)} %counts_hbm.3) | copy-start | bytes 580
  0.7 61.0 %copy-start.4 = (s32[1,48,2]{1,2,0:T(2,128)S(1)}, s32[1,48,2]{1,2,0:T(2,128)}, u32[]{:S(2)}) copy-start(s32[1,48,2]{1,2,0:T(2,128)} %param.16) | copy-start | bytes 1156
  3.1 58.6 %copy-start = (bf16[1,48,2,128,128]{4,3,2,1,0:T(8,128)(2,1)S(1)}, bf16[1,48,2,128,128]{4,3,2,1,0:T(8,128)(2,1)}, u32[]{:S(2)}) copy-start(bf16[1,48,2,128,128]{4,3,2,1,0:T(8,128)(2,1)} %param.17) | copy-start | bytes 9437188
  3.1 44.2 %all-to-all-start = ((bf16[12,16,1280]{2,1,0:T(8,128)(2,1)}), bf16[12,16,1280]{2,1,0:T(8,128)(2,1)}, u32[]{:S(2)}, u32[]{:S(2)}) async-start(bf16[12,16,1280]{2,1,0:T(8,128)(2,1)} %get-tuple-element.13), calls=%async_computation | async-start | bytes 983040 | tf_op jit(solution)/shard_map/all_to_all | solution.py:399
  47.2 34.0 %copy-start.1 = (bf16[256,1792]{1,0:T(8,128)(2,1)S(1)}, bf16[256,1792]{1,0:T(8,128)(2,1)}, u32[]{:S(2)}) copy-start(bf16[256,1792]{1,0:T(8,128)(2,1)} %all_gather.14.bundle_hbm) | copy-start | bytes 2752516
  61.6 2.0 %copy-start.2 = (bf16[4,26,16,128]{3,2,1,0:T(8,128)(2,1)}, bf16[4,26,16,128]{3,2,1,0:T(8,128)(2,1)S(1)}, u32[]{:S(2)}) copy-start(bf16[4,26,16,128]{3,2,1,0:T(8,128)(2,1)S(1)} %all_to_all.15.fetched_ref) | copy-start | bytes 1277956
  85.6 33.8 %all-to-all-start.2 = ((bf16[48,2,16,128]{3,2,1,0:T(8,128)(2,1)}), bf16[48,2,16,128]{3,2,1,0:T(8,128)(2,1)S(1)}, u32[]{:S(2)}, u32[]{:S(2)}) async-start(bf16[48,2,16,128]{3,2,1,0:T(8,128)(2,1)} %bitcast.8), calls=%async_computation.2 | async-start | bytes 786432 | tf_op jit(solution)/shard_map/all_to_all | solution.py:410

commit v8 on v7

--- a/solution.py
+++ b/solution.py
@@ -398,10 +398,12 @@
     )
     slabs = lax.all_to_all(slabs, "z", 0, 0)
     asked = lax.all_gather(ask, "x", axis=0)
+    slabs, asked = lax.optimization_barrier((slabs, asked))
+    picked = select(asked, slabs, along)
+    picked, bundle = lax.optimization_barrier((picked, bundle))
+    fetched = lax.all_to_all(picked, "x", 0, 0)
     bundle = lax.all_gather(bundle, "feat", axis=0, tiled=True)
-    slabs, asked, bundle = lax.optimization_barrier((slabs, asked, bundle))
-    picked = select(asked, slabs, along)
-    fetched = lax.all_to_all(picked, "x", 0, 0)
+    fetched, bundle = lax.optimization_barrier((fetched, bundle))
     agg, inverse = aggregate(dst, req_counts, cotangent, fetched, adj)
     agg_all = lax.all_gather(agg, "feat", axis=0, tiled=True)
     output, self_grad, grads = update(

time: 122 us -> 125 us (1.025)
  waiting for transfers between devices: 20 us -> 35.8 us
  blocking collectives: 59.3 us -> 46.3 us
    all_to_all x1, waiting for transfers between devices: 0.01 us -> 15.7 us  [per_device(): slabs = lax.all_to_all(slabs, 'z', 0, 0)]
    all_to_all x1 -> x0, blocking collectives: 13 us -> none  [per_device(): fetched = lax.all_to_all(picked, 'x', 0, 0)]
    all_to_all x1, starting transfers between devices: 12.7 us -> 7.13 us  [per_device(): lax.all_to_all(grads.reshape(graph_parts, CAP, rows, BLK), ('x', 'z'), 0, 0)]
    all_to_all x0 -> x1, starting transfers between devices: none -> 4.77 us  [per_device(): fetched = lax.all_to_all(picked, 'x', 0, 0)]
  transfers between devices with their start and end apart: 2 -> 3, of which waited for: 1 -> 2; matrix products, arithmetic and copies ran while one was open for 1% -> 1% of each run, Pallas kernels for 0% -> 0%
where the time goes in v8:
time: 125 us
  blocking collectives  46.3 us (37%)
  waiting for transfers between devices  35.8 us (29%)
  starting transfers between devices  27.3 us (22%)
  Pallas kernels  12.9 us (10%)
    all_gather x1, blocking collectives, per_device(): bundle = lax.all_gather(bundle, 'feat', axis=0, tiled=True)  21.7 us
    all_to_all x1, waiting for transfers between devices, per_device(): lax.all_to_all(grads.reshape(graph_parts, CAP, rows, BLK), ('x', 'z'), 0, 0)  20 us
    all_gather x1, blocking collectives, per_device(): agg_all = lax.all_gather(agg, 'feat', axis=0, tiled=True)  17.6 us
    all_to_all x1, waiting for transfers between devices, per_device(): slabs = lax.all_to_all(slabs, 'z', 0, 0)  15.7 us
    all_to_all x1, starting transfers between devices, per_device(): slabs = lax.all_to_all(slabs, 'z', 0, 0)  15.4 us
    all_to_all x1, starting transfers between devices, per_device(): lax.all_to_all(grads.reshape(graph_parts, CAP, rows, BLK), ('x', 'z'), 0, 0)  7.13 us
    all_gather x1, blocking collectives, per_device(): asked = lax.all_gather(ask, 'x', axis=0)  6.97 us
    all_to_all x1, starting transfers between devices, per_device(): fetched = lax.all_to_all(picked, 'x', 0, 0)  4.77 us
  transfers between devices with their start and end apart: 3, of which 2 were waited for; matrix products, arithmetic and copies ran while one was open for 1% of the time, Pallas kernels for 0%

profile of v8, /device:TPU:6, one launch (start us, length us, event | category | flops | bytes accessed | tf_op | source)
XLA Modules:
  0.0 124.9 jit_solution(11466825839110466829)
XLA Ops:
  0.6 0.0 copy-start.3
  0.6 0.0 copy-start.5
  0.7 0.0 copy-start.4
  0.7 2.4 %prepare.1 = (bf16[12,16,1280]{2,1,0:T(8,128)(2,1)}, s32[2,128]{1,0:T(2,128)}, bf16[16,1792]{1,0:T(8,128)(2,1)}) custom-call(s32[2,48]{1,0:T(2,128)} %bitcast.17, f32[1,16]{1,0:T(1,128)} %bitcast.18, bf16[16,1024]{1,0:T(8,128)(2,1)} %feats_hbm.1, bf16[16,1024]{1,0:T(8,128)(2,1)} %cot_hbm.3, bf16[16,256]{1,0:T(8,128)(2,1)} %w_self_hbm.1, ...), custom_call_target="tpu_custom_call" | custom-call | tf_op jit(solution)/shard_map/prepare/pallas_call | solution.py:292
  3.0 0.0 copy-start
  3.0 15.4 %all-to-all-start = ((bf16[12,16,1280]{2,1,0:T(8,128)(2,1)}), bf16[12,16,1280]{2,1,0:T(8,128)(2,1)}, u32[]{:S(2)}, u32[]{:S(2)}) async-start(bf16[12,16,1280]{2,1,0:T(8,128)(2,1)} %get-tuple-element.16), calls=%async_computation | async-start | bytes 983040 | tf_op jit(solution)/shard_map/all_to_all | solution.py:399
  18.5 7.0 %all-gather.1.ask_ref = s32[4,2,128]{2,1,0:T(2,128)S(1)} all-gather(s32[1,2,128]{2,1,0:T(2,128)} %bitcast.16), channel_id=2, replica_groups=mesh['x'=4,'z'=12,'feat'=16] {'x'}, dimensions={0}, use_global_device_ids=true | all-gather | bytes 5120 | tf_op jit(solution)/shard_map/all_gather | solution.py:400
  25.5 15.7 %all-to-all-done.slabs_ref = bf16[12,16,1280]{2,1,0:T(8,128)(2,1)} async-done(((bf16[12,16,1280]{2,1,0:T(8,128)(2,1)}), bf16[12,16,1280]{2,1,0:T(8,128)(2,1)}, u32[]{:S(2)}, u32[]{:S(2)}) %all-to-all-start) | async-done | bytes 491552 | tf_op jit(solution)/shard_map/all_to_all | solution.py:399
  41.2 1.3 %select_blocks.1 = bf16[4,26,16,128]{3,2,1,0:T(8,128)(2,1)S(1)} custom-call(s32[4,2,128]{2,1,0:T(2,128)S(1)} %all-gather.1.ask_ref, bf16[12,16,1280]{2,1,0:T(8,128)(2,1)} %all-to-all-done.slabs_ref), custom_call_target="tpu_custom_call" | custom-call | tf_op jit(solution)/shard_map/select_blocks/pallas_call | solution.py:315
  42.5 0.0 copy-start.2
  42.5 0.7 copy-done.2
  43.2 4.8 %all-to-all-start.1 = ((bf16[4,26,16,128]{3,2,1,0:T(8,128)(2,1)}), bf16[4,26,16,128]{3,2,1,0:T(8,128)(2,1)}, u32[]{:S(2)}, u32[]{:S(2)}) async-start(bf16[4,26,16,128]{3,2,1,0:T(8,128)(2,1)} %copy-done.2), calls=%async_computation.1 | async-start | bytes 851968 | tf_op jit(solution)/shard_map/all_to_all | solution.py:404
  48.0 21.7 %all_gather.14.bundle_hbm = bf16[256,1792]{1,0:T(8,128)(2,1)} all-gather(bf16[16,1792]{1,0:T(8,128)(2,1)} %get-tuple-element.22), channel_id=1, replica_groups=mesh['x'=4,'z'=12,'feat'=16] {'feat'}, dimensions={0}, use_global_device_ids=true | all-gather | bytes 974848 | tf_op jit(solution)/shard_map/all_gather | solution.py:405
  69.7 0.0 all-to-all-done.1.fetched_ref
  69.7 0.0 copy-start.1
  69.8 0.0 copy-done.3
  69.8 0.0 copy-done.5
  69.8 0.0 copy-done.4
  69.8 0.0 copy-done
  69.8 3.0 %aggregate.1 = (bf16[16,1920]{1,0:T(8,128)(2,1)S(1)}, f32[8,128]{1,0:T(8,128)S(1)}) custom-call(s32[2,48]{1,0:T(2,128)S(1)} %bitcast.14, s32[1,48]{1,0:T(1,128)S(1)} %copy-done.5, bf16[16,1024]{1,0:T(8,128)(2,1)S(1)} %copy-done.3, bf16[4,26,16,128]{3,2,1,0:T(8,128)(2,1)} %all-to-all-done.1.fetched_ref, bf16[12288,128]{1,0:T(8,128)(2,1)S(1)} %bitcast.11), custom_call_target="tpu_custom_call" | custom-call | tf_op jit(solution)/shard_map/aggregate/pallas_call | solution.py:328
  72.8 17.6 %all_gather.15.agg_ref = bf16[256,1920]{1,0:T(8,128)(2,1)S(1)} all-gather(bf16[16,1920]{1,0:T(8,128)(2,1)S(1)} %get-tuple-element.25), channel_id=1, replica_groups=mesh['x'=4,'z'=12,'feat'=16] {'feat'}, dimensions={0}, use_global_device_ids=true | all-gather | bytes 1044480 | tf_op jit(solution)/shard_map/all_gather | solution.py:408
  90.5 0.0 copy-done.1
  90.5 4.4 %update.1 = (bf16[16,1024]{1,0:T(8,128)(2,1)}, f32[16,1024]{1,0:T(8,128)S(1)}, bf16[96,16,128]{2,1,0:T(8,128)(2,1)}) custom-call(s32[2,48]{1,0:T(2,128)S(1)} %bitcast.15, s32[1,48]{1,0:T(1,128)S(1)} %copy-done.5, f32[8,128]{1,0:T(8,128)S(1)} %get-tuple-element.24.inv_hbm, bf16[256,1920]{1,0:T(8,128)(2,1)S(1)} %all_gather.15.agg_ref, ...), custom_call_target="tpu_custom_call" | custom-call | tf_op jit(solution)/shard_map/update/pallas_call | solution.py:348
  94.9 7.1 %all-to-all-start.2 = ((bf16[48,2,16,128]{3,2,1,0:T(8,128)(2,1)}), bf16[48,2,16,128]{3,2,1,0:T(8,128)(2,1)S(1)}, u32[]{:S(2)}, u32[]{:S(2)}) async-start(bf16[48,2,16,128]{3,2,1,0:T(8,128)(2,1)} %bitcast.8), calls=%async_computation.2 | async-start | bytes 786432 | tf_op jit(solution)/shard_map/all_to_all | solution.py:412
  102.0 1.1 convert_reduce_fusion.ids_ref
  103.1 20.0 %all-to-all-done.2 = bf16[48,2,16,128]{3,2,1,0:T(8,128)(2,1)S(1)} async-done(((bf16[48,2,16,128]{3,2,1,0:T(8,128)(2,1)}), bf16[48,2,16,128]{3,2,1,0:T(8,128)(2,1)S(1)}, u32[]{:S(2)}, u32[]{:S(2)}) %all-to-all-start.2) | async-done | bytes 393248 | tf_op jit(solution)/shard_map/all_to_all | solution.py:412
  123.1 1.8 %sum_returned.1 = f32[16,1024]{1,0:T(8,128)} custom-call(s32[4,2,16]{2,1,0:T(2,128)S(1)} %convert_reduce_fusion.ids_ref, bf16[96,16,128]{2,1,0:T(8,128)(2,1)S(1)} %bitcast.13, f32[16,1024]{1,0:T(8,128)S(1)} %get-tuple-element.29.self_hbm), custom_call_target="tpu_custom_call" | custom-call | tf_op jit(solution)/shard_map/sum_returned/pallas_call | solution.py:372
Async XLA Ops:
  0.6 69.1 %copy-start.3 = (bf16[16,1024]{1,0:T(8,128)(2,1)S(1)}, bf16[16,1024]{1,0:T(8,128)(2,1)}, u32[]{:S(2)}) copy-start(bf16[16,1024]{1,0:T(8,128)(2,1)} %cot_hbm.3) | copy-start | bytes 98308
  0.6 69.1 %copy-start.5 = (s32[1,48]{1,0:T(1,128)S(1)}, s32[1,48]{1,0:T(1,128)}, u32[]{:S(2)}) copy-start(s32[1,48]{1,0:T(1,128)} %counts_hbm.3) | copy-start | bytes 580
  0.7 69.1 %copy-start.4 = (s32[1,48,2]{1,2,0:T(2,128)S(1)}, s32[1,48,2]{1,2,0:T(2,128)}, u32[]{:S(2)}) copy-start(s32[1,48,2]{1,2,0:T(2,128)} %param.16) | copy-start | bytes 1156
  3.0 66.7 %copy-start = (bf16[1,48,2,128,128]{4,3,2,1,0:T(8,128)(2,1)S(1)}, bf16[1,48,2,128,128]{4,3,2,1,0:T(8,128)(2,1)}, u32[]{:S(2)}) copy-start(bf16[1,48,2,128,128]{4,3,2,1,0:T(8,128)(2,1)} %param.17) | copy-start | bytes 9437188
  3.0 38.2 %all-to-all-start = ((bf16[12,16,1280]{2,1,0:T(8,128)(2,1)}), bf16[12,16,1280]{2,1,0:T(8,128)(2,1)}, u32[]{:S(2)}, u32[]{:S(2)}) async-start(bf16[12,16,1280]{2,1,0:T(8,128)(2,1)} %get-tuple-element.16), calls=%async_computation | async-start | bytes 983040 | tf_op jit(solution)/shard_map/all_to_all | solution.py:399
  42.5 0.7 copy-start.2
  43.2 26.5 %all-to-all-start.1 = ((bf16[4,26,16,128]{3,2,1,0:T(8,128)(2,1)}), bf16[4,26,16,128]{3,2,1,0:T(8,128)(2,1)}, u32[]{:S(2)}, u32[]{:S(2)}) async-start(bf16[4,26,16,128]{3,2,1,0:T(8,128)(2,1)} %copy-done.2), calls=%async_computation.1 | async-start | bytes 851968 | tf_op jit(solution)/shard_map/all_to_all | solution.py:404
  69.7 20.7 %copy-start.1 = (bf16[256,1792]{1,0:T(8,128)(2,1)S(1)}, bf16[256,1792]{1,0:T(8,128)(2,1)}, u32[]{:S(2)}) copy-start(bf16[256,1792]{1,0:T(8,128)(2,1)} %all_gather.14.bundle_hbm) | copy-start | bytes 2752516
  94.9 28.2 %all-to-all-start.2 = ((bf16[48,2,16,128]{3,2,1,0:T(8,128)(2,1)}), bf16[48,2,16,128]{3,2,1,0:T(8,128)(2,1)S(1)}, u32[]{:S(2)}, u32[]{:S(2)}) async-start(bf16[48,2,16,128]{3,2,1,0:T(8,128)(2,1)} %bitcast.8), calls=%async_computation.2 | async-start | bytes 786432 | tf_op jit(solution)/shard_map/all_to_all | solution.py:412

commit v9 on v7

--- a/solution.py
+++ b/solution.py
@@ -396,10 +396,11 @@
     slabs, ask, bundle = prepare(
         block_ids[0].T, bias.reshape(1, rows), feats, cotangent, w_self, w_neigh, column
     )
+    asked = lax.all_gather(ask, "x", axis=0)
+    slabs, bundle, asked = lax.optimization_barrier((slabs, bundle, asked))
     slabs = lax.all_to_all(slabs, "z", 0, 0)
-    asked = lax.all_gather(ask, "x", axis=0)
     bundle = lax.all_gather(bundle, "feat", axis=0, tiled=True)
-    slabs, asked, bundle = lax.optimization_barrier((slabs, asked, bundle))
+    slabs, bundle = lax.optimization_barrier((slabs, bundle))
     picked = select(asked, slabs, along)
     fetched = lax.all_to_all(picked, "x", 0, 0)
     agg, inverse = aggregate(dst, req_counts, cotangent, fetched, adj)

time: 122 us -> 122 us (level)
  starting transfers between devices: 28.2 us -> 19.2 us
  blocking collectives: 59.3 us -> 68.1 us
    all_to_all x1, starting transfers between devices: 15.4 us -> 6.65 us  [per_device(): slabs = lax.all_to_all(slabs, 'z', 0, 0)]
    all_gather x1, blocking collectives: 6.97 us -> 15.6 us  [per_device(): asked = lax.all_gather(ask, 'x', axis=0)]
where the time goes in v9:
time: 122 us; the launch traced here: 121 us
  blocking collectives  68.1 us (56%)
  waiting for transfers between devices  20 us (16%)
  starting transfers between devices  19.2 us (16%)
  Pallas kernels  11.9 us (10%)
    all_gather x1, blocking collectives, per_device(): bundle = lax.all_gather(bundle, 'feat', axis=0, tiled=True)  21.7 us
    all_to_all x1, waiting for transfers between devices, per_device(): lax.all_to_all(grads.reshape(graph_parts, CAP, rows, BLK), ('x', 'z'), 0, 0)  20 us
    all_gather x1, blocking collectives, per_device(): agg_all = lax.all_gather(agg, 'feat', axis=0, tiled=True)  17.8 us
    all_gather x1, blocking collectives, per_device(): asked = lax.all_gather(ask, 'x', axis=0)  15.6 us
    all_to_all x1, blocking collectives, per_device(): fetched = lax.all_to_all(picked, 'x', 0, 0)  13 us
    all_to_all x1, starting transfers between devices, per_device(): lax.all_to_all(grads.reshape(graph_parts, CAP, rows, BLK), ('x', 'z'), 0, 0)  12.6 us
    all_to_all x1, starting transfers between devices, per_device(): slabs = lax.all_to_all(slabs, 'z', 0, 0)  6.65 us
    pallas_call x1, Pallas kernels, update(): pl.pallas_call(update_kernel, out_shape=(shape((rows, slab), bf16), shape...  4.42 us
  transfers between devices with their start and end apart: 2, of which 1 were waited for; matrix products, arithmetic and copies ran while one was open for 1% of the time, Pallas kernels for 0%

profile of v9, /device:TPU:6, one launch (start us, length us, event | category | flops | bytes accessed | tf_op | source)
XLA Modules:
  0.0 121.1 jit_solution(4169601237069159218)
XLA Ops:
  0.6 0.0 copy-start.3
  0.6 0.0 copy-start.5
  0.7 0.0 copy-start.4
  0.7 2.4 %prepare.1 = (bf16[12,16,1280]{2,1,0:T(8,128)(2,1)}, s32[2,128]{1,0:T(2,128)}, bf16[16,1792]{1,0:T(8,128)(2,1)}) custom-call(s32[2,48]{1,0:T(2,128)} %bitcast.17, f32[1,16]{1,0:T(1,128)} %bitcast.18, bf16[16,1024]{1,0:T(8,128)(2,1)} %feats_hbm.1, bf16[16,1024]{1,0:T(8,128)(2,1)} %cot_hbm.3, bf16[16,256]{1,0:T(8,128)(2,1)} %w_self_hbm.1, ...), custom_call_target="tpu_custom_call" | custom-call | tf_op jit(solution)/shard_map/prepare/pallas_call | solution.py:292
  3.1 0.0 copy-start
  3.1 15.6 %all-gather.1.ask_ref = s32[4,2,128]{2,1,0:T(2,128)S(1)} all-gather(s32[1,2,128]{2,1,0:T(2,128)} %bitcast.16), channel_id=2, replica_groups=mesh['x'=4,'z'=12,'feat'=16] {'x'}, dimensions={0}, use_global_device_ids=true | all-gather | bytes 5120 | tf_op jit(solution)/shard_map/all_gather | solution.py:399
  18.7 6.6 %all-to-all-start = ((bf16[12,16,1280]{2,1,0:T(8,128)(2,1)}), bf16[12,16,1280]{2,1,0:T(8,128)(2,1)}, u32[]{:S(2)}, u32[]{:S(2)}) async-start(bf16[12,16,1280]{2,1,0:T(8,128)(2,1)} %get-tuple-element.19), calls=%async_computation | async-start | bytes 983040 | tf_op jit(solution)/shard_map/all_to_all | solution.py:401
  25.4 21.7 %all_gather.14.bundle_hbm = bf16[256,1792]{1,0:T(8,128)(2,1)} all-gather(bf16[16,1792]{1,0:T(8,128)(2,1)} %get-tuple-element.20), channel_id=1, replica_groups=mesh['x'=4,'z'=12,'feat'=16] {'feat'}, dimensions={0}, use_global_device_ids=true | all-gather | bytes 974848 | tf_op jit(solution)/shard_map/all_gather | solution.py:402
  47.1 0.0 all-to-all-done.slabs_ref
  47.1 0.0 copy-start.1
  47.1 1.4 %select_blocks.1 = bf16[4,26,16,128]{3,2,1,0:T(8,128)(2,1)S(1)} custom-call(s32[4,2,128]{2,1,0:T(2,128)S(1)} %all-gather.1.ask_ref, bf16[12,16,1280]{2,1,0:T(8,128)(2,1)} %all-to-all-done.slabs_ref), custom_call_target="tpu_custom_call" | custom-call | tf_op jit(solution)/shard_map/select_blocks/pallas_call | solution.py:315
  48.5 13.0 %all_to_all.15.fetched_ref = bf16[4,26,16,128]{3,2,1,0:T(8,128)(2,1)S(1)} all-to-all(bf16[4,26,16,128]{3,2,1,0:T(8,128)(2,1)S(1)} %select_blocks.1), channel_id=1, replica_groups=mesh['x'=4,'z'=12,'feat'=16] {'x'}, dimensions={0} | all-to-all | bytes 851968 | tf_op jit(solution)/shard_map/all_to_all | solution.py:405
  61.5 0.0 copy-start.2
  61.5 0.0 copy-done.3
  61.5 0.0 copy-done.5
  61.5 0.0 copy-done.4
  61.5 0.0 copy-done
  61.5 1.9 %aggregate.1 = (bf16[16,1920]{1,0:T(8,128)(2,1)S(1)}, f32[8,128]{1,0:T(8,128)S(1)}) custom-call(s32[2,48]{1,0:T(2,128)S(1)} %bitcast.14, s32[1,48]{1,0:T(1,128)S(1)} %copy-done.5, bf16[16,1024]{1,0:T(8,128)(2,1)S(1)} %copy-done.3, bf16[4,26,16,128]{3,2,1,0:T(8,128)(2,1)S(1)} %all_to_all.15.fetched_ref, bf16[12288,128]{1,0:T(8,128)(2,1)S(1)} %bitcast.11), custom_call_target="tpu_custom_call" | custom-call | tf_op jit(solution)/shard_map/aggregate/pallas_call | solution.py:328
  63.5 0.0 copy-done.2
  63.5 17.8 %all_gather.15.agg_ref = bf16[256,1920]{1,0:T(8,128)(2,1)S(1)} all-gather(bf16[16,1920]{1,0:T(8,128)(2,1)S(1)} %get-tuple-element.23), channel_id=1, replica_groups=mesh['x'=4,'z'=12,'feat'=16] {'feat'}, dimensions={0}, use_global_device_ids=true | all-gather | bytes 1044480 | tf_op jit(solution)/shard_map/all_gather | solution.py:407
  81.2 0.0 copy-done.1
  81.2 4.4 %update.1 = (bf16[16,1024]{1,0:T(8,128)(2,1)}, f32[16,1024]{1,0:T(8,128)S(1)}, bf16[96,16,128]{2,1,0:T(8,128)(2,1)}) custom-call(s32[2,48]{1,0:T(2,128)S(1)} %bitcast.15, s32[1,48]{1,0:T(1,128)S(1)} %copy-done.5, f32[8,128]{1,0:T(8,128)S(1)} %get-tuple-element.22.inv_hbm, bf16[256,1920]{1,0:T(8,128)(2,1)S(1)} %all_gather.15.agg_ref, ...), custom_call_target="tpu_custom_call" | custom-call | tf_op jit(solution)/shard_map/update/pallas_call | solution.py:348
  85.7 12.6 %all-to-all-start.2 = ((bf16[48,2,16,128]{3,2,1,0:T(8,128)(2,1)}), bf16[48,2,16,128]{3,2,1,0:T(8,128)(2,1)S(1)}, u32[]{:S(2)}, u32[]{:S(2)}) async-start(bf16[48,2,16,128]{3,2,1,0:T(8,128)(2,1)} %bitcast.8), calls=%async_computation.2 | async-start | bytes 786432 | tf_op jit(solution)/shard_map/all_to_all | solution.py:411
  98.2 1.1 convert_reduce_fusion.ids_ref
  99.3 20.0 %all-to-all-done.2 = bf16[48,2,16,128]{3,2,1,0:T(8,128)(2,1)S(1)} async-done(((bf16[48,2,16,128]{3,2,1,0:T(8,128)(2,1)}), bf16[48,2,16,128]{3,2,1,0:T(8,128)(2,1)S(1)}, u32[]{:S(2)}, u32[]{:S(2)}) %all-to-all-start.2) | async-done | bytes 393248 | tf_op jit(solution)/shard_map/all_to_all | solution.py:411
  119.3 1.8 %sum_returned.1 = f32[16,1024]{1,0:T(8,128)} custom-call(s32[4,2,16]{2,1,0:T(2,128)S(1)} %convert_reduce_fusion.ids_ref, bf16[96,16,128]{2,1,0:T(8,128)(2,1)S(1)} %bitcast.13, f32[16,1024]{1,0:T(8,128)S(1)} %get-tuple-element.27.self_hbm), custom_call_target="tpu_custom_call" | custom-call | tf_op jit(solution)/shard_map/sum_returned/pallas_call | solution.py:372
Async XLA Ops:
  0.6 60.9 %copy-start.3 = (bf16[16,1024]{1,0:T(8,128)(2,1)S(1)}, bf16[16,1024]{1,0:T(8,128)(2,1)}, u32[]{:S(2)}) copy-start(bf16[16,1024]{1,0:T(8,128)(2,1)} %cot_hbm.3) | copy-start | bytes 98308
  0.6 60.9 %copy-start.5 = (s32[1,48]{1,0:T(1,128)S(1)}, s32[1,48]{1,0:T(1,128)}, u32[]{:S(2)}) copy-start(s32[1,48]{1,0:T(1,128)} %counts_hbm.3) | copy-start | bytes 580
  0.7 60.8 %copy-start.4 = (s32[1,48,2]{1,2,0:T(2,128)S(1)}, s32[1,48,2]{1,2,0:T(2,128)}, u32[]{:S(2)}) copy-start(s32[1,48,2]{1,2,0:T(2,128)} %param.16) | copy-start | bytes 1156
  3.1 58.4 %copy-start = (bf16[1,48,2,128,128]{4,3,2,1,0:T(8,128)(2,1)S(1)}, bf16[1,48,2,128,128]{4,3,2,1,0:T(8,128)(2,1)}, u32[]{:S(2)}) copy-start(bf16[1,48,2,128,128]{4,3,2,1,0:T(8,128)(2,1)} %param.17) | copy-start | bytes 9437188
  18.7 28.4 %all-to-all-start = ((bf16[12,16,1280]{2,1,0:T(8,128)(2,1)}), bf16[12,16,1280]{2,1,0:T(8,128)(2,1)}, u32[]{:S(2)}, u32[]{:S(2)}) async-start(bf16[12,16,1280]{2,1,0:T(8,128)(2,1)} %get-tuple-element.19), calls=%async_computation | async-start | bytes 983040 | tf_op jit(solution)/shard_map/all_to_all | solution.py:401
  47.1 34.1 %copy-start.1 = (bf16[256,1792]{1,0:T(8,128)(2,1)S(1)}, bf16[256,1792]{1,0:T(8,128)(2,1)}, u32[]{:S(2)}) copy-start(bf16[256,1792]{1,0:T(8,128)(2,1)} %all_gather.14.bundle_hbm) | copy-start | bytes 2752516
  61.5 2.0 %copy-start.2 = (bf16[4,26,16,128]{3,2,1,0:T(8,128)(2,1)}, bf16[4,26,16,128]{3,2,1,0:T(8,128)(2,1)S(1)}, u32[]{:S(2)}) copy-start(bf16[4,26,16,128]{3,2,1,0:T(8,128)(2,1)S(1)} %all_to_all.15.fetched_ref) | copy-start | bytes 1277956
  85.7 33.7 %all-to-all-start.2 = ((bf16[48,2,16,128]{3,2,1,0:T(8,128)(2,1)}), bf16[48,2,16,128]{3,2,1,0:T(8,128)(2,1)S(1)}, u32[]{:S(2)}, u32[]{:S(2)}) async-start(bf16[48,2,16,128]{3,2,1,0:T(8,128)(2,1)} %bitcast.8), calls=%async_computation.2 | async-start | bytes 786432 | tf_op jit(solution)/shard_map/all_to_all | solution.py:411

commit v10 on v7

--- a/solution.py
+++ b/solution.py
@@ -88,13 +88,19 @@
         copy.wait()
 
 
-def select_kernel(ask_ref, slabs_ref, out_ref):
+def select_kernel(ask_ref, slabs_hbm, out_ref, slabs_ref, sems):
     along, _, rows, _ = out_ref.shape
     column = slabs_ref.shape[0]
     slab = NB * BLK
     first = lax.axis_index("x") * column
-    for i in range(along):
-        for k in range(column):
+    copies = [
+        pltpu.make_async_copy(slabs_hbm.at[k], slabs_ref.at[k], sems.at[k]) for k in range(column)
+    ]
+    for copy in copies:
+        copy.start()
+    for k in range(column):
+        copies[k].wait()
+        for i in range(along):
             for c in range(CAP):
                 start = pl.multiple_of(ask_ref[i, c, first + k] * BLK, BLK)
                 out_ref[i, k * CAP + c] = slabs_ref[k, :, pl.ds(start, BLK)]
@@ -175,13 +181,15 @@
     adj_ref,
     out_ref,
     self_ref,
-    grads_ref,
+    grads_hbm,
     dst_ref,
     counts_ref,
     inv_ref,
     bundle_ref,
     out_all,
     scaled,
+    grads_ref,
+    out_sems,
     small,
 ):
     hidden = agg_ref.shape[0]
@@ -242,6 +250,10 @@
     zero = jnp.zeros((rows, BLK), bf16)
     contract_columns = (((1,), (1,)), ((), ()))
 
+    def grads_copy(k):
+        part = pl.ds(k * chunk, chunk)
+        return pltpu.make_async_copy(grads_ref.at[part], grads_hbm.at[part], out_sems.at[k])
+
     def step(k, carry):
         for i in range(chunk):
             t = k * chunk + i
@@ -253,9 +265,12 @@
                 chosen, adj_ref[pl.ds(start, BLK), :], contract_columns, preferred_element_type=f32
             )
             grads_ref[t] = grads.astype(bf16)
+        grads_copy(k).start()
         return carry
 
     lax.fori_loop(0, tiles // chunk, step, 0)
+    for k in range(tiles // chunk):
+        grads_copy(k).wait()
 
 
 def sum_kernel(ids_ref, grads_ref, self_hbm, out_ref, self_ref, sums, sem):
@@ -315,8 +330,12 @@
     return pl.pallas_call(
         select_kernel,
         out_shape=shape((along, column * CAP + CAP, rows, BLK), bf16),
-        in_specs=[SMEM, VMEM],
+        in_specs=[SMEM, HBM],
         out_specs=VMEM,
+        scratch_shapes=[
+            pltpu.VMEM(slabs.shape, bf16),
+            pltpu.SemaphoreType.DMA((column,)),
+        ],
         compiler_params=params(),
         name="select_blocks",
     )(asked, slabs)
@@ -353,7 +372,7 @@
             shape((tiles, rows, BLK), bf16),
         ),
         in_specs=[HBM] * 3 + [VMEM, HBM, VMEM],
-        out_specs=(VMEM,) * 3,
+        out_specs=(VMEM, VMEM, HBM),
         scratch_shapes=[
             pltpu.SMEM(dst.shape, jnp.int32),
             pltpu.SMEM(counts.shape, jnp.int32),
@@ -361,6 +380,8 @@
             pltpu.VMEM(bundle.shape, bf16),
             pltpu.VMEM((hidden, slab), bf16),
             pltpu.VMEM((NB, rows, BLK), bf16),
+            pltpu.VMEM((tiles, rows, BLK), bf16),
+            pltpu.SemaphoreType.DMA((tiles // chunk_of(tiles),)),
             pltpu.SemaphoreType.DMA((4,)),
         ],
         compiler_params=params(),

time: 122 us -> 123 us (level)
  no operation moved by 1% of the time
where the time goes in v10:
time: 123 us; the launch traced here: 122 us
  blocking collectives  59.3 us (48%)
  starting transfers between devices  28.2 us (23%)
  waiting for transfers between devices  20 us (16%)
  Pallas kernels  12.8 us (10%)
    all_gather x1, blocking collectives, per_device(): bundle = lax.all_gather(bundle, 'feat', axis=0, tiled=True)  21.7 us
    all_to_all x1, waiting for transfers between devices, per_device(): lax.all_to_all(grads.reshape(graph_parts, CAP, rows, BLK), ('x', 'z'), 0, 0)  20 us
    all_gather x1, blocking collectives, per_device(): agg_all = lax.all_gather(agg, 'feat', axis=0, tiled=True)  17.6 us
    all_to_all x1, starting transfers between devices, per_device(): slabs = lax.all_to_all(slabs, 'z', 0, 0)  15.4 us
    all_to_all x1, blocking collectives, per_device(): fetched = lax.all_to_all(picked, 'x', 0, 0)  13 us
    all_to_all x1, starting transfers between devices, per_device(): lax.all_to_all(grads.reshape(graph_parts, CAP, rows, BLK), ('x', 'z'), 0, 0)  12.7 us
    all_gather x1, blocking collectives, per_device(): asked = lax.all_gather(ask, 'x', axis=0)  6.97 us
    pallas_call x1, Pallas kernels, update(): pl.pallas_call(update_kernel, out_shape=(shape((rows, slab), bf16), shape...  4.97 us
  transfers between devices with their start and end apart: 2, of which 1 were waited for; matrix products, arithmetic and copies ran while one was open for 1% of the time, Pallas kernels for 0%

profile of v10, /device:TPU:6, one launch (start us, length us, event | category | flops | bytes accessed | tf_op | source)
XLA Modules:
  0.0 122.1 jit_solution(8518736006926527182)
XLA Ops:
  0.6 0.0 copy-start.3
  0.6 0.0 copy-start.5
  0.7 0.0 copy-start.4
  0.7 2.4 %prepare.1 = (bf16[12,16,1280]{2,1,0:T(8,128)(2,1)}, s32[2,128]{1,0:T(2,128)}, bf16[16,1792]{1,0:T(8,128)(2,1)}) custom-call(s32[2,48]{1,0:T(2,128)} %bitcast.17, f32[1,16]{1,0:T(1,128)} %bitcast.18, bf16[16,1024]{1,0:T(8,128)(2,1)} %feats_hbm.1, bf16[16,1024]{1,0:T(8,128)(2,1)} %cot_hbm.3, bf16[16,256]{1,0:T(8,128)(2,1)} %w_self_hbm.1, ...), custom_call_target="tpu_custom_call" | custom-call | tf_op jit(solution)/shard_map/prepare/pallas_call | solution.py:307
  3.1 0.0 copy-start
  3.1 15.4 %all-to-all-start = ((bf16[12,16,1280]{2,1,0:T(8,128)(2,1)}), bf16[12,16,1280]{2,1,0:T(8,128)(2,1)}, u32[]{:S(2)}, u32[]{:S(2)}) async-start(bf16[12,16,1280]{2,1,0:T(8,128)(2,1)} %get-tuple-element.13), calls=%async_computation | async-start | bytes 983040 | tf_op jit(solution)/shard_map/all_to_all | solution.py:420
  18.5 7.0 %all-gather.1.ask_ref = s32[4,2,128]{2,1,0:T(2,128)S(1)} all-gather(s32[1,2,128]{2,1,0:T(2,128)} %bitcast.16), channel_id=2, replica_groups=mesh['x'=4,'z'=12,'feat'=16] {'x'}, dimensions={0}, use_global_device_ids=true | all-gather | bytes 5120 | tf_op jit(solution)/shard_map/all_gather | solution.py:421
  25.5 21.7 %all_gather.14.bundle_hbm = bf16[256,1792]{1,0:T(8,128)(2,1)} all-gather(bf16[16,1792]{1,0:T(8,128)(2,1)} %get-tuple-element.15), channel_id=1, replica_groups=mesh['x'=4,'z'=12,'feat'=16] {'feat'}, dimensions={0}, use_global_device_ids=true | all-gather | bytes 974848 | tf_op jit(solution)/shard_map/all_gather | solution.py:422
  47.2 0.0 all-to-all-done.slabs_hbm
  47.2 0.0 copy-start.1
  47.2 1.7 %select_blocks.1 = bf16[4,26,16,128]{3,2,1,0:T(8,128)(2,1)S(1)} custom-call(s32[4,2,128]{2,1,0:T(2,128)S(1)} %all-gather.1.ask_ref, bf16[12,16,1280]{2,1,0:T(8,128)(2,1)} %all-to-all-done.slabs_hbm), custom_call_target="tpu_custom_call" | custom-call | tf_op jit(solution)/shard_map/select_blocks/pallas_call | solution.py:330
  49.0 13.0 %all_to_all.15.fetched_ref = bf16[4,26,16,128]{3,2,1,0:T(8,128)(2,1)S(1)} all-to-all(bf16[4,26,16,128]{3,2,1,0:T(8,128)(2,1)S(1)} %select_blocks.1), channel_id=1, replica_groups=mesh['x'=4,'z'=12,'feat'=16] {'x'}, dimensions={0} | all-to-all | bytes 851968 | tf_op jit(solution)/shard_map/all_to_all | solution.py:425
  62.0 0.0 copy-start.2
  62.0 0.0 copy-done.3
  62.0 0.0 copy-done.5
  62.0 0.0 copy-done.4
  62.0 0.0 copy-done
  62.0 1.9 %aggregate.1 = (bf16[16,1920]{1,0:T(8,128)(2,1)S(1)}, f32[8,128]{1,0:T(8,128)S(1)}) custom-call(s32[2,48]{1,0:T(2,128)S(1)} %bitcast.14, s32[1,48]{1,0:T(1,128)S(1)} %copy-done.5, bf16[16,1024]{1,0:T(8,128)(2,1)S(1)} %copy-done.3, bf16[4,26,16,128]{3,2,1,0:T(8,128)(2,1)S(1)} %all_to_all.15.fetched_ref, bf16[12288,128]{1,0:T(8,128)(2,1)S(1)} %bitcast.11), custom_call_target="tpu_custom_call" | custom-call | tf_op jit(solution)/shard_map/aggregate/pallas_call | solution.py:347
  63.9 0.0 copy-done.2
  63.9 17.6 %all_gather.15.agg_ref = bf16[256,1920]{1,0:T(8,128)(2,1)S(1)} all-gather(bf16[16,1920]{1,0:T(8,128)(2,1)S(1)} %get-tuple-element.19), channel_id=1, replica_groups=mesh['x'=4,'z'=12,'feat'=16] {'feat'}, dimensions={0}, use_global_device_ids=true | all-gather | bytes 1044480 | tf_op jit(solution)/shard_map/all_gather | solution.py:427
  81.5 0.0 copy-done.1
  81.5 5.0 %update.1 = (bf16[16,1024]{1,0:T(8,128)(2,1)}, f32[16,1024]{1,0:T(8,128)S(1)}, bf16[96,16,128]{2,1,0:T(8,128)(2,1)}) custom-call(s32[2,48]{1,0:T(2,128)S(1)} %bitcast.15, s32[1,48]{1,0:T(1,128)S(1)} %copy-done.5, f32[8,128]{1,0:T(8,128)S(1)} %get-tuple-element.18.inv_hbm, bf16[256,1920]{1,0:T(8,128)(2,1)S(1)} %all_gather.15.agg_ref, ...), custom_call_target="tpu_custom_call" | custom-call | tf_op jit(solution)/shard_map/update/pallas_call | solution.py:367
  86.5 12.7 %all-to-all-start.2 = ((bf16[48,2,16,128]{3,2,1,0:T(8,128)(2,1)}), bf16[48,2,16,128]{3,2,1,0:T(8,128)(2,1)S(1)}, u32[]{:S(2)}, u32[]{:S(2)}) async-start(bf16[48,2,16,128]{3,2,1,0:T(8,128)(2,1)} %bitcast.8), calls=%async_computation.2 | async-start | bytes 786432 | tf_op jit(solution)/shard_map/all_to_all | solution.py:431
  99.3 1.1 convert_reduce_fusion.ids_ref
  100.3 20.0 %all-to-all-done.2 = bf16[48,2,16,128]{3,2,1,0:T(8,128)(2,1)S(1)} async-done(((bf16[48,2,16,128]{3,2,1,0:T(8,128)(2,1)}), bf16[48,2,16,128]{3,2,1,0:T(8,128)(2,1)S(1)}, u32[]{:S(2)}, u32[]{:S(2)}) %all-to-all-start.2) | async-done | bytes 393248 | tf_op jit(solution)/shard_map/all_to_all | solution.py:431
  120.3 1.8 %sum_returned.1 = f32[16,1024]{1,0:T(8,128)} custom-call(s32[4,2,16]{2,1,0:T(2,128)S(1)} %convert_reduce_fusion.ids_ref, bf16[96,16,128]{2,1,0:T(8,128)(2,1)S(1)} %bitcast.13, f32[16,1024]{1,0:T(8,128)S(1)} %get-tuple-element.23.self_hbm), custom_call_target="tpu_custom_call" | custom-call | tf_op jit(solution)/shard_map/sum_returned/pallas_call | solution.py:393
Async XLA Ops:
  0.6 61.3 %copy-start.3 = (bf16[16,1024]{1,0:T(8,128)(2,1)S(1)}, bf16[16,1024]{1,0:T(8,128)(2,1)}, u32[]{:S(2)}) copy-start(bf16[16,1024]{1,0:T(8,128)(2,1)} %cot_hbm.3) | copy-start | bytes 98308
  0.6 61.3 %copy-start.5 = (s32[1,48]{1,0:T(1,128)S(1)}, s32[1,48]{1,0:T(1,128)}, u32[]{:S(2)}) copy-start(s32[1,48]{1,0:T(1,128)} %counts_hbm.3) | copy-start | bytes 580
  0.7 61.3 %copy-start.4 = (s32[1,48,2]{1,2,0:T(2,128)S(1)}, s32[1,48,2]{1,2,0:T(2,128)}, u32[]{:S(2)}) copy-start(s32[1,48,2]{1,2,0:T(2,128)} %param.16) | copy-start | bytes 1156
  3.1 58.9 %copy-start = (bf16[1,48,2,128,128]{4,3,2,1,0:T(8,128)(2,1)S(1)}, bf16[1,48,2,128,128]{4,3,2,1,0:T(8,128)(2,1)}, u32[]{:S(2)}) copy-start(bf16[1,48,2,128,128]{4,3,2,1,0:T(8,128)(2,1)} %param.17) | copy-start | bytes 9437188
  3.1 44.2 %all-to-all-start = ((bf16[12,16,1280]{2,1,0:T(8,128)(2,1)}), bf16[12,16,1280]{2,1,0:T(8,128)(2,1)}, u32[]{:S(2)}, u32[]{:S(2)}) async-start(bf16[12,16,1280]{2,1,0:T(8,128)(2,1)} %get-tuple-element.13), calls=%async_computation | async-start | bytes 983040 | tf_op jit(solution)/shard_map/all_to_all | solution.py:420
  47.2 34.3 %copy-start.1 = (bf16[256,1792]{1,0:T(8,128)(2,1)S(1)}, bf16[256,1792]{1,0:T(8,128)(2,1)}, u32[]{:S(2)}) copy-start(bf16[256,1792]{1,0:T(8,128)(2,1)} %all_gather.14.bundle_hbm) | copy-start | bytes 2752516
  62.0 2.0 %copy-start.2 = (bf16[4,26,16,128]{3,2,1,0:T(8,128)(2,1)}, bf16[4,26,16,128]{3,2,1,0:T(8,128)(2,1)S(1)}, u32[]{:S(2)}) copy-start(bf16[4,26,16,128]{3,2,1,0:T(8,128)(2,1)S(1)} %all_to_all.15.fetched_ref) | copy-start | bytes 1277956
  86.5 33.8 %all-to-all-start.2 = ((bf16[48,2,16,128]{3,2,1,0:T(8,128)(2,1)}), bf16[48,2,16,128]{3,2,1,0:T(8,128)(2,1)S(1)}, u32[]{:S(2)}, u32[]{:S(2)}) async-start(bf16[48,2,16,128]{3,2,1,0:T(8,128)(2,1)} %bitcast.8), calls=%async_computation.2 | async-start | bytes 786432 | tf_op jit(solution)/shard_map/all_to_all | solution.py:431
